TPU v7x, 32 devices: a whole 2x2x4 slice. The times are simulated.
32 devices in a mesh: dp: 8 (over z, x), tensor: 4 (over y, core).
Axes of the slice: x: 2, y: 2, z: 4, core: 2. Of those that a mesh axis runs over, the one named last changes fastest.
Arguments:
- tokens: bfloat16 [8192, 2048], P(('dp', 'tensor')), may hold values from -6 to 6
- norm1_gain: float32 [2048], replicated, may hold values from 0.5 to 1.5
- w_query: bfloat16 [2048, 2048], P(None, 'tensor'), may hold values from -0.125 to 0.125
- w_key: bfloat16 [2048, 2048], P(None, 'tensor'), may hold values from -0.125 to 0.125
- w_value: bfloat16 [2048, 4096], P(None, 'tensor'), may hold values from -0.125 to 0.125
- w_gate_out: bfloat16 [2048, 4096], P(None, 'tensor'), may hold values from -0.125 to 0.125
- w_decay: bfloat16 [2048, 16], P(None, 'tensor'), may hold values from -0.125 to 0.125
- w_beta: bfloat16 [2048, 16], P(None, 'tensor'), may hold values from -0.125 to 0.125
- conv_query: float32 [4, 2048], P(None, 'tensor'), may hold values from -3 to 3
- conv_key: float32 [4, 2048], P(None, 'tensor'), may hold values from -3 to 3
- conv_value: float32 [4, 4096], P(None, 'tensor'), may hold values from -3 to 3
- decay_log: float32 [16], P('tensor'), may hold values from 0 to 2.8
- decay_bias: float32 [16], P('tensor'), may hold values from -9 to -3
- head_gain: float32 [256], replicated, may hold values from 0.5 to 1.5
- w_out: bfloat16 [4096, 2048], P('tensor'), may hold values from -0.1875 to 0.1875
- norm2_gain: float32 [2048], replicated, may hold values from 0.5 to 1.5
- w_gate: bfloat16 [2048, 5504], P(None, 'tensor'), may hold values from -0.125 to 0.125
- w_up: bfloat16 [2048, 5504], P(None, 'tensor'), may hold values from -0.125 to 0.125
- w_down: bfloat16 [5504, 2048], P('tensor'), may hold values from -0.078125 to 0.078125
- state_in: float32 [8, 16, 128, 256], P('dp', 'tensor'), may hold values from -2 to 2
- seq_blocks: int32 [8], P('dp'), may hold values from 1 to 16, 96 in all
- seq_tail: int32 [8], P('dp'), may hold values from 1 to 64
- cotangent: bfloat16 [8192, 2048], P(('dp', 'tensor')), may hold values from -6 to 6
Outputs:
- mixed: bfloat16 [8192, 2048], P(('dp', 'tensor'))
- final_state: float32 [8, 16, 128, 256], P('dp', 'tensor')
- tokens_grad: bfloat16 [8192, 2048], P(('dp', 'tensor'))
- norm1_gain_grad: float32 [2048], replicated
- w_query_grad: float32 [2048, 2048], P('dp', 'tensor')
- w_key_grad: float32 [2048, 2048], P('dp', 'tensor')
- w_value_grad: float32 [2048, 4096], P('dp', 'tensor')
- w_gate_out_grad: float32 [2048, 4096], P('dp', 'tensor')
- w_decay_grad: float32 [2048, 16], P('dp', 'tensor')
- w_beta_grad: float32 [2048, 16], P('dp', 'tensor')
- conv_query_grad: float32 [4, 2048], P(None, 'tensor')
- conv_key_grad: float32 [4, 2048], P(None, 'tensor')
- conv_value_grad: float32 [4, 4096], P(None, 'tensor')
- decay_log_grad: float32 [16], P('tensor')
- decay_bias_grad: float32 [16], P('tensor')
- head_gain_grad: float32 [256], replicated
- w_out_grad: float32 [4096, 2048], P('tensor', 'dp')
- norm2_gain_grad: float32 [2048], replicated
- w_gate_grad: float32 [2048, 5504], P('dp', 'tensor')
- w_up_grad: float32 [2048, 5504], P('dp', 'tensor')
- w_down_grad: float32 [5504, 2048], P('tensor', 'dp')
Inputs may be any that keep to these rules, and one draw needn't show every extreme that they name: `seq_blocks`: one group's sequence fills all 16 blocks in every draw.
All inputs are finite; a program needn't handle non-finite values.
Results may differ from a plain program's by a relative error of at most 0.019.
Values may be sent and summed in bfloat16 or wider, within the bound.
A program may use at most 320 MiB of HBM per device.

v0:
```python
import jax
import jax.numpy as jnp
from jax import lax
from jax.sharding import PartitionSpec as P

BLOCK = 64


highest_precision = lax.Precision.HIGHEST


def product_tn(left, right):
    return lax.dot_general(
        left, right, (((0,), (0,)), ((), ())), preferred_element_type=jnp.float32
    )


def product_nt(left, right):
    return lax.dot_general(
        left, right, (((1,), (1,)), ((), ())), preferred_element_type=jnp.float32
    )


def precise_einsum(form, left, right):
    return jnp.einsum(form, left, right, precision=highest_precision)


def row_stats(rows):
    inverse = lax.rsqrt(jnp.mean(rows * rows, axis=-1, keepdims=True) + 1e-05)
    return (rows * inverse, inverse)


def norm_back(scaled, inverse, gain, upstream):
    along = upstream * gain
    inner = jnp.mean(along * scaled, axis=-1, keepdims=True)
    return (inverse * (along - scaled * inner), jnp.sum(upstream * scaled, axis=0))


def unit_rows(rows):
    return rows * lax.rsqrt(jnp.sum(rows * rows, axis=-1, keepdims=True) + 1e-06)


def causal_conv(series, kernel):
    length = series.shape[0]
    taps = kernel.shape[0]
    padded = jnp.pad(series, ((taps - 1, 0), (0, 0)))
    total = padded[0:length] * kernel[0]
    for tap_index in range(1, taps):
        total = total + padded[tap_index : tap_index + length] * kernel[tap_index]
    return jax.nn.silu(total)


def local_mixer(
    projected,
    kernel_query,
    kernel_key,
    kernel_value,
    log_scale,
    bias_decay,
    gain_head,
    state_carried_over,
    validity,
):
    rows = projected.shape[0]
    heads = log_scale.shape[0]
    key_width = kernel_query.shape[1]
    value_width = kernel_value.shape[1]
    key_size = key_width // heads
    value_size = value_width // heads
    query_rows = unit_rows(
        causal_conv(projected[:, :key_width], kernel_query).reshape(rows, heads, key_size)
    ) * key_size ** (-0.5)
    keys_all = unit_rows(
        causal_conv(projected[:, key_width : 2 * key_width], kernel_key).reshape(
            rows, heads, key_size
        )
    )
    values_all = causal_conv(
        projected[:, 2 * key_width : 2 * key_width + value_width], kernel_value
    ).reshape(rows, heads, value_size)
    gate_start = 2 * key_width + value_width
    out_gate = projected[:, gate_start : gate_start + value_width].reshape(rows, heads, value_size)
    decay_start = gate_start + value_width
    decay_in = projected[:, decay_start : decay_start + heads]
    beta_in = projected[:, decay_start + heads : decay_start + 2 * heads]
    decays = -jnp.exp(log_scale) * jax.nn.softplus(decay_in + bias_decay) * validity[:, None]
    strength = jax.nn.sigmoid(beta_in) * validity[:, None]
    blocks = rows // BLOCK

    def arrange(array):
        return jnp.swapaxes(array.reshape((blocks, BLOCK) + array.shape[1:]), 1, 2)

    queries_b = arrange(query_rows)
    keys_b = arrange(keys_all)
    values_b = arrange(values_all)
    decays_b = arrange(decays)
    strength_b = arrange(strength)
    running = jnp.cumsum(decays_b, axis=-1)
    gaps = running[..., :, None] - running[..., None, :]
    lower_strict = jnp.tril(jnp.ones((BLOCK, BLOCK), jnp.float32), -1) > 0
    lower_full = jnp.tril(jnp.ones((BLOCK, BLOCK), jnp.float32), 0) > 0
    weights_strict = jnp.where(lower_strict, jnp.exp(jnp.where(lower_strict, gaps, 0.0)), 0.0)
    weights_full = jnp.where(lower_full, jnp.exp(jnp.where(lower_full, gaps, 0.0)), 0.0)
    key_key = precise_einsum("bhik,bhjk->bhij", keys_b, keys_b)
    system = jnp.eye(BLOCK, dtype=jnp.float32) + strength_b[..., :, None] * key_key * weights_strict
    right_side = jnp.concatenate(
        [strength_b[..., None] * values_b, (strength_b * jnp.exp(running))[..., None] * keys_b],
        axis=-1,
    )
    solved = lax.linalg.triangular_solve(
        system, right_side, left_side=True, lower=True, unit_diagonal=True
    )
    values_new = solved[..., :value_size]
    keys_new = solved[..., value_size:]
    attend = precise_einsum("bhik,bhjk->bhij", queries_b, keys_b) * weights_full
    queries_decayed = queries_b * jnp.exp(running)[..., None]
    keys_decayed = keys_b * jnp.exp(running[..., -1:] - running)[..., None]
    carry_factor = jnp.exp(running[..., -1])

    def block_step(memory_state, inputs):
        fresh_values, mixing_output, attention, query_portion, key_portion, decay_factor = inputs
        delta_update = fresh_values - precise_einsum("qmi,qia->qma", mixing_output, memory_state)
        output_rows = precise_einsum("qmi,qia->qma", query_portion, memory_state) + precise_einsum(
            "hcj,hjv->hcv", attention, delta_update
        )
        memory_state = decay_factor[:, None, None] * memory_state + precise_einsum(
            "ytp,ytq->ypq", key_portion, delta_update
        )
        return (memory_state, output_rows)

    final, outputs = lax.scan(
        block_step,
        state_carried_over,
        (values_new, keys_new, attend, queries_decayed, keys_decayed, carry_factor),
    )
    outputs = jnp.swapaxes(outputs, 1, 2).reshape(rows, heads, value_size)
    normed = (
        outputs * lax.rsqrt(jnp.mean(outputs * outputs, axis=-1, keepdims=True) + 1e-05) * gain_head
    )
    gated = normed * jax.nn.silu(out_gate) * validity[:, None, None]
    return (gated.reshape(rows, value_width), final)


def per_device(
    tokens,
    norm1_gain,
    w_query,
    w_key,
    w_value,
    w_gate_out,
    w_decay,
    w_beta,
    conv_query,
    conv_key,
    conv_value,
    decay_log,
    decay_bias,
    head_gain,
    w_out,
    norm2_gain,
    w_gate,
    w_up,
    w_down,
    state_in,
    seq_blocks,
    seq_tail,
    cotangent,
):
    local_rows = tokens.shape[0]
    rows_in = tokens.astype(jnp.float32)
    scaled1, inverse1 = row_stats(rows_in)
    normed1 = (scaled1 * norm1_gain).astype(jnp.bfloat16)
    gathered1 = lax.all_gather(normed1, "tensor", axis=0, tiled=True)
    in_weights = (w_query, w_key, w_value, w_gate_out, w_decay, w_beta)
    projected = jnp.concatenate(
        [jnp.dot(gathered1, weight, preferred_element_type=jnp.float32) for weight in in_weights],
        axis=1,
    )
    bounds = [0]
    for weight in in_weights:
        bounds.append(bounds[-1] + weight.shape[1])
    group_rows = gathered1.shape[0]
    seq_length = BLOCK * (seq_blocks[0] - 1) + seq_tail[0]
    validity = (jnp.arange(group_rows, dtype=jnp.int32) < seq_length).astype(jnp.float32)
    state_carried_over = state_in[0]

    def mixer_part(
        inputs_proj, kernel_query, kernel_key, kernel_value, log_scale, bias_decay, gain_head
    ):
        return local_mixer(
            inputs_proj,
            kernel_query,
            kernel_key,
            kernel_value,
            log_scale,
            bias_decay,
            gain_head,
            state_carried_over,
            validity,
        )

    (gated, final), mixer_pull = jax.vjp(
        mixer_part, projected, conv_query, conv_key, conv_value, decay_log, decay_bias, head_gain
    )
    gated_low = gated.astype(jnp.bfloat16)
    resid = rows_in + lax.psum_scatter(
        jnp.dot(gated_low, w_out, preferred_element_type=jnp.float32).astype(jnp.bfloat16),
        "tensor",
        scatter_dimension=0,
        tiled=True,
    ).astype(jnp.float32)
    scaled2, inverse2 = row_stats(resid)
    normed2 = (scaled2 * norm2_gain).astype(jnp.bfloat16)
    gathered2 = lax.all_gather(normed2, "tensor", axis=0, tiled=True)
    gate_pre = jnp.dot(gathered2, w_gate, preferred_element_type=jnp.float32)
    up_pre = jnp.dot(gathered2, w_up, preferred_element_type=jnp.float32)
    sigmoid_gate = jax.nn.sigmoid(gate_pre)
    silu_gate = gate_pre * sigmoid_gate
    hidden = (silu_gate * up_pre).astype(jnp.bfloat16)
    mixed = (
        resid
        + lax.psum_scatter(
            jnp.dot(hidden, w_down, preferred_element_type=jnp.float32).astype(jnp.bfloat16),
            "tensor",
            scatter_dimension=0,
            tiled=True,
        ).astype(jnp.float32)
    ).astype(jnp.bfloat16)
    cot_full = lax.all_gather(cotangent, "tensor", axis=0, tiled=True)
    d_hidden = product_nt(cot_full, w_down)
    d_gate = (d_hidden * up_pre * sigmoid_gate * (1.0 + gate_pre * (1.0 - sigmoid_gate))).astype(
        jnp.bfloat16
    )
    d_up = (d_hidden * silu_gate).astype(jnp.bfloat16)
    grad_down = product_tn(hidden, cot_full)
    grad_gate = product_tn(gathered2, d_gate)
    grad_up = product_tn(gathered2, d_up)
    d_normed2 = lax.psum_scatter(
        (product_nt(d_gate, w_gate) + product_nt(d_up, w_up)).astype(jnp.bfloat16),
        "tensor",
        scatter_dimension=0,
        tiled=True,
    ).astype(jnp.float32)
    d_resid_part, grad_norm2 = norm_back(scaled2, inverse2, norm2_gain, d_normed2)
    d_resid = (cotangent.astype(jnp.float32) + d_resid_part).astype(jnp.bfloat16)
    resid_full = lax.all_gather(d_resid, "tensor", axis=0, tiled=True)
    d_gated = product_nt(resid_full, w_out)
    grad_out = product_tn(gated_low, resid_full)
    mixer_grads = mixer_pull((d_gated, jnp.zeros_like(final)))
    d_projected = mixer_grads[0].astype(jnp.bfloat16)
    total = jnp.zeros((local_rows * lax.axis_size("tensor"), w_query.shape[0]), jnp.float32)
    for mixer_position, weight in enumerate(in_weights):
        total = total + product_nt(
            d_projected[:, bounds[mixer_position] : bounds[mixer_position + 1]], weight
        )
    d_normed1 = lax.psum_scatter(
        total.astype(jnp.bfloat16), "tensor", scatter_dimension=0, tiled=True
    ).astype(jnp.float32)
    d_tokens_part, grad_norm1 = norm_back(scaled1, inverse1, norm1_gain, d_normed1)
    tokens_grad = (d_resid.astype(jnp.float32) + d_tokens_part).astype(jnp.bfloat16)
    grad_inputs = product_tn(gathered1, d_projected)
    in_grads = tuple(
        (grad_inputs[:, bounds[position] : bounds[position + 1]] for position in range(6))
    )
    vector_sums = (
        lax.psum(mixer_grads[1].astype(jnp.bfloat16), "dp").astype(jnp.float32),
        lax.psum(mixer_grads[2].astype(jnp.bfloat16), "dp").astype(jnp.float32),
        lax.psum(mixer_grads[3].astype(jnp.bfloat16), "dp").astype(jnp.float32),
        lax.psum(mixer_grads[4].astype(jnp.bfloat16), "dp").astype(jnp.float32),
        lax.psum(mixer_grads[5].astype(jnp.bfloat16), "dp").astype(jnp.float32),
    )
    gain_sums = lax.psum((grad_norm1, grad_norm2, mixer_grads[6]), ("dp", "tensor"))
    all_sums = (
        lax.psum_scatter(
            in_grads[0].astype(jnp.bfloat16), "dp", scatter_dimension=0, tiled=True
        ).astype(jnp.float32),
        lax.psum_scatter(
            in_grads[1].astype(jnp.bfloat16), "dp", scatter_dimension=0, tiled=True
        ).astype(jnp.float32),
        lax.psum_scatter(
            in_grads[2].astype(jnp.bfloat16), "dp", scatter_dimension=0, tiled=True
        ).astype(jnp.float32),
        lax.psum_scatter(
            in_grads[3].astype(jnp.bfloat16), "dp", scatter_dimension=0, tiled=True
        ).astype(jnp.float32),
        lax.psum_scatter(
            in_grads[4].astype(jnp.bfloat16), "dp", scatter_dimension=0, tiled=True
        ).astype(jnp.float32),
        lax.psum_scatter(
            in_grads[5].astype(jnp.bfloat16), "dp", scatter_dimension=0, tiled=True
        ).astype(jnp.float32),
        lax.psum_scatter(
            grad_out.astype(jnp.bfloat16), "dp", scatter_dimension=1, tiled=True
        ).astype(jnp.float32),
        lax.psum_scatter(
            grad_gate.astype(jnp.bfloat16), "dp", scatter_dimension=0, tiled=True
        ).astype(jnp.float32),
        lax.psum_scatter(
            grad_up.astype(jnp.bfloat16), "dp", scatter_dimension=0, tiled=True
        ).astype(jnp.float32),
        lax.psum_scatter(
            grad_down.astype(jnp.bfloat16), "dp", scatter_dimension=1, tiled=True
        ).astype(jnp.float32),
    )
    mixer_sums = all_sums[:7]
    gate_sum, up_sum, down_sum = (all_sums[7], all_sums[8], all_sums[9])
    return (
        mixed,
        final[None],
        tokens_grad,
        gain_sums[0],
        mixer_sums[0],
        mixer_sums[1],
        mixer_sums[2],
        mixer_sums[3],
        mixer_sums[4],
        mixer_sums[5],
        vector_sums[0],
        vector_sums[1],
        vector_sums[2],
        vector_sums[3],
        vector_sums[4],
        gain_sums[2],
        mixer_sums[6],
        gain_sums[1],
        gate_sum,
        up_sum,
        down_sum,
    )


def solution(mesh):
    in_specs = (
        P(("dp", "tensor"), None),
        P(),
        P(None, "tensor"),
        P(None, "tensor"),
        P(None, "tensor"),
        P(None, "tensor"),
        P(None, "tensor"),
        P(None, "tensor"),
        P(None, "tensor"),
        P(None, "tensor"),
        P(None, "tensor"),
        P("tensor"),
        P("tensor"),
        P(),
        P("tensor", None),
        P(),
        P(None, "tensor"),
        P(None, "tensor"),
        P("tensor", None),
        P("dp", "tensor", None, None),
        P("dp"),
        P("dp"),
        P(("dp", "tensor"), None),
    )
    out_specs = (
        P(("dp", "tensor"), None),
        P("dp", "tensor", None, None),
        P(("dp", "tensor"), None),
        P(),
        P("dp", "tensor"),
        P("dp", "tensor"),
        P("dp", "tensor"),
        P("dp", "tensor"),
        P("dp", "tensor"),
        P("dp", "tensor"),
        P(None, "tensor"),
        P(None, "tensor"),
        P(None, "tensor"),
        P("tensor"),
        P("tensor"),
        P(),
        P("tensor", "dp"),
        P(),
        P("dp", "tensor"),
        P("dp", "tensor"),
        P("tensor", "dp"),
    )
    return jax.shard_map(
        per_device, mesh=mesh, in_specs=in_specs, out_specs=out_specs, check_vma=False
    )
```

profile of v0, /device:TPU:0, one launch (start us, length us, event | category | flops | bytes accessed | tf_op | source)
XLA Modules:
  0.0 2088.5 jit_solution(13351433097824436248)
XLA Ops:
  12.2 35.5 %all-gather.5.cloned.1.call-done = bf16[1024,2048]{1,0:T(8,128)(2,1)} async-done(((bf16[256,2048]{1,0:T(8,128)(2,1)}), bf16[1024,2048]{1,0:T(8,128)(2,1)}) %all-gather.5.cloned.1.call-update) | async-done | bytes 4194320 | tf_op jit(solution)/shard_map/all_gather | solution.py:173
  92.9 6.7 fusion.138
  106.7 316.0 %custom-call.7 = f32[16,4,1,64,64]{3,4,2,1,0:T(8,128)} custom-call(f32[16,4,1,64,64]{4,3,2,1,0:T(8,128)} %get-tuple-element.797), custom_call_target="InvertDiagBlocksLowerTriangular" | custom-call | tf_op jit(solution)/shard_map/jvp()/triangular_solve | solution.py:110
  422.8 7.6 fusion.227
  430.5 6.4 fusion.75
  436.9 7.3 reshape.397
  444.1 6.8 copy.224
  457.3 6.9 fusion.56
  475.4 138.9 %while.45 = (s32[]{:T(128)}, f32[4,128,256]{2,1,0:T(8,128)S(1)}, f32[16,4,64,256]{3,1,2,0:T(4,128)}, f32[16,4,128,256]{3,2,1,0:T(8,128)}, f32[16,4,64,256]{3,2,1...) while((s32[]{:T(128)}, f32[4,128,256]{2,1,0:T(8,128)S(1)}, ...), condition=%wide.region_5.6_spmd, body=%wide.region_4.5_spmd.sunk | while | flops 352714752 | bytes 6296257 | solution.py:131
  621.0 5.3 copy.236
  626.7 12.3 multiply_convert_fusion.3
  640.4 6.3 convolution_convert_fusion.6
  646.8 44.6 %reduce-scatter.19.cloned.1.call-done = bf16[256,2048]{1,0:T(8,128)(2,1)} async-done(((bf16[1024,2048]{1,0:T(8,128)(2,1)}), bf16[256,2048]{1,0:T(8,128)(2,1)}) %reduce-scatter.19.cloned.1.call-update) | async-done | bytes 1048592 | tf_op jit(solution)/shard_map/reduce_scatter | solution.py:206
  695.3 34.0 %all-gather.7.cloned.1.call-done = bf16[1024,2048]{1,0:T(8,128)(2,1)} async-done(((bf16[256,2048]{1,0:T(8,128)(2,1)}), bf16[1024,2048]{1,0:T(8,128)(2,1)}) %all-gather.7.cloned.1.call-update) | async-done | bytes 4194320 | tf_op jit(solution)/shard_map/all_gather | solution.py:214
  729.3 11.8 fusion.229
  741.1 9.6 fusion.230
  750.7 14.6 all-gather.9.cloned.1.call-done
  765.3 14.8 multiply_convert_fusion
  780.1 11.0 fusion.231
  791.2 11.7 add_convert_fusion.2
  803.0 11.0 convolution_convert_fusion.4
  814.0 33.5 %reduce-scatter.23.cloned.1.call-done = bf16[256,2048]{1,0:T(8,128)(2,1)} async-done(((bf16[1024,2048]{1,0:T(8,128)(2,1)}), bf16[256,2048]{1,0:T(8,128)(2,1)}) %reduce-scatter.23.cloned.1.call-update) | async-done | bytes 1048592 | tf_op jit(solution)/shard_map/reduce_scatter | solution.py:238
  850.7 43.9 %reduce-scatter.21.cloned.1.call-done = bf16[256,2048]{1,0:T(8,128)(2,1)} async-done(((bf16[1024,2048]{1,0:T(8,128)(2,1)}), bf16[256,2048]{1,0:T(8,128)(2,1)}) %reduce-scatter.21.cloned.1.call-update) | async-done | bytes 1048592 | tf_op jit(solution)/shard_map/reduce_scatter | solution.py:222
  899.4 10.2 convolution_convert_fusion.2
  909.8 10.4 convolution_convert_fusion.1
  920.5 5.4 copy.238
  925.9 5.6 reshape.376
  937.3 10.2 convolution_convert_fusion.3
  947.6 15.0 fusion.66
  962.6 5.6 copy.237
  968.2 5.8 reshape.375
  974.0 19.4 fusion.71
  995.7 6.9 fusion.64
  1011.5 294.7 %while.46 = (s32[]{:T(128)}, f32[4,128,256]{2,1,0:T(8,128)S(1)}, f32[16,4,64,256]{3,2,1,0:T(8,128)}, f32[16,4,64,128]{3,2,1,0:T(8,128)}, f32[16,4,64,64]{3,2,1,0...) while((s32[]{:T(128)}, f32[4,128,256]{2,1,0:T(8,128)S(1)}, ...), condition=%wide.region_15.16_spmd.clone, body=%wide.region_13.15_spmd.clone.sunk | while | flops 706019328 | bytes 9967425 | solution.py:131
  1306.2 8.8 fusion.62
  1315.2 12.8 fusion.61
  1328.0 7.6 multiply_reduce_fusion.12
  1335.7 5.3 fusion.135
  1344.4 7.4 add_bitcast_fusion.1
  1363.1 8.1 copy.301
  1371.3 7.8 reshape.405
  1383.9 6.4 broadcast_multiply_fusion.4
  1416.7 6.4 multiply_reduce_fusion.7
  1442.0 6.6 broadcast_multiply_fusion
  1448.6 9.3 pad_add_fusion.3
  1459.9 5.5 add_convert_fusion
  1465.4 19.7 convolution_convert_fusion
  1493.7 6.2 fusion.220
  1500.8 5.6 fusion.196
  1508.5 5.7 fusion.162
  1514.2 5.8 fusion.161
  1520.0 6.9 fusion.116
  1526.9 6.9 fusion.118
  1533.8 16.5 add_convert_fusion.1
  1550.6 9.3 convolution_convert_fusion.5
  1567.0 37.3 %all-reduce.38 = (bf16[4,512]{1,0:T(4,128)(2,1)S(1)}, bf16[4,512]{1,0:T(4,128)(2,1)S(1)}, bf16[4,1024]{1,0:T(4,128)(2,1)S(1)}, bf16[4]{0:T(256)(128)(2,1)S(1)}, bf16[4]{0:T(256)(128)(2,1)S(1)}) all-reduce(bf16[4,512]{1,0:T(4,128)(2,1)S(1)} %add_convert_fusion.14, ...), channel_id=1, replica_groups=mesh['dp'=8,'tensor'=4] {'dp'}, use_global_device_ids=true, to_apply=%region_41.42 | all-reduce | flops 8200 | bytes 32800 | tf_op jit(solution)/shard_map/psum | solution.py:266
  1608.6 5.3 reduce-scatter.45.cloned.1.call-done
  1615.4 69.7 %reduce-scatter.27.cloned.1.call-done = bf16[256,512]{0,1:T(8,128)(2,1)} async-done(((bf16[2048,512]{0,1:T(8,128)(2,1)}), bf16[256,512]{0,1:T(8,128)(2,1)}) %reduce-scatter.27.cloned.1.call-update) | async-done | bytes 262160 | tf_op jit(solution)/shard_map/reduce_scatter | solution.py:274
  1687.0 69.3 %reduce-scatter.29.cloned.1.call-done = bf16[256,512]{0,1:T(8,128)(2,1)} async-done(((bf16[2048,512]{0,1:T(8,128)(2,1)}), bf16[256,512]{0,1:T(8,128)(2,1)}) %reduce-scatter.29.cloned.1.call-update) | async-done | bytes 262160 | tf_op jit(solution)/shard_map/reduce_scatter | solution.py:277
  1758.2 89.5 %reduce-scatter.31.cloned.1.call-done = bf16[256,1024]{0,1:T(8,128)(2,1)} async-done(((bf16[2048,1024]{0,1:T(8,128)(2,1)}), bf16[256,1024]{0,1:T(8,128)(2,1)}) %reduce-scatter.31.cloned.1.call-update) | async-done | bytes 524304 | tf_op jit(solution)/shard_map/reduce_scatter | solution.py:280
  1849.9 89.5 %reduce-scatter.33.cloned.1.call-done = bf16[256,1024]{0,1:T(8,128)(2,1)} async-done(((bf16[2048,1024]{0,1:T(8,128)(2,1)}), bf16[256,1024]{0,1:T(8,128)(2,1)}) %reduce-scatter.33.cloned.1.call-update) | async-done | bytes 524304 | tf_op jit(solution)/shard_map/reduce_scatter | solution.py:283
  1941.6 44.6 %reduce-scatter.25.cloned.1.call-done = bf16[256,2048]{1,0:T(8,128)(2,1)} async-done(((bf16[1024,2048]{1,0:T(8,128)(2,1)}), bf16[256,2048]{1,0:T(8,128)(2,1)}) %reduce-scatter.25.cloned.1.call-update) | async-done | bytes 1048592 | tf_op jit(solution)/shard_map/reduce_scatter | solution.py:256
  1988.3 42.3 %all-reduce.37 = (f32[2048]{0:T(1024)}, f32[256]{0:T(256)}, f32[2048]{0:T(1024)}) all-reduce(f32[2048]{0:T(1024)S(1)} %get-tuple-element.680, f32[256]{0:T(256)S(1)} %copy-done.134, f32[2048]{0:T(1024)S(1)} %copy-done.106), channel_id=1, replica_groups=mesh['dp'=8,'tensor'=4] {'dp','tensor'}, use_global_device_ids=true, to_apply=%region_30.31 | all-reduce | flops 4352 | bytes 34816 | tf_op jit(solution)/shard_map/psum | solution.py:272
  2033.9 45.3 %reduce-scatter.35.cloned.1.call-done = bf16[1024,256]{1,0:T(8,128)(2,1)} async-done(((bf16[1024,2048]{1,0:T(8,128)(2,1)}), bf16[1024,256]{1,0:T(8,128)(2,1)}) %reduce-scatter.35.cloned.1.call-update) | async-done | bytes 524304 | tf_op jit(solution)/shard_map/reduce_scatter | solution.py:292
  (788 shorter events, 649.9 us)
Async XLA Ops:
  7.2 47.2 %copy-start = (bf16[2048,512]{1,0:T(8,128)(2,1)S(1)}, bf16[2048,512]{1,0:T(8,128)(2,1)}, u32[]{:S(2)}) copy-start(bf16[2048,512]{1,0:T(8,128)(2,1)} %param.30) | copy-start | bytes 6291460
  7.2 40.5 %all-gather.5.cloned.1.call-start = ((), (), s32[]{:S(2)}) async-start(), calls=%async_computation.14 | async-start | bytes 5242880 | tf_op jit(solution)/shard_map/all_gather | solution.py:173
  7.3 40.4 %copy-start.90 = (bf16[2048,4]{0,1:T(4,128)(2,1)S(1)}, bf16[2048,4]{0,1:T(4,128)(2,1)}, u32[]{:S(2)}) copy-start(bf16[2048,4]{0,1:T(4,128)(2,1)} %param.33) | copy-start | bytes 49156
  7.3 40.4 %copy-start.135 = (f32[4]{0:T(128)S(1)}, f32[4]{0:T(128)}, u32[]{:S(2)}) copy-start(f32[4]{0:T(128)} %param.39) | copy-start | bytes 52
  10.4 681.0 %reduce-scatter.19.cloned.1.call-start = ((), (), s32[]{:S(2)}) async-start(), calls=%async_computation.15 | async-start | bytes 5242880 | tf_op jit(solution)/shard_map/reduce_scatter | solution.py:206
  11.9 39.4 %copy-start.132 = (f32[4]{0:T(128)}, f32[4]{0:T(128)S(1)}, u32[]{:S(2)}) copy-start(f32[4]{0:T(128)S(1)} %exponential_negate_fusion) | copy-start | bytes 52
  11.9 47.1 %copy-start.117 = (f32[1,512]{1,0:T(1,128)}, f32[1,512]{1,0:T(1,128)S(1)}, u32[]{:S(2)}) copy-start(f32[1,512]{1,0:T(1,128)S(1)} %get-tuple-element.811) | copy-start | bytes 6148
  11.9 47.1 %copy-start.119 = (f32[1,512]{1,0:T(1,128)}, f32[1,512]{1,0:T(1,128)S(1)}, u32[]{:S(2)}) copy-start(f32[1,512]{1,0:T(1,128)S(1)} %get-tuple-element.812) | copy-start | bytes 6148
  11.9 47.1 %copy-start.121 = (f32[1,512]{1,0:T(1,128)}, f32[1,512]{1,0:T(1,128)S(1)}, u32[]{:S(2)}) copy-start(f32[1,512]{1,0:T(1,128)S(1)} %get-tuple-element.813) | copy-start | bytes 6148
  11.9 47.1 %copy-start.123 = (f32[1,512]{1,0:T(1,128)}, f32[1,512]{1,0:T(1,128)S(1)}, u32[]{:S(2)}) copy-start(f32[1,512]{1,0:T(1,128)S(1)} %get-tuple-element.814) | copy-start | bytes 6148
  11.9 66.9 %copy-start.109 = (f32[1,512]{1,0:T(1,128)}, f32[1,512]{1,0:T(1,128)S(1)}, u32[]{:S(2)}) copy-start(f32[1,512]{1,0:T(1,128)S(1)} %get-tuple-element.807) | copy-start | bytes 6148
  12.0 66.9 %copy-start.111 = (f32[1,512]{1,0:T(1,128)}, f32[1,512]{1,0:T(1,128)S(1)}, u32[]{:S(2)}) copy-start(f32[1,512]{1,0:T(1,128)S(1)} %get-tuple-element.808) | copy-start | bytes 6148
  12.0 66.9 %copy-start.113 = (f32[1,512]{1,0:T(1,128)}, f32[1,512]{1,0:T(1,128)S(1)}, u32[]{:S(2)}) copy-start(f32[1,512]{1,0:T(1,128)S(1)} %get-tuple-element.809) | copy-start | bytes 6148
  12.0 66.9 %copy-start.115 = (f32[1,512]{1,0:T(1,128)}, f32[1,512]{1,0:T(1,128)S(1)}, u32[]{:S(2)}) copy-start(f32[1,512]{1,0:T(1,128)S(1)} %get-tuple-element.810) | copy-start | bytes 6148
  12.1 91.9 %copy-start.84 = (pred[64,64]{1,0:T(8,128)(4,1)}, pred[64,64]{1,0:T(8,128)(4,1)S(1)}, u32[]{:S(2)}) copy-start(pred[64,64]{1,0:T(8,128)(4,1)S(1)} %get-tuple-element.828) | copy-start | bytes 12292
  12.1 91.9 %copy-start.102 = (pred[64,64]{1,0:T(8,128)(4,1)}, pred[64,64]{1,0:T(8,128)(4,1)S(1)}, u32[]{:S(2)}) copy-start(pred[64,64]{1,0:T(8,128)(4,1)S(1)} %get-tuple-element.818) | copy-start | bytes 12292
  12.1 91.9 %copy-start.104 = (pred[64,64]{1,0:T(8,128)(4,1)}, pred[64,64]{1,0:T(8,128)(4,1)S(1)}, u32[]{:S(2)}) copy-start(pred[64,64]{1,0:T(8,128)(4,1)S(1)} %get-tuple-element.819) | copy-start | bytes 12292
  12.1 418.3 %copy-start.94 = (f32[1,1024]{1,0:T(1,128)}, f32[1,1024]{1,0:T(1,128)S(1)}, u32[]{:S(2)}) copy-start(f32[1,1024]{1,0:T(1,128)S(1)} %get-tuple-element.803) | copy-start | bytes 12292
  12.1 418.3 %copy-start.96 = (f32[1,1024]{1,0:T(1,128)}, f32[1,1024]{1,0:T(1,128)S(1)}, u32[]{:S(2)}) copy-start(f32[1,1024]{1,0:T(1,128)S(1)} %get-tuple-element.804) | copy-start | bytes 12292
  12.2 418.3 %copy-start.98 = (f32[1,1024]{1,0:T(1,128)}, f32[1,1024]{1,0:T(1,128)S(1)}, u32[]{:S(2)}) copy-start(f32[1,1024]{1,0:T(1,128)S(1)} %get-tuple-element.805) | copy-start | bytes 12292
  12.2 418.3 %copy-start.100 = (f32[1,1024]{1,0:T(1,128)}, f32[1,1024]{1,0:T(1,128)S(1)}, u32[]{:S(2)}) copy-start(f32[1,1024]{1,0:T(1,128)S(1)} %get-tuple-element.806) | copy-start | bytes 12292
  12.2 39.0 %copy-start.92 = (bf16[2048,4]{0,1:T(4,128)(2,1)S(1)}, bf16[2048,4]{0,1:T(4,128)(2,1)}, u32[]{:S(2)}) copy-start(bf16[2048,4]{0,1:T(4,128)(2,1)} %param.34) | copy-start | bytes 49156
  54.2 368.4 %copy-start.62 = (f32[16,4,64]{2,0,1:T(8,128)}, f32[16,4,64]{2,0,1:T(8,128)S(1)}, u32[]{:S(2)}) copy-start(f32[16,4,64]{2,0,1:T(8,128)S(1)} %reduce_window_sum.22) | copy-start | bytes 49156
  54.2 49.7 %copy-start.56 = (f32[16,4,64]{2,1,0:T(4,128)}, f32[16,4,64]{2,1,0:T(4,128)S(1)}, u32[]{:S(2)}) copy-start(f32[16,4,64]{2,1,0:T(4,128)S(1)} %copy.218) | copy-start | bytes 49156
  54.4 415.3 %copy-start.107 = (f32[16,4]{0,1:T(4,128)}, f32[16,4]{0,1:T(4,128)S(1)}, u32[]{:S(2)}) copy-start(f32[16,4]{0,1:T(4,128)S(1)} %slice_reduce_fusion) | copy-start | bytes 772
  73.5 380.2 %copy-start.58 = (f32[16,64,4]{1,2,0:T(4,128)}, f32[16,64,4]{1,2,0:T(4,128)S(1)}, u32[]{:S(2)}) copy-start(f32[16,64,4]{1,2,0:T(4,128)S(1)} %copy.213) | copy-start | bytes 49156
  92.8 377.0 %copy-start.60 = (f32[16,64,4]{1,2,0:T(4,128)}, f32[16,64,4]{1,2,0:T(4,128)S(1)}, u32[]{:S(2)}) copy-start(f32[16,64,4]{1,2,0:T(4,128)S(1)} %copy.230) | copy-start | bytes 49156
  92.8 329.8 %copy-start.66 = (f32[16,64,4]{1,0,2:T(8,128)}, f32[16,64,4]{1,0,2:T(8,128)S(1)}, u32[]{:S(2)}) copy-start(f32[16,64,4]{1,0,2:T(8,128)S(1)} %reshape.370) | copy-start | bytes 49156
  92.9 358.1 %copy-start.64 = (f32[16,4,64]{2,1,0:T(4,128)}, f32[16,4,64]{2,1,0:T(4,128)S(1)}, u32[]{:S(2)}) copy-start(f32[16,4,64]{2,1,0:T(4,128)S(1)} %copy.216) | copy-start | bytes 49156
  422.8 31.0 %copy-start.70 = (f32[16,4,64]{2,1,0:T(4,128)}, f32[16,4,64]{2,1,0:T(4,128)S(1)}, u32[]{:S(2)}) copy-start(f32[16,4,64]{2,1,0:T(4,128)S(1)} %copy.215) | copy-start | bytes 49156
  422.8 30.9 %copy-start.72 = (f32[16,4,64]{2,1,0:T(4,128)}, f32[16,4,64]{2,1,0:T(4,128)S(1)}, u32[]{:S(2)}) copy-start(f32[16,4,64]{2,1,0:T(4,128)S(1)} %copy.225) | copy-start | bytes 49156
  626.7 13.7 copy-start.52
  646.7 44.7 %copy-start.15 = (bf16[256,2048]{1,0:T(8,128)(2,1)S(1)}, bf16[256,2048]{1,0:T(8,128)(2,1)}, u32[]{:S(2)}) copy-start(bf16[256,2048]{1,0:T(8,128)(2,1)} %param.27) | copy-start | bytes 3145732
  646.7 46.4 %copy-start.87 = (f32[2048]{0:T(1024)S(1)}, f32[2048]{0:T(1024)}, u32[]{:S(2)}) copy-start(f32[2048]{0:T(1024)} %param.42) | copy-start | bytes 24580
  646.7 82.6 %all-gather.7.cloned.1.call-start = ((), (), s32[]{:S(2)}) async-start(), calls=%async_computation.16 | async-start | bytes 5242880 | tf_op jit(solution)/shard_map/all_gather | solution.py:214
  694.7 70.7 %all-gather.9.cloned.1.call-start = ((), (), s32[]{:S(2)}) async-start(), calls=%async_computation.18 | async-start | bytes 5242880 | tf_op jit(solution)/shard_map/all_gather | solution.py:229
  695.2 152.3 %reduce-scatter.23.cloned.1.call-start = ((), (), s32[]{:S(2)}) async-start(), calls=%async_computation.19 | async-start | bytes 5242880 | tf_op jit(solution)/shard_map/reduce_scatter | solution.py:238
  802.9 91.6 %reduce-scatter.21.cloned.1.call-start = ((), (), s32[]{:S(2)}) async-start(), calls=%async_computation.17 | async-start | bytes 5242880 | tf_op jit(solution)/shard_map/reduce_scatter | solution.py:222
  814.0 133.6 %all-gather.11.cloned.1.call-start = ((), (), s32[]{:S(2)}) async-start(), calls=%async_computation.20 | async-start | bytes 5242880 | tf_op jit(solution)/shard_map/all_gather | solution.py:246
  899.4 660.6 %reduce-scatter.37.cloned.1.call-start = ((), (), s32[]{:S(2)}) async-start(), calls=%async_computation.27 | async-start | bytes 6340608 | tf_op jit(solution)/shard_map/reduce_scatter | solution.py:295
  909.7 652.5 %reduce-scatter.39.cloned.1.call-start = ((), (), s32[]{:S(2)}) async-start(), calls=%async_computation.28 | async-start | bytes 6340608 | tf_op jit(solution)/shard_map/reduce_scatter | solution.py:298
  920.2 644.4 %reduce-scatter.41.cloned.1.call-start = ((), (), s32[]{:S(2)}) async-start(), calls=%async_computation.29 | async-start | bytes 6340608 | tf_op jit(solution)/shard_map/reduce_scatter | solution.py:301
  947.5 659.5 %reduce-scatter.43.cloned.1.call-start = ((), (), s32[]{:S(2)}) async-start(), calls=%async_computation.30 | async-start | bytes 589824
  1315.1 29.2 %copy-start.26 = (f32[16,4,64,384]{3,2,1,0:T(8,128)}, f32[16,4,64,384]{3,2,1,0:T(8,128)S(1)}, u32[]{:S(2)}) copy-start(f32[16,4,64,384]{3,2,1,0:T(8,128)S(1)} %fusion.62) | copy-start | bytes 18874372
  1315.1 12.8 copy-start.34
  1315.1 12.8 copy-start.41
  1315.1 12.8 copy-start.43
  1315.1 12.8 copy-start.57
  1315.2 12.8 copy-start.65
  1315.2 12.8 copy-start.85
  1315.2 12.8 copy-start.103
  1430.9 27.3 %copy-start.11 = (f32[1024,512]{0,1:T(8,128)}, f32[1024,512]{0,1:T(8,128)S(1)}, u32[]{:S(2)}) copy-start(f32[1024,512]{0,1:T(8,128)S(1)} %pad_add_fusion.9) | copy-start | bytes 6291460
  1487.0 126.9 %reduce-scatter.45.cloned.1.call-start = ((), (), s32[]{:S(2)}) async-start(), calls=%async_computation.31 | async-start | bytes 589824
  1488.2 197.0 %reduce-scatter.27.cloned.1.call-start = ((), (), s32[]{:S(2)}) async-start(), calls=%async_computation.22 | async-start | bytes 2359296 | tf_op jit(solution)/shard_map/reduce_scatter | solution.py:274
  1493.0 263.3 %reduce-scatter.29.cloned.1.call-start = ((), (), s32[]{:S(2)}) async-start(), calls=%async_computation.23 | async-start | bytes 2359296 | tf_op jit(solution)/shard_map/reduce_scatter | solution.py:277
  1493.6 354.1 %reduce-scatter.31.cloned.1.call-start = ((), (), s32[]{:S(2)}) async-start(), calls=%async_computation.24 | async-start | bytes 4718592 | tf_op jit(solution)/shard_map/reduce_scatter | solution.py:280
  1499.9 439.5 %reduce-scatter.33.cloned.1.call-start = ((), (), s32[]{:S(2)}) async-start(), calls=%async_computation.25 | async-start | bytes 4718592 | tf_op jit(solution)/shard_map/reduce_scatter | solution.py:283
  1500.4 485.8 %reduce-scatter.25.cloned.1.call-start = ((), (), s32[]{:S(2)}) async-start(), calls=%async_computation.21 | async-start | bytes 5242880 | tf_op jit(solution)/shard_map/reduce_scatter | solution.py:256
  1550.3 529.0 %reduce-scatter.35.cloned.1.call-start = ((), (), s32[]{:S(2)}) async-start(), calls=%async_computation.26 | async-start | bytes 4718592 | tf_op jit(solution)/shard_map/reduce_scatter | solution.py:292
  1687.0 299.2 %copy-start.16 = (bf16[256,2048]{1,0:T(8,128)(2,1)S(1)}, bf16[256,2048]{1,0:T(8,128)(2,1)}, u32[]{:S(2)}) copy-start(bf16[256,2048]{1,0:T(8,128)(2,1)} %param.27) | copy-start | bytes 3145732
  1687.0 299.2 %copy-start.89 = (f32[2048]{0:T(1024)S(1)}, f32[2048]{0:T(1024)}, u32[]{:S(2)}) copy-start(f32[2048]{0:T(1024)} %param.28) | copy-start | bytes 24580
  1687.0 299.2 %copy-start.127 = (f32[256]{0:T(256)S(1)}, f32[256]{0:T(256)}, u32[]{:S(2)}) copy-start(f32[256]{0:T(256)} %copy-done.126) | copy-start | bytes 3076
  1849.9 138.4 %copy-start.106 = (f32[2048]{0:T(1024)S(1)}, f32[2048]{0:T(1024)}, u32[]{:S(2)}) copy-start(f32[2048]{0:T(1024)} %get-tuple-element.676) | copy-start | bytes 24580
  1849.9 138.4 %copy-start.134 = (f32[256]{0:T(256)S(1)}, f32[256]{0:T(256)}, u32[]{:S(2)}) copy-start(f32[256]{0:T(256)} %get-tuple-element.662) | copy-start | bytes 3076
  (98 other events, 472.9 us)
Sparse Core Ops, SparseCore 0:
  10.5 37.1 all-gather.4
  646.8 44.5 reduce-scatter.18
  694.8 34.4 all-gather.6
  730.8 34.4 all-gather.8
  803.0 44.5 reduce-scatter.22
  850.0 44.5 reduce-scatter.20
  899.5 34.4 all-gather.10
  938.1 108.6 reduce-scatter.36
  1050.9 108.2 reduce-scatter.38
  1163.1 108.2 reduce-scatter.40
  1487.1 61.9 reduce-scatter.42
  1552.9 60.9 reduce-scatter.44
  1617.8 67.2 reduce-scatter.26
  1688.9 67.3 reduce-scatter.28
  1760.2 87.4 reduce-scatter.30
  1851.2 88.1 reduce-scatter.32
  1941.9 44.2 reduce-scatter.24
  1989.7 89.5 reduce-scatter.34
where the time goes:
time: 2100 us; the launch traced here: 2090 us
  matrix products  653 us (31%)
  waiting for transfers between devices  621 us (30%)
  other arithmetic  485 us (23%)
  local copies, waits for them, and re-layouts  230 us (11%)
  blocking collectives  79.6 us (4%)
    dot_general x198, matrix products, precise_einsum(): return jnp.einsum(form, left, right, precision=highest_precision)  384 us
    another operation x3, other arithmetic, local_mixer(): lax.linalg.triangular_solve(system, right_side, left_side=True, lower=Tru...  316 us
    dot_general x10, matrix products, product_nt(): lax.dot_general(left, right, (((1,), (1,)), ((), ())), preferred_element_...  99.9 us
    reduce_scatter x1, waiting for transfers between devices, per_device(): lax.psum_scatter(in_grads[2].astype(jnp.bfloat16), 'dp', scatter_dimensio...  89.5 us
    reduce_scatter x1, waiting for transfers between devices, per_device(): lax.psum_scatter(in_grads[3].astype(jnp.bfloat16), 'dp', scatter_dimensio...  89.5 us
    reduce_scatter x1, waiting for transfers between devices, per_device(): lax.psum_scatter(in_grads[0].astype(jnp.bfloat16), 'dp', scatter_dimensio...  69.7 us
    reduce_scatter x1, waiting for transfers between devices, per_device(): lax.psum_scatter(in_grads[1].astype(jnp.bfloat16), 'dp', scatter_dimensio...  69.3 us
    dot_general x5, matrix products, product_tn(): lax.dot_general(left, right, (((0,), (0,)), ((), ())), preferred_element_...  59.9 us
  transfers between devices with their start and end apart: 18, of which 13 were waited for; matrix products, arithmetic and copies ran while one was open for 34% of the time, Pallas kernels for 0%

commit v1 on v0

v1 whole, which is shorter than its diff:
```python
import jax
import jax.numpy as jnp
from jax import lax
from jax.experimental import pallas as pl
from jax.experimental.pallas import tpu as pltpu
from jax.sharding import PartitionSpec as P

BLOCK = 64

CHUNK = 128
f32 = jnp.float32
bf16 = jnp.bfloat16


def mm(left, right):
    return lax.dot_general(
        left.astype(bf16), right.astype(bf16), (((1,), (0,)), ((), ())), preferred_element_type=f32
    )


def mm_nt(left, right):
    return lax.dot_general(
        left.astype(bf16), right.astype(bf16), (((1,), (1,)), ((), ())), preferred_element_type=f32
    )


def mm_tn(left, right):
    return lax.dot_general(
        left.astype(bf16), right.astype(bf16), (((0,), (0,)), ((), ())), preferred_element_type=f32
    )


def conv_rows(rows, before, taps):
    count = rows.shape[0]
    longer = jnp.concatenate([before, rows], axis=0)
    total = rows * taps[3:4]
    for tap in range(3):
        total = total + longer[5 + tap : 5 + tap + count] * taps[tap : tap + 1]
    return total


def sigmoid(value):
    return 1.0 / (1.0 + jnp.exp(-value))


def unit_factor(rows):
    return lax.rsqrt(jnp.sum(rows * rows, axis=-1, keepdims=True) + 1e-06)


def chunk_masks():
    down = lax.broadcasted_iota(jnp.int32, (CHUNK, CHUNK), 0)
    across = lax.broadcasted_iota(jnp.int32, (CHUNK, CHUNK), 1)
    return down, across


def mixer_forward_kernel(
    length_ref, pq, pk, pv, pg, grow, gcol, cq, ck, cv, gain, s0,
    gated_out, final_out, o_out, delta_out, s_out, tt_out,
    state, tq, tk, tv,
):
    chunk = pl.program_id(0)
    heads = s0.shape[0]
    dk, dv = s0.shape[1], s0.shape[2]
    every = range(heads)

    @pl.when(chunk == 0)
    def _():
        state[...] = s0[...]
        tq[...] = jnp.zeros_like(tq)
        tk[...] = jnp.zeros_like(tk)
        tv[...] = jnp.zeros_like(tv)

    down, across = chunk_masks()
    lower = down > across
    full = down >= across
    level = jnp.where(lower, down ^ across, 0)
    eye = jnp.where(down == across, 1.0, 0.0)
    eye_low = eye.astype(bf16)
    kslice = [slice(h * dk, (h + 1) * dk) for h in every]
    vslice = [slice(h * dv, (h + 1) * dv) for h in every]

    def activated(ref, tail, taps, where):
        pre = conv_rows(ref[:, where], tail[:, where], taps[:, where])
        return pre * sigmoid(pre)

    keys, queries, values = [], [], []
    for h in every:
        u = activated(pk, tk, ck, kslice[h])
        keys.append((u * unit_factor(u)).astype(bf16))
    for h in every:
        u = activated(pq, tq, cq, kslice[h])
        queries.append((u * (unit_factor(u) * dk ** (-0.5))).astype(bf16))
    gc = [gcol[:, h : h + 1] for h in every]
    bc = [gcol[:, heads + h : heads + h + 1] for h in every]
    products = [mm_nt(jnp.concatenate([keys[h], queries[h]], axis=0), keys[h]) for h in every]
    gam = [jnp.exp(jnp.where(full, gc[h] - grow[0, h : h + 1, :], -1e30)) for h in every]
    system = [jnp.where(lower, products[h][:CHUNK] * gam[h] * bc[h], 0.0) for h in every]
    attend = [(products[h][CHUNK:] * gam[h]).astype(bf16) for h in every]
    system_low = [system[h].astype(bf16) for h in every]
    first = jnp.where(level == 1, 1.0, 0.0).astype(bf16)
    inverse = [eye_low - system_low[h] * first for h in every]
    size = 2
    while size < CHUNK:
        mask = jnp.where((level >= size) & (level < 2 * size), 1.0, 0.0).astype(bf16)
        inner = [mm(system_low[h] * mask, inverse[h]).astype(bf16) for h in every]
        inverse = [inverse[h] - mm(inverse[h], inner[h]).astype(bf16) for h in every]
        size *= 2
    left_over = [
        (eye - inverse[h].astype(f32))
        - mm(system_low[h], inverse[h])
        - mm((system[h] - system_low[h].astype(f32)).astype(bf16), inverse[h])
        for h in every
    ]
    inverse = [(inverse[h].astype(f32) + mm(inverse[h], left_over[h])) for h in every]
    for h in every:
        tt_out[0, h] = jnp.transpose(inverse[h]).astype(bf16)
    inverse = [inverse[h].astype(bf16) for h in every]
    for h in every:
        values.append(activated(pv, tv, cv, vslice[h]))
    for ref, tail in ((pq, tq), (pk, tk), (pv, tv)):
        tail[...] = ref[CHUNK - 8 :, :]
    growth = [jnp.exp(gc[h]) for h in every]
    keys_f = [keys[h].astype(f32) for h in every]
    pair = [
        jnp.concatenate(
            [(keys_f[h] * growth[h]).astype(bf16), (queries[h].astype(f32) * growth[h]).astype(bf16)], axis=0
        )
        for h in every
    ]
    for h in every:
        s_out[0, h] = state[h].astype(bf16)
    carried = [mm(pair[h], state[h]) for h in every]
    delta = [
        mm(inverse[h], bc[h] * (values[h] - carried[h][:CHUNK])).astype(bf16) for h in every
    ]
    out = [carried[h][CHUNK:] + mm(attend[h], delta[h]) for h in every]
    for h in every:
        last = gc[h][CHUNK - 1 : CHUNK]
        late = (keys_f[h] * jnp.exp(last - gc[h])).astype(bf16)
        state[h] = jnp.exp(last) * state[h] + mm_tn(late, delta[h])
    row_at = chunk * CHUNK + lax.broadcasted_iota(jnp.int32, (CHUNK, 1), 0)
    valid = jnp.where(row_at < length_ref[0], 1.0, 0.0)
    for h in every:
        delta_out[:, vslice[h]] = delta[h]
        o_out[:, vslice[h]] = out[h].astype(bf16)
        inv = lax.rsqrt(jnp.mean(out[h] * out[h], axis=-1, keepdims=True) + 1e-05)
        gate = pg[:, vslice[h]]
        gated_out[:, vslice[h]] = (
            out[h] * (inv * valid) * gain[...] * (gate * sigmoid(gate))
        ).astype(bf16)

    @pl.when(chunk == pl.num_programs(0) - 1)
    def _():
        final_out[...] = state[...]


def mixer_forward(length, pq, pk, pv, pg, grow, gcol, cq, ck, cv, gain, s0):
    rows = pq.shape[0]
    heads, dk, dv = s0.shape
    chunks = rows // CHUNK

    def by_rows(width):
        return pl.BlockSpec((CHUNK, width), lambda c: (c, 0))

    def whole(*shape):
        return pl.BlockSpec(shape, lambda c: (0,) * len(shape))

    def by_chunk(*shape):
        return pl.BlockSpec((1,) + shape, lambda c: (c,) + (0,) * len(shape))

    kw, vw = heads * dk, heads * dv
    return pl.pallas_call(
        mixer_forward_kernel,
        grid=(chunks,),
        in_specs=[
            pl.BlockSpec(memory_space=pltpu.SMEM),
            by_rows(kw), by_rows(kw), by_rows(vw), by_rows(vw),
            by_chunk(grow.shape[1], CHUNK),
            by_rows(2 * heads),
            whole(4, kw), whole(4, kw), whole(4, vw), whole(1, dv), whole(heads, dk, dv),
        ],
        out_specs=[
            by_rows(vw), whole(heads, dk, dv), by_rows(vw), by_rows(vw),
            by_chunk(heads, dk, dv), by_chunk(heads, CHUNK, CHUNK),
        ],
        out_shape=[
            jax.ShapeDtypeStruct((rows, vw), bf16),
            jax.ShapeDtypeStruct((heads, dk, dv), f32),
            jax.ShapeDtypeStruct((rows, vw), bf16),
            jax.ShapeDtypeStruct((rows, vw), bf16),
            jax.ShapeDtypeStruct((chunks, heads, dk, dv), bf16),
            jax.ShapeDtypeStruct((chunks, heads, CHUNK, CHUNK), bf16),
        ],
        scratch_shapes=[
            pltpu.VMEM((heads, dk, dv), f32),
            pltpu.VMEM((8, kw), f32), pltpu.VMEM((8, kw), f32), pltpu.VMEM((8, vw), f32),
        ],
        compiler_params=pltpu.CompilerParams(vmem_limit_bytes=48 * 1024 * 1024),
        cost_estimate=pl.CostEstimate(flops=8_000_000_000, bytes_accessed=32_000_000, transcendentals=4_000_000),
        name="mixer_forward",
    )(length, pq, pk, pv, pg, grow, gcol, cq, ck, cv, gain, s0)


def mixer_backward_kernel(
    length_ref, pq, pk, pv, pg, pq8, pk8, pv8, dgated, o_in, delta_in, s_in, tt_in,
    grow, gcol, cq, ck, cv, gain,
    dpq, dpk, dpv, dpg, dscal, dcq, dck, dcv, dgain,
    dstate, nq, nk, nv,
):
    step = pl.program_id(0)
    chunk = pl.num_programs(0) - 1 - step
    heads, dk, dv = dstate.shape
    every = range(heads)

    @pl.when(step == 0)
    def _():
        for ref in (dstate, nq, nk, nv, dcq, dck, dcv, dgain):
            ref[...] = jnp.zeros_like(ref)

    down, across = chunk_masks()
    lower = down > across
    full = down >= across
    upper = down < across
    ufull = down <= across
    kslice = [slice(h * dk, (h + 1) * dk) for h in every]
    vslice = [slice(h * dv, (h + 1) * dv) for h in every]
    has_before = jnp.where(chunk > 0, 1.0, 0.0)

    def preact(ref, ref8, taps, where):
        pre = conv_rows(ref[:, where], ref8[:, where] * has_before, taps[:, where])
        sig = sigmoid(pre)
        return pre, sig

    def conv_back(dpre, ref, ref8, taps, where, later, dtaps, dref):
        rows = ref[:, where]
        longer = jnp.concatenate([ref8[:, where] * has_before, rows], axis=0)
        after = jnp.concatenate([dpre, later[:, where]], axis=0)
        total = dpre * taps[3:4, where]
        sums = [jnp.sum(dpre * longer[5 + tap : 5 + tap + CHUNK], axis=0, keepdims=True) for tap in range(3)]
        sums.append(jnp.sum(dpre * rows, axis=0, keepdims=True))
        for tap in range(3):
            total = total + after[3 - tap : 3 - tap + CHUNK] * taps[tap : tap + 1, where]
        dtaps[:, where] += jnp.concatenate(sums, axis=0)
        later[:, where] = dpre[:8]
        dref[:, where] = total.astype(bf16)

    row_at = chunk * CHUNK + lax.broadcasted_iota(jnp.int32, (CHUNK, 1), 0)
    valid = jnp.where(row_at < length_ref[0], 1.0, 0.0)
    last_row = lax.broadcasted_iota(jnp.int32, (CHUNK, 1), 0) == CHUNK - 1
    kpre, ksig, kinv, kunit, keys = [], [], [], [], []
    qpre, qsig, qinv, qunit, queries = [], [], [], [], []
    for h in every:
        pre, sig = preact(pk, pk8, ck, kslice[h])
        u = pre * sig
        inv = unit_factor(u)
        kpre.append(pre), ksig.append(sig), kinv.append(inv), kunit.append(u * inv)
        keys.append(kunit[h].astype(bf16))
    for h in every:
        pre, sig = preact(pq, pq8, cq, kslice[h])
        u = pre * sig
        inv = unit_factor(u)
        qpre.append(pre), qsig.append(sig), qinv.append(inv), qunit.append(u * inv)
        queries.append((qunit[h] * dk ** (-0.5)).astype(bf16))
    gc = [gcol[:, h : h + 1] for h in every]
    gr = [grow[0, h : h + 1, :] for h in every]
    bc = [gcol[:, heads + h : heads + h + 1] for h in every]
    br = [grow[0, heads + h : heads + h + 1, :] for h in every]
    do = []
    for h in every:
        dg = dgated[:, vslice[h]].astype(f32) * valid
        gate = pg[:, vslice[h]]
        sig = sigmoid(gate)
        act = gate * sig
        o = o_in[:, vslice[h]].astype(f32)
        inv = lax.rsqrt(jnp.mean(o * o, axis=-1, keepdims=True) + 1e-05)
        norm = o * inv
        through = dg * norm
        dgain[...] += jnp.sum(through * act, axis=0, keepdims=True)
        dpg[:, vslice[h]] = (through * gain[...] * (sig + act * (1.0 - sig))).astype(bf16)
        dn = dg * gain[...] * act
        do.append((inv * (dn - norm * jnp.mean(dn * norm, axis=-1, keepdims=True))).astype(bf16))
    delta = [delta_in[:, vslice[h]] for h in every]
    dnext = [dstate[h].astype(bf16) for h in every]
    growth = [jnp.exp(gc[h]) for h in every]
    ending = [jnp.exp(gc[h][CHUNK - 1 : CHUNK] - gc[h]) for h in every]
    final = [jnp.exp(gc[h][CHUNK - 1 : CHUNK]) for h in every]
    gamma = [jnp.exp(jnp.where(full, gc[h] - gr[h], -1e30)) for h in every]
    gamma_t = [jnp.exp(jnp.where(ufull, gr[h] - gc[h], -1e30)) for h in every]
    kq = [mm_nt(keys[h], queries[h]) for h in every]
    keys_late = [(keys[h].astype(f32) * ending[h]).astype(bf16) for h in every]
    d_delta = [
        mm(
            jnp.concatenate([(kq[h] * gamma_t[h]).astype(bf16), keys_late[h]], axis=1),
            jnp.concatenate([do[h], dnext[h]], axis=0),
        ).astype(bf16)
        for h in every
    ]
    dr = [mm(tt_in[0, h], d_delta[h]) for h in every]
    dr_low = [dr[h].astype(bf16) for h in every]
    both = [jnp.concatenate([do[h], dr_low[h]], axis=0) for h in every]
    pair = [
        jnp.concatenate(
            [
                (queries[h].astype(f32) * growth[h]).astype(bf16),
                (keys[h].astype(f32) * (-growth[h] * bc[h])).astype(bf16),
            ],
            axis=0,
        )
        for h in every
    ]
    state = [s_in[0, h] for h in every]
    new_dstate = [final[h] * dstate[h] + mm_tn(pair[h], both[h]) for h in every]
    dgamma_end = [
        jnp.sum(jnp.sum(state[h].astype(f32) * dstate[h], axis=0, keepdims=True), axis=1, keepdims=True)
        * final[h]
        for h in every
    ]
    d_keys_late = [mm_nt(delta[h], dnext[h]) * ending[h] for h in every]
    for h in every:
        dstate[h] = new_dstate[h]
    strict = [jnp.where(lower, gamma[h] * bc[h], 0.0) for h in every]
    strict_t = [jnp.where(upper, gamma_t[h] * br[h], 0.0) for h in every]
    outer = [mm_nt(both[h], delta[h]) for h in every]
    outer_t = [mm_nt(delta[h], both[h]) for h in every]
    inner = [
        jnp.concatenate(
            [(outer[h][:CHUNK] * gamma[h]).astype(bf16), (-outer[h][CHUNK:] * strict[h]).astype(bf16)], axis=0
        )
        for h in every
    ]
    inner_t = [
        jnp.concatenate(
            [
                (outer_t[h][:, :CHUNK] * gamma_t[h]).astype(bf16),
                (-outer_t[h][:, CHUNK:] * strict_t[h]).astype(bf16),
            ],
            axis=1,
        )
        for h in every
    ]
    by_state = [mm_nt(both[h], state[h]) for h in every]
    by_key = [mm(inner[h], keys[h]) for h in every]
    d_col = [
        mm(inner_t[h], jnp.concatenate([queries[h], keys[h]], axis=0)) + d_keys_late[h] for h in every
    ]
    scal = []
    dbs = []
    for h in every:
        dq = by_key[h][:CHUNK] + by_state[h][:CHUNK] * growth[h]
        d_row = by_key[h][CHUNK:] - by_state[h][CHUNK:] * (growth[h] * bc[h])
        key_f = keys[h].astype(f32)
        q_along = jnp.sum(queries[h].astype(f32) * dq, axis=-1, keepdims=True)
        row_along = jnp.sum(key_f * d_row, axis=-1, keepdims=True)
        col_along = jnp.sum(key_f * d_col[h], axis=-1, keepdims=True)
        late_along = jnp.sum(key_f * d_keys_late[h], axis=-1, keepdims=True)
        at_end = dgamma_end[h] + jnp.sum(late_along, axis=0, keepdims=True)
        scal.append(q_along + row_along - col_along + jnp.where(last_row, at_end, 0.0))
        dbs.append(jnp.sum(dr[h] * delta[h].astype(f32), axis=-1, keepdims=True))
        du = qinv[h] * (dq * dk ** (-0.5) - qunit[h] * q_along)
        dpre = du * (qsig[h] * (1.0 + qpre[h] * (1.0 - qsig[h])))
        conv_back(dpre, pq, pq8, cq, kslice[h], nq, dcq, dpq)
        du = kinv[h] * (d_row + d_col[h] - kunit[h] * (row_along + col_along))
        dpre = du * (ksig[h] * (1.0 + kpre[h] * (1.0 - ksig[h])))
        conv_back(dpre, pk, pk8, ck, kslice[h], nk, dck, dpk)
        pre, sig = preact(pv, pv8, cv, vslice[h])
        dpre = dr[h] * bc[h] * (sig * (1.0 + pre * (1.0 - sig)))
        conv_back(dpre, pv, pv8, cv, vslice[h], nv, dcv, dpv)
    dscal[...] = jnp.concatenate(scal + dbs, axis=1)


def mixer_backward(length, pq, pk, pv, pg, dgated, o, delta, s, tt, grow, gcol, cq, ck, cv, gain):
    rows = pq.shape[0]
    chunks, heads, dk, dv = s.shape
    kw, vw = heads * dk, heads * dv
    per = CHUNK // 8

    def by_rows(width):
        return pl.BlockSpec((CHUNK, width), lambda c: (chunks - 1 - c, 0))

    def before(width):
        return pl.BlockSpec((8, width), lambda c: (jnp.maximum((chunks - 1 - c) * per - 1, 0), 0))

    def whole(*shape):
        return pl.BlockSpec(shape, lambda c: (0,) * len(shape))

    def by_chunk(*shape):
        return pl.BlockSpec((1,) + shape, lambda c: (chunks - 1 - c,) + (0,) * len(shape))

    return pl.pallas_call(
        mixer_backward_kernel,
        grid=(chunks,),
        in_specs=[
            pl.BlockSpec(memory_space=pltpu.SMEM),
            by_rows(kw), by_rows(kw), by_rows(vw), by_rows(vw),
            before(kw), before(kw), before(vw),
            by_rows(vw), by_rows(vw), by_rows(vw),
            by_chunk(heads, dk, dv), by_chunk(heads, CHUNK, CHUNK),
            by_chunk(grow.shape[1], CHUNK), by_rows(2 * heads),
            whole(4, kw), whole(4, kw), whole(4, vw), whole(1, dv),
        ],
        out_specs=[
            by_rows(kw), by_rows(kw), by_rows(vw), by_rows(vw), by_rows(2 * heads),
            whole(4, kw), whole(4, kw), whole(4, vw), whole(1, dv),
        ],
        out_shape=[
            jax.ShapeDtypeStruct((rows, kw), bf16),
            jax.ShapeDtypeStruct((rows, kw), bf16),
            jax.ShapeDtypeStruct((rows, vw), bf16),
            jax.ShapeDtypeStruct((rows, vw), bf16),
            jax.ShapeDtypeStruct((rows, 2 * heads), f32),
            jax.ShapeDtypeStruct((4, kw), f32),
            jax.ShapeDtypeStruct((4, kw), f32),
            jax.ShapeDtypeStruct((4, vw), f32),
            jax.ShapeDtypeStruct((1, dv), f32),
        ],
        scratch_shapes=[
            pltpu.VMEM((heads, dk, dv), f32),
            pltpu.VMEM((8, kw), f32), pltpu.VMEM((8, kw), f32), pltpu.VMEM((8, vw), f32),
        ],
        compiler_params=pltpu.CompilerParams(vmem_limit_bytes=48 * 1024 * 1024),
        cost_estimate=pl.CostEstimate(flops=8_000_000_000, bytes_accessed=40_000_000, transcendentals=6_000_000),
        name="mixer_backward",
    )(length, pq, pk, pv, pg, pq, pk, pv, dgated, o, delta, s, tt, grow, gcol, cq, ck, cv, gain)


def decay_parts(pa, pb, log_scale, bias, valid):
    rows, heads = pa.shape
    decays = -jnp.exp(log_scale) * jax.nn.softplus(pa + bias) * valid
    strength = jax.nn.sigmoid(pb) * valid
    by_chunk = decays.reshape(rows // CHUNK, CHUNK, heads)
    at = jnp.arange(CHUNK)
    ones = (at[:, None] >= at[None, :]).astype(f32)
    running = jnp.einsum("ij,cjh->cih", ones, by_chunk, precision=lax.Precision.HIGHEST)
    strength_c = strength.reshape(rows // CHUNK, CHUNK, heads)
    cols = jnp.concatenate([running, strength_c], axis=-1)
    return jnp.swapaxes(cols, 1, 2), cols.reshape(rows, 2 * heads)


def decay_back(dscal, pa, pb, log_scale, bias, valid):
    rows, heads = pa.shape
    at = jnp.arange(CHUNK)
    ones = (at[:, None] <= at[None, :]).astype(f32)
    dg = dscal[:, :heads].reshape(rows // CHUNK, CHUNK, heads)
    da = jnp.einsum("ij,cjh->cih", ones, dg, precision=lax.Precision.HIGHEST).reshape(rows, heads)
    shifted = pa + bias
    scale = -jnp.exp(log_scale)
    dlog = jnp.sum(da * scale * jax.nn.softplus(shifted) * valid, axis=0)
    dpa = da * scale * jax.nn.sigmoid(shifted) * valid
    dpb = dscal[:, heads:] * jax.nn.sigmoid(-pb)
    return dlog, jnp.sum(dpa, axis=0), dpa, dpb


def product_tn(left, right):
    return lax.dot_general(
        left, right, (((0,), (0,)), ((), ())), preferred_element_type=jnp.float32
    )


def product_nt(left, right):
    return lax.dot_general(
        left, right, (((1,), (1,)), ((), ())), preferred_element_type=jnp.float32
    )


def row_stats(rows):
    inverse = lax.rsqrt(jnp.mean(rows * rows, axis=-1, keepdims=True) + 1e-05)
    return (rows * inverse, inverse)


def norm_back(scaled, inverse, gain, upstream):
    along = upstream * gain
    inner = jnp.mean(along * scaled, axis=-1, keepdims=True)
    return (inverse * (along - scaled * inner), jnp.sum(upstream * scaled, axis=0))


def per_device(
    tokens,
    norm1_gain,
    w_query,
    w_key,
    w_value,
    w_gate_out,
    w_decay,
    w_beta,
    conv_query,
    conv_key,
    conv_value,
    decay_log,
    decay_bias,
    head_gain,
    w_out,
    norm2_gain,
    w_gate,
    w_up,
    w_down,
    state_in,
    seq_blocks,
    seq_tail,
    cotangent,
):
    local_rows = tokens.shape[0]
    rows_in = tokens.astype(jnp.float32)
    scaled1, inverse1 = row_stats(rows_in)
    normed1 = (scaled1 * norm1_gain).astype(jnp.bfloat16)
    gathered1 = lax.all_gather(normed1, "tensor", axis=0, tiled=True)
    in_weights = (w_query, w_key, w_value, w_gate_out, w_decay, w_beta)
    group_rows = gathered1.shape[0]
    heads = decay_log.shape[0]
    w_small = jnp.concatenate([w_decay, w_beta], axis=1)
    p_query, p_key, p_value, p_gate = [
        jnp.dot(gathered1, weight, preferred_element_type=jnp.float32) for weight in in_weights[:4]
    ]
    p_small = jnp.dot(gathered1, w_small, preferred_element_type=jnp.float32)
    p_decay, p_beta = p_small[:, :heads], p_small[:, heads:]
    seq_length = BLOCK * (seq_blocks - 1) + seq_tail
    validity = (jnp.arange(group_rows, dtype=jnp.int32) < seq_length[0]).astype(jnp.float32)[:, None]
    grow, gcol = decay_parts(p_decay, p_beta, decay_log, decay_bias, validity)
    gain_row = head_gain[None]
    gated_low, final, mixer_out, delta, states, inverse_t = mixer_forward(
        seq_length, p_query, p_key, p_value, p_gate, grow, gcol,
        conv_query, conv_key, conv_value, gain_row, state_in[0],
    )
    resid = rows_in + lax.psum_scatter(
        jnp.dot(gated_low, w_out, preferred_element_type=jnp.float32).astype(jnp.bfloat16),
        "tensor",
        scatter_dimension=0,
        tiled=True,
    ).astype(jnp.float32)
    scaled2, inverse2 = row_stats(resid)
    normed2 = (scaled2 * norm2_gain).astype(jnp.bfloat16)
    gathered2 = lax.all_gather(normed2, "tensor", axis=0, tiled=True)
    gate_pre = jnp.dot(gathered2, w_gate, preferred_element_type=jnp.float32)
    up_pre = jnp.dot(gathered2, w_up, preferred_element_type=jnp.float32)
    sigmoid_gate = jax.nn.sigmoid(gate_pre)
    silu_gate = gate_pre * sigmoid_gate
    hidden = (silu_gate * up_pre).astype(jnp.bfloat16)
    mixed = (
        resid
        + lax.psum_scatter(
            jnp.dot(hidden, w_down, preferred_element_type=jnp.float32).astype(jnp.bfloat16),
            "tensor",
            scatter_dimension=0,
            tiled=True,
        ).astype(jnp.float32)
    ).astype(jnp.bfloat16)
    cot_full = lax.all_gather(cotangent, "tensor", axis=0, tiled=True)
    d_hidden = product_nt(cot_full, w_down)
    d_gate = (d_hidden * up_pre * sigmoid_gate * (1.0 + gate_pre * (1.0 - sigmoid_gate))).astype(
        jnp.bfloat16
    )
    d_up = (d_hidden * silu_gate).astype(jnp.bfloat16)
    grad_down = product_tn(hidden, cot_full)
    grad_gate = product_tn(gathered2, d_gate)
    grad_up = product_tn(gathered2, d_up)
    d_normed2 = lax.psum_scatter(
        (product_nt(d_gate, w_gate) + product_nt(d_up, w_up)).astype(jnp.bfloat16),
        "tensor",
        scatter_dimension=0,
        tiled=True,
    ).astype(jnp.float32)
    d_resid_part, grad_norm2 = norm_back(scaled2, inverse2, norm2_gain, d_normed2)
    d_resid = (cotangent.astype(jnp.float32) + d_resid_part).astype(jnp.bfloat16)
    resid_full = lax.all_gather(d_resid, "tensor", axis=0, tiled=True)
    d_gated = product_nt(resid_full, w_out)
    grad_out = product_tn(gated_low, resid_full)
    dp_query, dp_key, dp_value, dp_gate, dscal, dc_query, dc_key, dc_value, dgain = mixer_backward(
        seq_length, p_query, p_key, p_value, p_gate, d_gated, mixer_out, delta, states, inverse_t,
        grow, gcol, conv_query, conv_key, conv_value, gain_row,
    )
    dlog, dbias, dp_decay, dp_beta = decay_back(dscal, p_decay, p_beta, decay_log, decay_bias, validity)
    dp_small = jnp.concatenate([dp_decay, dp_beta], axis=1).astype(jnp.bfloat16)
    dps = (dp_query, dp_key, dp_value, dp_gate, dp_small)
    weights = (w_query, w_key, w_value, w_gate_out, w_small)
    total = product_nt(dps[0], weights[0])
    for dp_part, weight in zip(dps[1:], weights[1:]):
        total = total + product_nt(dp_part, weight)
    d_normed1 = lax.psum_scatter(
        total.astype(jnp.bfloat16), "tensor", scatter_dimension=0, tiled=True
    ).astype(jnp.float32)
    d_tokens_part, grad_norm1 = norm_back(scaled1, inverse1, norm1_gain, d_normed1)
    tokens_grad = (d_resid.astype(jnp.float32) + d_tokens_part).astype(jnp.bfloat16)
    in_grads = [product_tn(gathered1, dp_part) for dp_part in dps]
    in_grads = in_grads[:4] + [in_grads[4][:, :heads], in_grads[4][:, heads:]]
    mixer_grads = (None, dc_query, dc_key, dc_value, dlog, dbias, dgain[0])
    vector_sums = (
        lax.psum(mixer_grads[1].astype(jnp.bfloat16), "dp").astype(jnp.float32),
        lax.psum(mixer_grads[2].astype(jnp.bfloat16), "dp").astype(jnp.float32),
        lax.psum(mixer_grads[3].astype(jnp.bfloat16), "dp").astype(jnp.float32),
        lax.psum(mixer_grads[4].astype(jnp.bfloat16), "dp").astype(jnp.float32),
        lax.psum(mixer_grads[5].astype(jnp.bfloat16), "dp").astype(jnp.float32),
    )
    gain_sums = lax.psum((grad_norm1, grad_norm2, mixer_grads[6]), ("dp", "tensor"))
    all_sums = (
        lax.psum_scatter(
            in_grads[0].astype(jnp.bfloat16), "dp", scatter_dimension=0, tiled=True
        ).astype(jnp.float32),
        lax.psum_scatter(
            in_grads[1].astype(jnp.bfloat16), "dp", scatter_dimension=0, tiled=True
        ).astype(jnp.float32),
        lax.psum_scatter(
            in_grads[2].astype(jnp.bfloat16), "dp", scatter_dimension=0, tiled=True
        ).astype(jnp.float32),
        lax.psum_scatter(
            in_grads[3].astype(jnp.bfloat16), "dp", scatter_dimension=0, tiled=True
        ).astype(jnp.float32),
        lax.psum_scatter(
            in_grads[4].astype(jnp.bfloat16), "dp", scatter_dimension=0, tiled=True
        ).astype(jnp.float32),
        lax.psum_scatter(
            in_grads[5].astype(jnp.bfloat16), "dp", scatter_dimension=0, tiled=True
        ).astype(jnp.float32),
        lax.psum_scatter(
            grad_out.astype(jnp.bfloat16), "dp", scatter_dimension=1, tiled=True
        ).astype(jnp.float32),
        lax.psum_scatter(
            grad_gate.astype(jnp.bfloat16), "dp", scatter_dimension=0, tiled=True
        ).astype(jnp.float32),
        lax.psum_scatter(
            grad_up.astype(jnp.bfloat16), "dp", scatter_dimension=0, tiled=True
        ).astype(jnp.float32),
        lax.psum_scatter(
            grad_down.astype(jnp.bfloat16), "dp", scatter_dimension=1, tiled=True
        ).astype(jnp.float32),
    )
    mixer_sums = all_sums[:7]
    gate_sum, up_sum, down_sum = (all_sums[7], all_sums[8], all_sums[9])
    return (
        mixed,
        final[None],
        tokens_grad,
        gain_sums[0],
        mixer_sums[0],
        mixer_sums[1],
        mixer_sums[2],
        mixer_sums[3],
        mixer_sums[4],
        mixer_sums[5],
        vector_sums[0],
        vector_sums[1],
        vector_sums[2],
        vector_sums[3],
        vector_sums[4],
        gain_sums[2],
        mixer_sums[6],
        gain_sums[1],
        gate_sum,
        up_sum,
        down_sum,
    )


def solution(mesh):
    in_specs = (
        P(("dp", "tensor"), None),
        P(),
        P(None, "tensor"),
        P(None, "tensor"),
        P(None, "tensor"),
        P(None, "tensor"),
        P(None, "tensor"),
        P(None, "tensor"),
        P(None, "tensor"),
        P(None, "tensor"),
        P(None, "tensor"),
        P("tensor"),
        P("tensor"),
        P(),
        P("tensor", None),
        P(),
        P(None, "tensor"),
        P(None, "tensor"),
        P("tensor", None),
        P("dp", "tensor", None, None),
        P("dp"),
        P("dp"),
        P(("dp", "tensor"), None),
    )
    out_specs = (
        P(("dp", "tensor"), None),
        P("dp", "tensor", None, None),
        P(("dp", "tensor"), None),
        P(),
        P("dp", "tensor"),
        P("dp", "tensor"),
        P("dp", "tensor"),
        P("dp", "tensor"),
        P("dp", "tensor"),
        P("dp", "tensor"),
        P(None, "tensor"),
        P(None, "tensor"),
        P(None, "tensor"),
        P("tensor"),
        P("tensor"),
        P(),
        P("tensor", "dp"),
        P(),
        P("dp", "tensor"),
        P("dp", "tensor"),
        P("tensor", "dp"),
    )
    return jax.shard_map(
        per_device, mesh=mesh, in_specs=in_specs, out_specs=out_specs, check_vma=False
    )
```

time: 2100 us -> 1360 us (0.65)
  other arithmetic: 485 us -> 47 us
  matrix products: 653 us -> 228 us
  waiting for transfers between devices: 621 us -> 902 us
  local copies, waits for them, and re-layouts: 230 us -> 13.1 us
  Pallas kernels: 0 us -> 68.1 us
    dot_general x199 -> x3, matrix products: 396 us -> 4.48 us  [the longest x1 3.37 us: per_device(): p_small = jnp.dot(gathered1, w_small, preferred_element_type=jnp.float32)]
    another operation x6 -> x1, other arithmetic: 319 us -> 0.03 us  [the longest x3 316 us: local_mixer(): lax.linalg.triangular_solve(system, right_side, left_side=True, lower=Tru...]
    reduce_scatter x1, waiting for transfers between devices: 0.02 us -> 110 us  [per_device(): lax.psum_scatter(grad_gate.astype(jnp.bfloat16), 'dp', scatter_dimension=...]
    reshape x22 -> x1, local copies, waits for them, and re-layouts: 87.5 us -> 0.19 us  [decay_parts(): strength_c = strength.reshape(rows // CHUNK, CHUNK, heads)]
    reduce_scatter x1, waiting for transfers between devices: 0.01 us -> 83.8 us  [per_device(): lax.psum_scatter(grad_up.astype(jnp.bfloat16), 'dp', scatter_dimension=0,...]
    unnamed x20, waiting for transfers between devices: 7.08 us -> 88.8 us
    reduce_sum x31 -> x1, other arithmetic: 77.5 us -> 0.56 us  [decay_back(): return (dlog, jnp.sum(dpa, axis=0), dpa, dpb)]
    pallas_call x0 -> x2, Pallas kernels: none -> 68.1 us  [the longest x1 36.6 us: mixer_backward(): pl.pallas_call(mixer_backward_kernel, grid=(chunks,), in_specs=[pl.BlockS...]
  transfers between devices with their start and end apart: 18 -> 18, of which waited for: 13 -> 17; matrix products, arithmetic and copies ran while one was open for 34% -> 14% of each run, Pallas kernels for 0% -> 3%
where the time goes in v1:
time: 1360 us; the launch traced here: 1350 us
  waiting for transfers between devices  902 us (66%)
  matrix products  228 us (17%)
  blocking collectives  78.2 us (6%)
  Pallas kernels  68.1 us (5%)
  other arithmetic  47 us (3%)
  between operations  16.3 us (1%)
    reduce_scatter x1, waiting for transfers between devices, per_device(): lax.psum_scatter(grad_gate.astype(jnp.bfloat16), 'dp', scatter_dimension=...  110 us
    reduce_scatter x1, waiting for transfers between devices, per_device(): lax.psum_scatter(grad_out.astype(jnp.bfloat16), 'dp', scatter_dimension=1...  89.6 us
    reduce_scatter x1, waiting for transfers between devices, per_device(): lax.psum_scatter(in_grads[2].astype(jnp.bfloat16), 'dp', scatter_dimensio...  89.1 us
    unnamed x20, waiting for transfers between devices  88.8 us
    dot_general x9, matrix products, product_nt(): lax.dot_general(left, right, (((1,), (1,)), ((), ())), preferred_element_...  88 us
    reduce_scatter x1, waiting for transfers between devices, per_device(): lax.psum_scatter(grad_up.astype(jnp.bfloat16), 'dp', scatter_dimension=0,...  83.8 us
    dot_general x9, matrix products, product_tn(): lax.dot_general(left, right, (((0,), (0,)), ((), ())), preferred_element_...  75 us
    reduce_scatter x1, waiting for transfers between devices, per_device(): lax.psum_scatter(in_grads[0].astype(jnp.bfloat16), 'dp', scatter_dimensio...  69 us
  transfers between devices with their start and end apart: 18, of which 17 were waited for; matrix products, arithmetic and copies ran while one was open for 14% of the time, Pallas kernels for 3%

profile of v1, /device:TPU:0, one launch (start us, length us, event | category | flops | bytes accessed | tf_op | source)
XLA Modules:
  0.0 1354.4 jit_solution(4479729456041635870)
XLA Ops:
  7.3 1.6 fusion.19
  9.5 2.5 fusion.16
  13.4 35.9 %all-gather.5.cloned.1.call-done = bf16[1024,2048]{1,0:T(8,128)(2,1)} async-done(((bf16[256,2048]{1,0:T(8,128)(2,1)}), bf16[1024,2048]{1,0:T(8,128)(2,1)}) %all-gather.5.cloned.1.call-update) | async-done | bytes 4194320 | tf_op jit(solution)/shard_map/all_gather | solution.py:505
  49.4 3.4 fusion.25
  59.1 6.0 fusion.36.pk.pk8
  65.2 3.7 fusion.35.pq.pq8
  68.9 6.6 fusion.38.pg
  75.5 6.1 fusion.37.pv.pv8
  81.6 31.5 %mixer_forward.1 = (bf16[1024,1024]{1,0:T(8,128)(2,1)S(1)}, f32[4,128,256]{2,1,0:T(8,128)}, bf16[1024,1024]{1,0:T(8,128)(2,1)}, bf16[1024,1024]{1,0:T(8,128)(2,1...) custom-call(s32[1]{0:T(128)} %add.123.length_ref, f32[1024,512]{1,0:T(8,128)} %fusion.35.pq.pq8, ...), custom_call_target="tpu_custom_call" | custom-call | flops 8000000000 | bytes 32000000 | tf_op jit(solution)/shard_map/mixer_forward/pallas_call | solution.py:172
  115.3 6.1 convolution_convert_fusion.7
  121.5 44.6 %reduce-scatter.19.cloned.1.call-done = bf16[256,2048]{1,0:T(8,128)(2,1)} async-done(((bf16[1024,2048]{1,0:T(8,128)(2,1)}), bf16[256,2048]{1,0:T(8,128)(2,1)}) %reduce-scatter.19.cloned.1.call-update) | async-done | bytes 1048592 | tf_op jit(solution)/shard_map/reduce_scatter | solution.py:523
  166.1 2.0 multiply_reduce_fusion
  168.1 2.9 multiply_convert_fusion.3
  171.7 34.0 %all-gather.7.cloned.1.call-done = bf16[1024,2048]{1,0:T(8,128)(2,1)} async-done(((bf16[256,2048]{1,0:T(8,128)(2,1)}), bf16[1024,2048]{1,0:T(8,128)(2,1)}) %all-gather.7.cloned.1.call-update) | async-done | bytes 4194320 | tf_op jit(solution)/shard_map/all_gather | solution.py:531
  205.7 11.6 fusion.40
  217.2 9.6 fusion.39
  226.8 14.8 %all-gather.9.cloned.1.call-done = bf16[1024,2048]{1,0:T(8,128)(2,1)} async-done(((bf16[256,2048]{1,0:T(8,128)(2,1)}), bf16[1024,2048]{1,0:T(8,128)(2,1)}) %all-gather.9.cloned.1.call-update) | async-done | bytes 4194320 | tf_op jit(solution)/shard_map/all_gather | solution.py:546
  241.7 14.8 %multiply_convert_fusion = (bf16[1024,1376]{0,1:T(8,128)(2,1)S(1)}, bf16[1024,1376]{0,1:T(8,128)(2,1)S(1)}, bf16[1024,1376]{0,1:T(8,128)(2,1)}) fusion(f32[1024,1376]{0,1:T(8,128)} %fusion.39, f32[1024,1376]{0,1:T(8,128)} %fusion.40, bf16[1024,2048]{1,0:T(8,128)(2,1)} %all-gather.9.cloned.1.call-done, bf16[1376,2048]{1,0:T(8,128)(2,1)} %param.41), kind=kOutput, calls=%fused_computation.5 | convolution fusion | flops 5792497664 | bytes 29556736 | tf_op jit(solution)/shard_map/dot_general | solution.py:460
  256.5 11.0 fusion.41
  267.6 11.5 add_convert_fusion.1
  279.2 11.1 convolution_convert_fusion.3
  290.3 33.4 %reduce-scatter.23.cloned.1.call-done = bf16[256,2048]{1,0:T(8,128)(2,1)} async-done(((bf16[1024,2048]{1,0:T(8,128)(2,1)}), bf16[256,2048]{1,0:T(8,128)(2,1)}) %reduce-scatter.23.cloned.1.call-update) | async-done | bytes 1048592 | tf_op jit(solution)/shard_map/reduce_scatter | solution.py:555
  323.8 2.8 fusion.15
  326.6 44.1 %reduce-scatter.21.cloned.1.call-done = bf16[256,2048]{1,0:T(8,128)(2,1)} async-done(((bf16[1024,2048]{1,0:T(8,128)(2,1)}), bf16[256,2048]{1,0:T(8,128)(2,1)}) %reduce-scatter.21.cloned.1.call-update) | async-done | bytes 1048592 | tf_op jit(solution)/shard_map/reduce_scatter | solution.py:539
  370.7 5.2 fusion.14
  376.0 10.2 convolution_convert_fusion.2
  386.3 10.6 convolution_convert_fusion
  397.0 10.3 convolution_convert_fusion.1
  407.3 3.3 all-gather.11.cloned.1.call-done
  410.6 10.1 fusion.42.dgated
  420.7 36.6 %mixer_backward.1 = (bf16[1024,512]{1,0:T(8,128)(2,1)S(1)}, bf16[1024,512]{1,0:T(8,128)(2,1)S(1)}, bf16[1024,1024]{1,0:T(8,128)(2,1)}, bf16[1024,1024]{1,0:T(8,1...) custom-call(s32[1]{0:T(128)} %add.123.length_ref, ...), custom_call_target="tpu_custom_call" | custom-call | flops 8000000000 | bytes 40000000 | tf_op jit(solution)/shard_map/mixer_backward/pallas_call | solution.py:389
  461.6 2.9 convolution_convert_fusion.10
  466.8 6.3 convolution_convert_fusion.9
  473.2 6.2 convolution_convert_fusion.8
  479.7 9.5 convolution_convert_fusion.4
  489.3 9.4 convolution_convert_fusion.6
  499.2 7.0 fusion.44
  506.2 5.7 fusion.43
  511.9 6.9 fusion.45
  518.8 6.9 fusion.46
  525.7 14.2 %add_convert_fusion = bf16[1024,2048]{1,0:T(8,128)(2,1)} fusion(f32[1024,2048]{1,0:T(8,128)} %fusion.46, f32[1024,2048]{1,0:T(8,128)} %fusion.45, f32[1024,2048]{1,0:T(8,128)} %fusion.43, f32[1024,2048]{1,0:T(8,128)} %fusion.44, bf16[2048,4]{0,1:T(4,128)(2,1)S(1)} %copy-done.21, bf16[2048,4]{0,1:T(4,128)(2,1)S(1)} %copy-done.23, ...), kind=kOutput, calls=%fused_computation | convolution fusion | flops 44138496 | bytes 37797888 | tf_op jit(solution)/shard_map/dot_general | solution.py:460
  540.1 9.5 convolution_convert_fusion.5
  549.6 2.3 convert_element_type.200
  551.9 83.8 %reduce-scatter.39.cloned.1.call-done = bf16[256,1376]{0,1:T(8,128)(2,1)} async-done(((bf16[2048,1376]{0,1:T(8,128)(2,1)}), bf16[256,1376]{0,1:T(8,128)(2,1)}) %reduce-scatter.39.cloned.1.call-update) | async-done | bytes 704528 | tf_op jit(solution)/shard_map/reduce_scatter | solution.py:618
  635.7 2.3 convert_element_type.198
  638.0 110.1 %reduce-scatter.37.cloned.1.call-done = bf16[256,1376]{0,1:T(8,128)(2,1)} async-done(((bf16[2048,1376]{0,1:T(8,128)(2,1)}), bf16[256,1376]{0,1:T(8,128)(2,1)}) %reduce-scatter.37.cloned.1.call-update) | async-done | bytes 704528 | tf_op jit(solution)/shard_map/reduce_scatter | solution.py:615
  748.1 2.3 convert_element_type.196
  750.4 36.1 %all-reduce.1 = (bf16[4,512]{1,0:T(4,128)(2,1)S(1)}, bf16[4,512]{1,0:T(4,128)(2,1)S(1)}, bf16[4,1024]{1,0:T(4,128)(2,1)S(1)}, bf16[4]{0:T(256)(128)(2,1)S(1)}, bf16[4]{0:T(256)(128)(2,1)S(1)}) all-reduce(bf16[4,512]{1,0:T(4,128)(2,1)S(1)} %convert_element_type.183, ...), channel_id=1, replica_groups=mesh['dp'=8,'tensor'=4] {'dp'}, use_global_device_ids=true, to_apply=%region_16.17 | all-reduce | flops 8200 | bytes 32800 | tf_op jit(solution)/shard_map/psum | solution.py:586
  789.3 24.8 %reduce-scatter.45.cloned.1.call-done = bf16[256,4]{1,0:T(8,128)(2,1)} async-done(((bf16[2048,4]{1,0:T(8,128)(2,1)}), bf16[256,4]{1,0:T(8,128)(2,1)}) %reduce-scatter.45.cloned.1.call-update) | async-done | bytes 2064
  815.7 63.2 %reduce-scatter.43.cloned.1.call-done = bf16[256,4]{1,0:T(8,128)(2,1)} async-done(((bf16[2048,4]{1,0:T(8,128)(2,1)}), bf16[256,4]{1,0:T(8,128)(2,1)}) %reduce-scatter.43.cloned.1.call-update) | async-done | bytes 2064
  880.4 69.0 %reduce-scatter.27.cloned.1.call-done = bf16[256,512]{1,0:T(8,128)(2,1)} async-done(((bf16[2048,512]{1,0:T(8,128)(2,1)}), bf16[256,512]{1,0:T(8,128)(2,1)}) %reduce-scatter.27.cloned.1.call-update) | async-done | bytes 262160 | tf_op jit(solution)/shard_map/reduce_scatter | solution.py:594
  949.4 1.8 convert_element_type.174
  951.2 68.8 %reduce-scatter.29.cloned.1.call-done = bf16[256,512]{1,0:T(8,128)(2,1)} async-done(((bf16[2048,512]{1,0:T(8,128)(2,1)}), bf16[256,512]{1,0:T(8,128)(2,1)}) %reduce-scatter.29.cloned.1.call-update) | async-done | bytes 262160 | tf_op jit(solution)/shard_map/reduce_scatter | solution.py:597
  1020.1 1.8 convert_element_type.176
  1021.9 89.6 %reduce-scatter.35.cloned.1.call-done = bf16[1024,256]{1,0:T(8,128)(2,1)} async-done(((bf16[1024,2048]{1,0:T(8,128)(2,1)}), bf16[1024,256]{1,0:T(8,128)(2,1)}) %reduce-scatter.35.cloned.1.call-update) | async-done | bytes 524304 | tf_op jit(solution)/shard_map/reduce_scatter | solution.py:612
  1111.5 2.1 convert_element_type.194
  1113.6 89.1 %reduce-scatter.31.cloned.1.call-done = bf16[256,1024]{1,0:T(8,128)(2,1)} async-done(((bf16[2048,1024]{1,0:T(8,128)(2,1)}), bf16[256,1024]{1,0:T(8,128)(2,1)}) %reduce-scatter.31.cloned.1.call-update) | async-done | bytes 524304 | tf_op jit(solution)/shard_map/reduce_scatter | solution.py:600
  1202.7 2.1 convert_element_type.178
  1204.8 44.7 %reduce-scatter.25.cloned.1.call-done = bf16[256,2048]{1,0:T(8,128)(2,1)} async-done(((bf16[1024,2048]{1,0:T(8,128)(2,1)}), bf16[256,2048]{1,0:T(8,128)(2,1)}) %reduce-scatter.25.cloned.1.call-update) | async-done | bytes 1048592 | tf_op jit(solution)/shard_map/reduce_scatter | solution.py:577
  1249.5 2.4 fusion.18
  1251.9 42.2 %all-reduce = (f32[2048]{0:T(1024)}, f32[256]{0:T(256)}, f32[2048]{0:T(1024)}) all-reduce(f32[2048]{0:T(1024)S(1)} %get-tuple-element.53, f32[256]{0:T(256)S(1)} %bitcast.84, f32[2048]{0:T(1024)S(1)} %get-tuple-element.51), channel_id=1, replica_groups=mesh['dp'=8,'tensor'=4] {'dp','tensor'}, use_global_device_ids=true, to_apply=%region_9.10 | all-reduce | flops 4352 | bytes 34816 | tf_op jit(solution)/shard_map/psum | solution.py:592
  1294.1 47.9 %reduce-scatter.33.cloned.1.call-done = bf16[256,1024]{1,0:T(8,128)(2,1)} async-done(((bf16[2048,1024]{1,0:T(8,128)(2,1)}), bf16[256,1024]{1,0:T(8,128)(2,1)}) %reduce-scatter.33.cloned.1.call-update) | async-done | bytes 524304 | tf_op jit(solution)/shard_map/reduce_scatter | solution.py:603
  1342.0 2.1 convert_element_type.180
  1344.1 3.3 fusion.10
  (164 shorter events, 24.0 us)
Async XLA Ops:
  7.2 51.9 %copy-start = (bf16[2048,512]{1,0:T(8,128)(2,1)S(1)}, bf16[2048,512]{1,0:T(8,128)(2,1)}, u32[]{:S(2)}) copy-start(bf16[2048,512]{1,0:T(8,128)(2,1)} %param.26) | copy-start | bytes 6291460
  7.2 6.2 copy-start.42
  7.2 42.2 %copy-start.20 = (bf16[2048,4]{0,1:T(4,128)(2,1)S(1)}, bf16[2048,4]{0,1:T(4,128)(2,1)}, u32[]{:S(2)}) copy-start(bf16[2048,4]{0,1:T(4,128)(2,1)} %param.30) | copy-start | bytes 49156
  7.2 42.2 %copy-start.22 = (bf16[2048,4]{0,1:T(4,128)(2,1)S(1)}, bf16[2048,4]{0,1:T(4,128)(2,1)}, u32[]{:S(2)}) copy-start(bf16[2048,4]{0,1:T(4,128)(2,1)} %param.29) | copy-start | bytes 49156
  7.2 42.1 %all-gather.5.cloned.1.call-start = ((), (), s32[]{:S(2)}) async-start(), calls=%async_computation.14 | async-start | bytes 5242880 | tf_op jit(solution)/shard_map/all_gather | solution.py:505
  8.9 0.6 copy-start.26
  12.0 42.6 %copy-start.28 = (f32[4]{0:T(128)S(1)}, f32[4]{0:T(128)}, u32[]{:S(2)}) copy-start(f32[4]{0:T(128)} %param.35) | copy-start | bytes 52
  12.0 154.1 %reduce-scatter.19.cloned.1.call-start = ((), (), s32[]{:S(2)}) async-start(), calls=%async_computation.15 | async-start | bytes 5242880 | tf_op jit(solution)/shard_map/reduce_scatter | solution.py:523
  13.4 42.6 %copy-start.24 = (f32[1024]{0:T(1024)}, f32[1024]{0:T(1024)S(1)}, u32[]{:S(2)}) copy-start(f32[1024]{0:T(1024)S(1)} %fusion.27) | copy-start | bytes 12292
  13.4 42.6 %copy-start.30 = (f32[4]{0:T(128)}, f32[4]{0:T(128)S(1)}, u32[]{:S(2)}) copy-start(f32[4]{0:T(128)S(1)} %exponential_negate_fusion) | copy-start | bytes 52
  52.7 0.6 copy-start.16
  53.6 3.2 copy-start.14
  59.1 6.1 copy-start.13
  59.1 6.1 copy-start.38
  65.2 3.7 copy-start.35
  68.9 6.6 copy-start.33
  75.4 6.1 copy-start.3
  75.4 6.1 copy-start.4
  75.4 6.1 copy-start.5
  75.4 6.1 copy-start.6
  75.4 6.1 copy-start.10
  81.6 33.8 %copy-start.32 = (bf16[1024,2048]{1,0:T(8,128)(2,1)S(1)}, bf16[1024,2048]{1,0:T(8,128)(2,1)}, u32[]{:S(2)}) copy-start(bf16[1024,2048]{1,0:T(8,128)(2,1)} %param.37) | copy-start | bytes 12582916
  113.0 1.0 copy-start.1
  114.0 1.3 copy-start.11
  121.4 46.7 %copy-start.18 = (f32[2048]{0:T(1024)S(1)}, f32[2048]{0:T(1024)}, u32[]{:S(2)}) copy-start(f32[2048]{0:T(1024)} %param.38) | copy-start | bytes 24580
  121.5 84.2 %all-gather.7.cloned.1.call-start = ((), (), s32[]{:S(2)}) async-start(), calls=%async_computation.16 | async-start | bytes 5242880 | tf_op jit(solution)/shard_map/all_gather | solution.py:531
  171.0 70.6 %all-gather.9.cloned.1.call-start = ((), (), s32[]{:S(2)}) async-start(), calls=%async_computation.18 | async-start | bytes 5242880 | tf_op jit(solution)/shard_map/all_gather | solution.py:546
  171.6 152.1 %reduce-scatter.23.cloned.1.call-start = ((), (), s32[]{:S(2)}) async-start(), calls=%async_computation.19 | async-start | bytes 5242880 | tf_op jit(solution)/shard_map/reduce_scatter | solution.py:555
  205.7 11.6 copy-start.37
  256.5 11.0 copy-start.44
  256.5 11.1 copy-start.43
  279.1 91.6 %reduce-scatter.21.cloned.1.call-start = ((), (), s32[]{:S(2)}) async-start(), calls=%async_computation.17 | async-start | bytes 5242880 | tf_op jit(solution)/shard_map/reduce_scatter | solution.py:539
  290.3 120.3 %all-gather.11.cloned.1.call-start = ((), (), s32[]{:S(2)}) async-start(), calls=%async_computation.20 | async-start | bytes 5242880 | tf_op jit(solution)/shard_map/all_gather | solution.py:563
  375.9 173.6 %reduce-scatter.41.cloned.1.call-start = ((), (), s32[]{:S(2)}) async-start(), calls=%async_computation.29 | async-start | bytes 6340608 | tf_op jit(solution)/shard_map/reduce_scatter | solution.py:621
  386.2 249.5 %reduce-scatter.39.cloned.1.call-start = ((), (), s32[]{:S(2)}) async-start(), calls=%async_computation.28 | async-start | bytes 6340608 | tf_op jit(solution)/shard_map/reduce_scatter | solution.py:618
  396.9 351.1 %reduce-scatter.37.cloned.1.call-start = ((), (), s32[]{:S(2)}) async-start(), calls=%async_computation.27 | async-start | bytes 6340608 | tf_op jit(solution)/shard_map/reduce_scatter | solution.py:615
  407.3 406.8 %reduce-scatter.45.cloned.1.call-start = ((), (), s32[]{:S(2)}) async-start(), calls=%async_computation.31 | async-start | bytes 589824
  410.6 10.1 copy-start.2
  420.7 40.1 %copy-start.15 = (f32[1024,4]{1,0:T(8,128)S(1)}, f32[1024,4]{1,0:T(8,128)}, u32[]{:S(2)}) copy-start(f32[1024,4]{1,0:T(8,128)} %copy-done.14) | copy-start | bytes 49156
  420.7 40.1 %copy-start.25 = (f32[1024]{0:T(1024)S(1)}, f32[1024]{0:T(1024)}, u32[]{:S(2)}) copy-start(f32[1024]{0:T(1024)} %copy-done.24) | copy-start | bytes 12292
  420.7 40.2 %copy-start.29 = (f32[4]{0:T(128)S(1)}, f32[4]{0:T(128)}, u32[]{:S(2)}) copy-start(f32[4]{0:T(128)} %param.35) | copy-start | bytes 52
  420.7 40.2 %copy-start.31 = (f32[4]{0:T(128)S(1)}, f32[4]{0:T(128)}, u32[]{:S(2)}) copy-start(f32[4]{0:T(128)} %copy-done.30) | copy-start | bytes 52
  457.3 1.2 copy-start.7
  457.3 1.5 copy-start.9
  457.3 4.2 copy-start.17
  465.6 413.3 %reduce-scatter.43.cloned.1.call-start = ((), (), s32[]{:S(2)}) async-start(), calls=%async_computation.30 | async-start | bytes 589824
  466.7 482.7 %reduce-scatter.27.cloned.1.call-start = ((), (), s32[]{:S(2)}) async-start(), calls=%async_computation.22 | async-start | bytes 2359296 | tf_op jit(solution)/shard_map/reduce_scatter | solution.py:594
  473.1 546.9 %reduce-scatter.29.cloned.1.call-start = ((), (), s32[]{:S(2)}) async-start(), calls=%async_computation.23 | async-start | bytes 2359296 | tf_op jit(solution)/shard_map/reduce_scatter | solution.py:597
  479.4 632.1 %reduce-scatter.35.cloned.1.call-start = ((), (), s32[]{:S(2)}) async-start(), calls=%async_computation.26 | async-start | bytes 4718592 | tf_op jit(solution)/shard_map/reduce_scatter | solution.py:612
  489.2 713.4 %reduce-scatter.31.cloned.1.call-start = ((), (), s32[]{:S(2)}) async-start(), calls=%async_computation.24 | async-start | bytes 4718592 | tf_op jit(solution)/shard_map/reduce_scatter | solution.py:600
  498.7 750.8 %reduce-scatter.25.cloned.1.call-start = ((), (), s32[]{:S(2)}) async-start(), calls=%async_computation.21 | async-start | bytes 5242880 | tf_op jit(solution)/shard_map/reduce_scatter | solution.py:577
  499.2 7.0 copy-start.8
  499.2 7.0 copy-start.39
  506.2 5.7 copy-start.34
  506.2 5.7 copy-start.41
  511.9 6.9 copy-start.36
  511.9 6.9 copy-start.40
  518.8 6.9 copy-start.21
  518.8 6.9 copy-start.23
  539.8 802.1 %reduce-scatter.33.cloned.1.call-start = ((), (), s32[]{:S(2)}) async-start(), calls=%async_computation.25 | async-start | bytes 4718592 | tf_op jit(solution)/shard_map/reduce_scatter | solution.py:603
  551.9 697.6 %copy-start.19 = (f32[2048]{0:T(1024)S(1)}, f32[2048]{0:T(1024)}, u32[]{:S(2)}) copy-start(f32[2048]{0:T(1024)} %param.24) | copy-start | bytes 24580
  551.9 697.6 %copy-start.27 = (f32[256]{0:T(256)S(1)}, f32[256]{0:T(256)}, u32[]{:S(2)}) copy-start(f32[256]{0:T(256)} %copy-done.26) | copy-start | bytes 3076
  880.4 463.7 %copy-start.12 = (bf16[256,2048]{1,0:T(8,128)(2,1)S(1)}, bf16[256,2048]{1,0:T(8,128)(2,1)}, u32[]{:S(2)}) copy-start(bf16[256,2048]{1,0:T(8,128)(2,1)} %param.23) | copy-start | bytes 3145732
Sparse Core Ops, SparseCore 0:
  12.2 37.1 all-gather.4
  121.6 44.4 reduce-scatter.18
  171.1 34.4 all-gather.6
  207.2 34.4 all-gather.8
  279.2 44.4 reduce-scatter.22
  326.1 44.4 reduce-scatter.20
  376.1 34.4 all-gather.10
  414.7 108.5 reduce-scatter.40
  527.4 108.2 reduce-scatter.38
  639.7 108.3 reduce-scatter.36
  752.4 61.6 reduce-scatter.44
  817.9 60.9 reduce-scatter.42
  882.8 66.5 reduce-scatter.26
  953.2 66.7 reduce-scatter.28
  1024.0 87.4 reduce-scatter.34
  1114.9 87.6 reduce-scatter.30
  1205.2 44.2 reduce-scatter.24
  1253.0 88.9 reduce-scatter.32

commit v2 on v1

v2 whole, which is shorter than its diff:
```python
import jax
import jax.numpy as jnp
from jax import lax
from jax.experimental import pallas as pl
from jax.experimental.pallas import tpu as pltpu
from jax.sharding import PartitionSpec as P

BLOCK = 64

CHUNK = 128
f32 = jnp.float32
bf16 = jnp.bfloat16


def mm(left, right):
    return lax.dot_general(
        left.astype(bf16), right.astype(bf16), (((1,), (0,)), ((), ())), preferred_element_type=f32
    )


def mm_nt(left, right):
    return lax.dot_general(
        left.astype(bf16), right.astype(bf16), (((1,), (1,)), ((), ())), preferred_element_type=f32
    )


def mm_tn(left, right):
    return lax.dot_general(
        left.astype(bf16), right.astype(bf16), (((0,), (0,)), ((), ())), preferred_element_type=f32
    )


def conv_rows(rows, before, taps):
    count = rows.shape[0]
    longer = jnp.concatenate([before, rows], axis=0)
    total = rows * taps[3:4]
    for tap in range(3):
        total = total + longer[5 + tap : 5 + tap + count] * taps[tap : tap + 1]
    return total


def sigmoid(value):
    return 1.0 / (1.0 + jnp.exp(-value))


def unit_factor(rows):
    return lax.rsqrt(jnp.sum(rows * rows, axis=-1, keepdims=True) + 1e-06)


def chunk_masks():
    down = lax.broadcasted_iota(jnp.int32, (CHUNK, CHUNK), 0)
    across = lax.broadcasted_iota(jnp.int32, (CHUNK, CHUNK), 1)
    return down, across


def softplus(value):
    return jnp.maximum(value, 0.0) + jnp.log1p(jnp.exp(-jnp.abs(value)))


def exact(left, right):
    return jnp.dot(left, right, preferred_element_type=f32, precision=lax.Precision.HIGHEST)


def block_place(chunk, place, per):
    return ((chunk // per) ^ place) * per + chunk % per


def decay_terms(small, log_scale, bias, valid, tri):
    heads = log_scale.shape[1]
    decays = -jnp.exp(log_scale) * softplus(small[:, :heads] + bias) * valid
    running = exact(tri, decays)
    strength = sigmoid(small[:, heads:]) * valid
    cols = jnp.concatenate([running, strength], axis=1)
    wide = jnp.concatenate([cols, jnp.zeros((CHUNK, CHUNK - 2 * heads), f32)], axis=1)
    return cols, jnp.transpose(wide)[: 2 * heads]


def mixer_forward_kernel(
    scal, pq, pk, pv, pg, small, cq, ck, cv, dlog, dbias, gain, s0,
    gated_out, final_out, o_out, delta_out, s_out, tt_out,
    state, tq, tk, tv,
):
    chunk = pl.program_id(0)
    heads = s0.shape[0]
    dk, dv = s0.shape[1], s0.shape[2]
    every = range(heads)

    @pl.when(chunk == 0)
    def _():
        state[...] = s0[...]
        tq[...] = jnp.zeros_like(tq)
        tk[...] = jnp.zeros_like(tk)
        tv[...] = jnp.zeros_like(tv)

    down, across = chunk_masks()
    lower = down > across
    full = down >= across
    level = jnp.where(lower, down ^ across, 0)
    eye = jnp.where(down == across, 1.0, 0.0)
    eye_low = eye.astype(bf16)
    kslice = [slice(h * dk, (h + 1) * dk) for h in every]
    vslice = [slice(h * dv, (h + 1) * dv) for h in every]

    row_at = chunk * CHUNK + lax.broadcasted_iota(jnp.int32, (CHUNK, 1), 0)
    valid = jnp.where(row_at < scal[0], 1.0, 0.0)
    tri = jnp.where(full, 1.0, 0.0)
    gcol, grow = decay_terms(small[...], dlog[...], dbias[...], valid, tri)

    def activated(ref, tail, taps, where):
        pre = conv_rows(ref[:, where].astype(f32), tail[:, where], taps[:, where])
        return pre * sigmoid(pre)

    keys, queries, values = [], [], []
    for h in every:
        u = activated(pk, tk, ck, kslice[h])
        keys.append((u * unit_factor(u)).astype(bf16))
    for h in every:
        u = activated(pq, tq, cq, kslice[h])
        queries.append((u * (unit_factor(u) * dk ** (-0.5))).astype(bf16))
    gc = [gcol[:, h : h + 1] for h in every]
    bc = [gcol[:, heads + h : heads + h + 1] for h in every]
    products = [mm_nt(jnp.concatenate([keys[h], queries[h]], axis=0), keys[h]) for h in every]
    gam = [jnp.exp(jnp.where(full, gc[h] - grow[h : h + 1, :], -1e30)) for h in every]
    system = [jnp.where(lower, products[h][:CHUNK] * gam[h] * bc[h], 0.0) for h in every]
    attend = [(products[h][CHUNK:] * gam[h]).astype(bf16) for h in every]
    system_low = [system[h].astype(bf16) for h in every]
    first = jnp.where(level == 1, 1.0, 0.0).astype(bf16)
    inverse = [eye_low - system_low[h] * first for h in every]
    size = 2
    while size < CHUNK:
        mask = jnp.where((level >= size) & (level < 2 * size), 1.0, 0.0).astype(bf16)
        inner = [mm(system_low[h] * mask, inverse[h]).astype(bf16) for h in every]
        inverse = [inverse[h] - mm(inverse[h], inner[h]).astype(bf16) for h in every]
        size *= 2
    left_over = [
        (eye - inverse[h].astype(f32))
        - mm(system_low[h], inverse[h])
        - mm((system[h] - system_low[h].astype(f32)).astype(bf16), inverse[h])
        for h in every
    ]
    inverse = [(inverse[h].astype(f32) + mm(inverse[h], left_over[h])) for h in every]
    for h in every:
        tt_out[0, h] = jnp.transpose(inverse[h]).astype(bf16)
    inverse = [inverse[h].astype(bf16) for h in every]
    for h in every:
        values.append(activated(pv, tv, cv, vslice[h]))
    for ref, tail in ((pq, tq), (pk, tk), (pv, tv)):
        tail[...] = ref[CHUNK - 16 :, :].astype(f32)[8:]
    growth = [jnp.exp(gc[h]) for h in every]
    keys_f = [keys[h].astype(f32) for h in every]
    pair = [
        jnp.concatenate(
            [(keys_f[h] * growth[h]).astype(bf16), (queries[h].astype(f32) * growth[h]).astype(bf16)], axis=0
        )
        for h in every
    ]
    for h in every:
        s_out[0, h] = state[h].astype(bf16)
    carried = [mm(pair[h], state[h]) for h in every]
    delta = [
        mm(inverse[h], bc[h] * (values[h] - carried[h][:CHUNK])).astype(bf16) for h in every
    ]
    out = [carried[h][CHUNK:] + mm(attend[h], delta[h]) for h in every]
    for h in every:
        last = gc[h][CHUNK - 1 : CHUNK]
        late = (keys_f[h] * jnp.exp(last - gc[h])).astype(bf16)
        state[h] = jnp.exp(last) * state[h] + mm_tn(late, delta[h])
    for h in every:
        delta_out[:, vslice[h]] = delta[h]
        o_out[:, vslice[h]] = out[h].astype(bf16)
        inv = lax.rsqrt(jnp.mean(out[h] * out[h], axis=-1, keepdims=True) + 1e-05)
        gate = pg[:, vslice[h]].astype(f32)
        gated_out[:, vslice[h]] = (
            out[h] * (inv * valid) * gain[...] * (gate * sigmoid(gate))
        ).astype(bf16)

    @pl.when(chunk == pl.num_programs(0) - 1)
    def _():
        final_out[...] = state[...]


def mixer_forward(scal, pq, pk, pv, pg, small, cq, ck, cv, dlog, dbias, gain, s0):
    rows = pq.shape[0]
    heads, dk, dv = s0.shape
    chunks = rows // CHUNK
    per = chunks // 4

    def by_rows(width):
        return pl.BlockSpec((CHUNK, width), lambda c, s: (block_place(c, s[1], per), 0))

    def whole(*shape):
        return pl.BlockSpec(shape, lambda c, s: (0,) * len(shape))

    def by_chunk(*shape):
        return pl.BlockSpec((1,) + shape, lambda c, s: (c,) + (0,) * len(shape))

    kw, vw = heads * dk, heads * dv
    return pl.pallas_call(
        mixer_forward_kernel,
        grid_spec=pltpu.PrefetchScalarGridSpec(
            num_scalar_prefetch=1,
            grid=(chunks,),
            in_specs=[
                by_rows(kw), by_rows(kw), by_rows(vw), by_rows(vw), by_rows(2 * heads),
                whole(4, kw), whole(4, kw), whole(4, vw), whole(1, heads), whole(1, heads),
                whole(1, dv), whole(heads, dk, dv),
            ],
            out_specs=[
                by_rows(vw), whole(heads, dk, dv), by_rows(vw), by_rows(vw),
                by_chunk(heads, dk, dv), by_chunk(heads, CHUNK, CHUNK),
            ],
            scratch_shapes=[
                pltpu.VMEM((heads, dk, dv), f32),
                pltpu.VMEM((8, kw), f32), pltpu.VMEM((8, kw), f32), pltpu.VMEM((8, vw), f32),
            ],
        ),
        out_shape=[
            jax.ShapeDtypeStruct((rows, vw), bf16),
            jax.ShapeDtypeStruct((heads, dk, dv), f32),
            jax.ShapeDtypeStruct((rows, vw), bf16),
            jax.ShapeDtypeStruct((rows, vw), bf16),
            jax.ShapeDtypeStruct((chunks, heads, dk, dv), bf16),
            jax.ShapeDtypeStruct((chunks, heads, CHUNK, CHUNK), bf16),
        ],
        compiler_params=pltpu.CompilerParams(vmem_limit_bytes=48 * 1024 * 1024),
        cost_estimate=pl.CostEstimate(flops=20_000_000_000, bytes_accessed=24_000_000, transcendentals=4_000_000),
        name="mixer_forward",
    )(scal, pq, pk, pv, pg, small, cq, ck, cv, dlog, dbias, gain, s0)


def mixer_backward_kernel(
    scal, pq, pk, pv, pq16, pk16, pv16, small, do_in, delta_in, s_in, tt_in,
    cq, ck, cv, dlog_in, dbias_in,
    dpqk, dpv, dsmall, dcq, dck, dcv, ddecay,
    dstate, nq, nk, nv,
):
    step = pl.program_id(0)
    chunk = pl.num_programs(0) - 1 - step
    heads, dk, dv = dstate.shape
    every = range(heads)

    @pl.when(step == 0)
    def _():
        for ref in (dstate, nq, nk, nv, dcq, dck, dcv, ddecay):
            ref[...] = jnp.zeros_like(ref)

    down, across = chunk_masks()
    lower = down > across
    full = down >= across
    upper = down < across
    ufull = down <= across
    kslice = [slice(h * dk, (h + 1) * dk) for h in every]
    vslice = [slice(h * dv, (h + 1) * dv) for h in every]
    has_before = jnp.where(chunk > 0, 1.0, 0.0)

    def preact(ref, ref16, taps, where):
        pre = conv_rows(
            ref[:, where].astype(f32), ref16[:, where].astype(f32)[8:] * has_before, taps[:, where]
        )
        sig = sigmoid(pre)
        return pre, sig

    def conv_back(dpre, ref, ref16, taps, where, later, dtaps, dref, base=0):
        rows = ref[:, where].astype(f32)
        longer = jnp.concatenate([ref16[:, where].astype(f32)[8:] * has_before, rows], axis=0)
        after = jnp.concatenate([dpre, later[:, where]], axis=0)
        total = dpre * taps[3:4, where]
        sums = [jnp.sum(dpre * longer[5 + tap : 5 + tap + CHUNK], axis=0, keepdims=True) for tap in range(3)]
        sums.append(jnp.sum(dpre * rows, axis=0, keepdims=True))
        for tap in range(3):
            total = total + after[3 - tap : 3 - tap + CHUNK] * taps[tap : tap + 1, where]
        dtaps[:, where] += jnp.concatenate(sums, axis=0)
        later[:, where] = dpre[:8]
        dref[:, where.start + base : where.stop + base] = total.astype(bf16)

    row_at = chunk * CHUNK + lax.broadcasted_iota(jnp.int32, (CHUNK, 1), 0)
    valid = jnp.where(row_at < scal[0], 1.0, 0.0)
    tri = jnp.where(full, 1.0, 0.0)
    gcol, grow = decay_terms(small[...], dlog_in[...], dbias_in[...], valid, tri)
    last_row = lax.broadcasted_iota(jnp.int32, (CHUNK, 1), 0) == CHUNK - 1
    kpre, ksig, kinv, kunit, keys = [], [], [], [], []
    qpre, qsig, qinv, qunit, queries = [], [], [], [], []
    for h in every:
        pre, sig = preact(pk, pk16, ck, kslice[h])
        u = pre * sig
        inv = unit_factor(u)
        kpre.append(pre), ksig.append(sig), kinv.append(inv), kunit.append(u * inv)
        keys.append(kunit[h].astype(bf16))
    for h in every:
        pre, sig = preact(pq, pq16, cq, kslice[h])
        u = pre * sig
        inv = unit_factor(u)
        qpre.append(pre), qsig.append(sig), qinv.append(inv), qunit.append(u * inv)
        queries.append((qunit[h] * dk ** (-0.5)).astype(bf16))
    gc = [gcol[:, h : h + 1] for h in every]
    gr = [grow[h : h + 1, :] for h in every]
    bc = [gcol[:, heads + h : heads + h + 1] for h in every]
    br = [grow[heads + h : heads + h + 1, :] for h in every]
    do = [do_in[:, vslice[h]] for h in every]
    delta = [delta_in[:, vslice[h]] for h in every]
    dnext = [dstate[h].astype(bf16) for h in every]
    growth = [jnp.exp(gc[h]) for h in every]
    ending = [jnp.exp(gc[h][CHUNK - 1 : CHUNK] - gc[h]) for h in every]
    final = [jnp.exp(gc[h][CHUNK - 1 : CHUNK]) for h in every]
    gamma = [jnp.exp(jnp.where(full, gc[h] - gr[h], -1e30)) for h in every]
    gamma_t = [jnp.exp(jnp.where(ufull, gr[h] - gc[h], -1e30)) for h in every]
    kq = [mm_nt(keys[h], queries[h]) for h in every]
    keys_late = [(keys[h].astype(f32) * ending[h]).astype(bf16) for h in every]
    d_delta = [
        mm(
            jnp.concatenate([(kq[h] * gamma_t[h]).astype(bf16), keys_late[h]], axis=1),
            jnp.concatenate([do[h], dnext[h]], axis=0),
        ).astype(bf16)
        for h in every
    ]
    dr = [mm(tt_in[0, h], d_delta[h]) for h in every]
    dr_low = [dr[h].astype(bf16) for h in every]
    both = [jnp.concatenate([do[h], dr_low[h]], axis=0) for h in every]
    pair = [
        jnp.concatenate(
            [
                (queries[h].astype(f32) * growth[h]).astype(bf16),
                (keys[h].astype(f32) * (-growth[h] * bc[h])).astype(bf16),
            ],
            axis=0,
        )
        for h in every
    ]
    state = [s_in[0, h] for h in every]
    new_dstate = [final[h] * dstate[h] + mm_tn(pair[h], both[h]) for h in every]
    dgamma_end = [
        jnp.sum(jnp.sum(state[h].astype(f32) * dstate[h], axis=0, keepdims=True), axis=1, keepdims=True)
        * final[h]
        for h in every
    ]
    d_keys_late = [mm_nt(delta[h], dnext[h]) * ending[h] for h in every]
    for h in every:
        dstate[h] = new_dstate[h]
    strict = [jnp.where(lower, gamma[h] * bc[h], 0.0) for h in every]
    strict_t = [jnp.where(upper, gamma_t[h] * br[h], 0.0) for h in every]
    outer = [mm_nt(both[h], delta[h]) for h in every]
    outer_t = [mm_nt(delta[h], both[h]) for h in every]
    inner = [
        jnp.concatenate(
            [(outer[h][:CHUNK] * gamma[h]).astype(bf16), (-outer[h][CHUNK:] * strict[h]).astype(bf16)], axis=0
        )
        for h in every
    ]
    inner_t = [
        jnp.concatenate(
            [
                (outer_t[h][:, :CHUNK] * gamma_t[h]).astype(bf16),
                (-outer_t[h][:, CHUNK:] * strict_t[h]).astype(bf16),
            ],
            axis=1,
        )
        for h in every
    ]
    by_state = [mm_nt(both[h], state[h]) for h in every]
    by_key = [mm(inner[h], keys[h]) for h in every]
    d_col = [
        mm(inner_t[h], jnp.concatenate([queries[h], keys[h]], axis=0)) + d_keys_late[h] for h in every
    ]
    scal_cols = []
    dbs = []
    for h in every:
        dq = by_key[h][:CHUNK] + by_state[h][:CHUNK] * growth[h]
        d_row = by_key[h][CHUNK:] - by_state[h][CHUNK:] * (growth[h] * bc[h])
        key_f = keys[h].astype(f32)
        q_along = jnp.sum(queries[h].astype(f32) * dq, axis=-1, keepdims=True)
        row_along = jnp.sum(key_f * d_row, axis=-1, keepdims=True)
        col_along = jnp.sum(key_f * d_col[h], axis=-1, keepdims=True)
        late_along = jnp.sum(key_f * d_keys_late[h], axis=-1, keepdims=True)
        at_end = dgamma_end[h] + jnp.sum(late_along, axis=0, keepdims=True)
        scal_cols.append(q_along + row_along - col_along + jnp.where(last_row, at_end, 0.0))
        dbs.append(jnp.sum(dr[h] * delta[h].astype(f32), axis=-1, keepdims=True))
        du = qinv[h] * (dq * dk ** (-0.5) - qunit[h] * q_along)
        dpre = du * (qsig[h] * (1.0 + qpre[h] * (1.0 - qsig[h])))
        conv_back(dpre, pq, pq16, cq, kslice[h], nq, dcq, dpqk)
        du = kinv[h] * (d_row + d_col[h] - kunit[h] * (row_along + col_along))
        dpre = du * (ksig[h] * (1.0 + kpre[h] * (1.0 - ksig[h])))
        conv_back(dpre, pk, pk16, ck, kslice[h], nk, dck, dpqk, heads * dk)
        pre, sig = preact(pv, pv16, cv, vslice[h])
        dpre = dr[h] * bc[h] * (sig * (1.0 + pre * (1.0 - sig)))
        conv_back(dpre, pv, pv16, cv, vslice[h], nv, dcv, dpv)
    da = exact(jnp.where(ufull, 1.0, 0.0), jnp.concatenate(scal_cols, axis=1))
    log_scale, shifted = dlog_in[...], small[:, :heads] + dbias_in[...]
    scale = -jnp.exp(log_scale) * valid
    dpa = da * scale * sigmoid(shifted)
    dpb = jnp.concatenate(dbs, axis=1) * sigmoid(-small[:, heads:])
    dsmall[...] = jnp.concatenate([dpa, dpb], axis=1).astype(bf16)
    along = jnp.concatenate([da * scale * softplus(shifted), dpa], axis=1)
    ddecay[...] += jnp.sum(along, axis=0, keepdims=True)


def mixer_backward(scal, pq, pk, pv, small, do, delta, s, tt, cq, ck, cv, dlog, dbias):
    rows = pq.shape[0]
    chunks, heads, dk, dv = s.shape
    kw, vw = heads * dk, heads * dv
    per = chunks // 4
    fine = CHUNK // 16

    def by_rows(width):
        return pl.BlockSpec((CHUNK, width), lambda c, s: (block_place(chunks - 1 - c, s[1], per), 0))

    def before(width):
        def place(c, s):
            earlier = jnp.maximum(chunks - 2 - c, 0)
            return (block_place(earlier, s[1], per) * fine + fine - 1, 0)

        return pl.BlockSpec((16, width), place)

    def whole(*shape):
        return pl.BlockSpec(shape, lambda c, s: (0,) * len(shape))

    def by_chunk(*shape):
        return pl.BlockSpec((1,) + shape, lambda c, s: (chunks - 1 - c,) + (0,) * len(shape))

    return pl.pallas_call(
        mixer_backward_kernel,
        grid_spec=pltpu.PrefetchScalarGridSpec(
            num_scalar_prefetch=1,
            grid=(chunks,),
            in_specs=[
                by_rows(kw), by_rows(kw), by_rows(vw),
                before(kw), before(kw), before(vw),
                by_rows(2 * heads), by_rows(vw), by_rows(vw),
                by_chunk(heads, dk, dv), by_chunk(heads, CHUNK, CHUNK),
                whole(4, kw), whole(4, kw), whole(4, vw), whole(1, heads), whole(1, heads),
            ],
            out_specs=[
                by_rows(2 * kw), by_rows(vw), by_rows(2 * heads),
                whole(4, kw), whole(4, kw), whole(4, vw), whole(1, 2 * heads),
            ],
            scratch_shapes=[
                pltpu.VMEM((heads, dk, dv), f32),
                pltpu.VMEM((8, kw), f32), pltpu.VMEM((8, kw), f32), pltpu.VMEM((8, vw), f32),
            ],
        ),
        out_shape=[
            jax.ShapeDtypeStruct((rows, 2 * kw), bf16),
            jax.ShapeDtypeStruct((rows, vw), bf16),
            jax.ShapeDtypeStruct((rows, 2 * heads), bf16),
            jax.ShapeDtypeStruct((4, kw), f32),
            jax.ShapeDtypeStruct((4, kw), f32),
            jax.ShapeDtypeStruct((4, vw), f32),
            jax.ShapeDtypeStruct((1, 2 * heads), f32),
        ],
        compiler_params=pltpu.CompilerParams(vmem_limit_bytes=48 * 1024 * 1024),
        cost_estimate=pl.CostEstimate(flops=22_000_000_000, bytes_accessed=28_000_000, transcendentals=6_000_000),
        name="mixer_backward",
    )(scal, pq, pk, pv, pq, pk, pv, small, do, delta, s, tt, cq, ck, cv, dlog, dbias)


def product_tn(left, right):
    return lax.dot_general(
        left, right, (((0,), (0,)), ((), ())), preferred_element_type=jnp.float32
    )


def product_nt(left, right):
    return lax.dot_general(
        left, right, (((1,), (1,)), ((), ())), preferred_element_type=jnp.float32
    )


def row_stats(rows):
    inverse = lax.rsqrt(jnp.mean(rows * rows, axis=-1, keepdims=True) + 1e-05)
    return (rows * inverse, inverse)


def norm_back(scaled, inverse, gain, upstream):
    along = upstream * gain
    inner = jnp.mean(along * scaled, axis=-1, keepdims=True)
    return (inverse * (along - scaled * inner), jnp.sum(upstream * scaled, axis=0))


VMEM_MOST = 56 * 1024 * 1024
COLUMNS = 512
MESH = pl.DeviceIdType.MESH


def flipped(place, mask, count):
    out, bit = 0, 1
    while bit < count:
        here = (place // bit) % 2
        out = out + bit * ((1 - here) if mask & bit else here)
        bit *= 2
    return out


def group_order(groups):
    order, bit = [0], groups // 2
    while bit >= 1:
        order = order + [place | bit for place in order]
        bit //= 2
    return order


def split_order(groups, place):
    half = groups // 2
    bit = place % 2
    return [2 * at + bit for at in range(half)] + [2 * at + 1 - bit for at in range(half)]


def column_order(kind, groups, place):
    if kind == "split":
        return split_order(groups, place)
    return [flipped(place, mask, groups) for mask in group_order(groups)]


def take_columns(array, kind):
    groups = lax.axis_size("dp")
    order = jnp.stack([jnp.asarray(at, jnp.int32) for at in column_order(kind, groups, lax.axis_index("dp"))])
    parts = array.reshape(array.shape[0], groups, array.shape[1] // groups)
    return jnp.take(parts, order, axis=1).reshape(array.shape)


def column_copies(kind, groups, source, target, sems):
    each = source.shape[1] // groups
    found = []
    for at, chunk in enumerate(column_order(kind, groups, lax.axis_index("dp"))):
        start = pl.multiple_of(chunk * each, each)
        found.append(
            pltpu.make_async_copy(
                source.at[:, pl.ds(start, each)], target.at[:, pl.ds(at * each, each)], sems.at[at]
            )
        )
    return found


class Gather:
    def __init__(self, own, held, whole, send_sem, recv_sem, out_sem, groups, kind):
        self.kind = kind
        self.own, self.held, self.whole, self.groups = own, held, whole, groups
        self.send_sem, self.recv_sem, self.out_sem = send_sem, recv_sem, out_sem
        place = lax.axis_index("tensor")
        self.beside = flipped(place, 1, 4)
        self.across = flipped(place, 2, 4)

    def copy(self, source, slot, to):
        rows = self.own.shape[0]
        return pltpu.make_async_remote_copy(
            src_ref=self.held.at[pl.ds(source * rows, rows)],
            dst_ref=self.held.at[pl.ds(slot * rows, rows)],
            send_sem=self.send_sem.at[slot - 1],
            recv_sem=self.recv_sem.at[slot - 1],
            device_id={"tensor": to},
            device_id_type=MESH,
        )

    def copies(self):
        return self.copy(0, 1, self.beside), self.copy(0, 2, self.across), self.copy(2, 3, self.beside)

    def outward(self):
        if self.groups == 1:
            return [pltpu.make_async_copy(self.held, self.whole, self.out_sem.at[0])]
        return column_copies(self.kind, self.groups, self.held, self.whole, self.out_sem)

    def begin(self):
        self.held[pl.ds(0, self.own.shape[0]), :] = self.own[...]
        barrier = pltpu.get_barrier_semaphore()
        for other in (self.beside, self.across):
            pl.semaphore_signal(barrier, inc=1, device_id={"tensor": other}, device_id_type=MESH)
        pl.semaphore_wait(barrier, 2)
        to_beside, to_across, _ = self.copies()
        to_across.start()
        to_beside.start()
        to_beside.wait_recv()

    def second(self):
        _, to_across, forward = self.copies()
        to_across.wait_recv()
        forward.start()
        forward.wait_recv()
        for copy in self.outward():
            copy.start()

    def end(self):
        for copy in self.copies():
            copy.wait_send()
        for copy in self.outward():
            copy.wait()

    def at(self, step, steps):
        pl.when(step == 0)(self.begin)
        pl.when(step == steps // 2)(self.second)

    def rows(self, half):
        count = 2 * self.own.shape[0]
        return self.held[pl.ds(pl.multiple_of(half * count, count), count), :]


def gather_call(kernel, name, collective, steps, own, operands, in_specs, out_specs, out_shape, flops, nbytes, kind, more=()):
    rows, width = own.shape
    groups = lax.axis_size("dp")
    if (width // groups) % 128:
        groups = 1

    def body(own_ref, *refs):
        count = len(operands)
        outs = refs[count : count + len(out_shape)]
        whole, held, send_sem, recv_sem, out_sem = refs[count + len(out_shape) :][:5]
        gather = Gather(own_ref, held, whole, send_sem, recv_sem, out_sem, groups, kind)
        outs = outs + refs[count + len(out_shape) + 5 :]
        step = pl.program_id(0)
        gather.at(step, steps)
        kernel(step, gather, *refs[:count], *outs)
        pl.when(step == steps - 1)(gather.end)

    outs = pl.pallas_call(
        body,
        name=name,
        grid=(steps,),
        in_specs=[pl.BlockSpec((rows, width), lambda j: (0, 0))] + in_specs,
        out_specs=out_specs + [pl.BlockSpec(memory_space=pl.ANY)],
        out_shape=out_shape + [jax.ShapeDtypeStruct((4 * rows, width), own.dtype)],
        scratch_shapes=[
            pltpu.VMEM((4 * rows, width), own.dtype),
            pltpu.SemaphoreType.DMA((3,)),
            pltpu.SemaphoreType.DMA((3,)),
            pltpu.SemaphoreType.DMA((groups,)),
        ]
        + list(more),
        compiler_params=pltpu.CompilerParams(
            vmem_limit_bytes=VMEM_MOST, collective_id=collective, has_side_effects=True
        ),
        cost_estimate=pl.CostEstimate(flops=flops, bytes_accessed=nbytes, transcendentals=0),
    )(own, *operands)
    if groups == 1:
        outs = list(outs[:-1]) + [take_columns(outs[-1], kind)]
    return outs


def project_kernel(step, gather, wq, wk, wv, wg, ws, pq, pk, pv, pg, small):
    steps = [(wq, pq), (wk, pk), (wv, pv), (wv, pv), (wg, pg), (wg, pg)]
    half = step // 6

    def run(weight, out):
        out[...] = mm(gather.rows(half), weight[...]).astype(bf16)

    for at, (weight, out) in enumerate(steps):
        pl.when(step % 6 == at)(lambda weight=weight, out=out: run(weight, out))

    @pl.when(step % 6 == 0)
    def _():
        small[...] = mm(gather.rows(half), ws[...])


def project(own, weights):
    rows, width = own.shape
    pair = 2 * rows
    n_small = weights[4].shape[1]
    places = [
        lambda j: 0,
        lambda j: 0,
        lambda j: jnp.clip(j % 6 - 2, 0, 1),
        lambda j: jnp.clip(j % 6 - 4, 0, 1),
    ]
    in_specs = [pl.BlockSpec((width, COLUMNS), lambda j, place=place: (0, place(j))) for place in places]
    in_specs.append(pl.BlockSpec((width, n_small), lambda j: (0, 0)))
    out_specs = [pl.BlockSpec((pair, COLUMNS), lambda j, place=place: (j // 6, place(j))) for place in places]
    out_specs.append(pl.BlockSpec((pair, n_small), lambda j: (j // 6, 0)))
    out_shape = [jax.ShapeDtypeStruct((2 * pair, weight.shape[1]), bf16) for weight in weights[:4]]
    out_shape.append(jax.ShapeDtypeStruct((2 * pair, n_small), f32))
    return gather_call(
        project_kernel, "project", 0, 12, own, weights, in_specs, out_specs, out_shape,
        40_000_000_000, 40_000_000, "flip",
    )


def feed_kernel(blocks, step, gather, e, wg, wu, wd, hidden, d_gate, d_up, e_split, e_sem):
    groups = e_sem.shape[0]
    half = step // blocks
    count = e.shape[0] // 2

    def copies():
        if groups == 1:
            return [pltpu.make_async_copy(e, e_split, e_sem.at[0])]
        return column_copies("split", groups, e, e_split, e_sem)

    @pl.when(step == 0)
    def _():
        for copy in copies():
            copy.start()

    x = gather.rows(half)
    gate = mm_nt(x, wg[...])
    up = mm_nt(x, wu[...])
    back = mm_nt(e[pl.ds(pl.multiple_of(half * count, count), count), :], wd[...])
    sig = sigmoid(gate)
    act = gate * sig
    hidden[...] = (act * up).astype(bf16)
    d_gate[...] = (back * up * (sig + act * (1.0 - sig))).astype(bf16)
    d_up[...] = (back * act).astype(bf16)

    @pl.when(step == 2 * blocks - 1)
    def _():
        for copy in copies():
            copy.wait()


def feed(own, e, wg, wu, wd):
    rows, width = own.shape
    pair = 2 * rows
    units = wd.shape[0]
    blocks = pl.cdiv(units, COLUMNS)
    groups = lax.axis_size("dp")
    if (width // groups) % 128:
        groups = 1
    by_rows = pl.BlockSpec((COLUMNS, width), lambda j: (j % blocks, 0))
    outs = gather_call(
        lambda *refs: feed_kernel(blocks, *refs), "feed", 1, 2 * blocks, own, [e, wg, wu, wd],
        [pl.BlockSpec((2 * pair, width), lambda j: (0, 0)), by_rows, by_rows, by_rows],
        [pl.BlockSpec((pair, COLUMNS), lambda j: (j // blocks, j % blocks))] * 3
        + [pl.BlockSpec(memory_space=pl.ANY)],
        [jax.ShapeDtypeStruct((2 * pair, units), bf16)] * 3
        + [jax.ShapeDtypeStruct((2 * pair, width), bf16)],
        40_000_000_000, 40_000_000, "split", [pltpu.SemaphoreType.DMA((groups,))],
    )
    if groups == 1:
        outs[3] = take_columns(outs[3], "split")
    return outs


def gate_back_kernel(heads, step, gather, length, w, pg, o_in, gain, dpg, do, dgain):
    pair = 2 * gather.own.shape[0]
    each = pair // 2
    dv = gain.shape[1]
    half = step // 2

    @pl.when(step == 0)
    def _():
        dgain[...] = jnp.zeros_like(dgain)

    at = half * pair + lax.broadcasted_iota(jnp.int32, (pair, 1), 0)
    at = (at // each ^ lax.axis_index("tensor").astype(jnp.int32)) * each + at % each
    valid = jnp.where(at < length[0], 1.0, 0.0)
    upstream = mm_nt(gather.rows(half), w[...]) * valid
    for head in range(heads):
        where = slice(head * dv, (head + 1) * dv)
        dg = upstream[:, where]
        gate = pg[:, where].astype(f32)
        sig = sigmoid(gate)
        act = gate * sig
        o = o_in[:, where].astype(f32)
        inv = lax.rsqrt(jnp.mean(o * o, axis=-1, keepdims=True) + 1e-05)
        norm = o * inv
        through = dg * norm
        dgain[...] += jnp.sum(through * act, axis=0, keepdims=True)
        dpg[:, where] = (through * gain[...] * (sig + act * (1.0 - sig))).astype(bf16)
        dn = dg * gain[...] * act
        do[:, where] = (inv * (dn - norm * jnp.mean(dn * norm, axis=-1, keepdims=True))).astype(bf16)


def gate_back(own, length, w_out, pg, o, gain):
    rows, width = own.shape
    pair = 2 * rows
    dv = gain.shape[1]
    heads = w_out.shape[0] // dv // 2
    by_head = pl.BlockSpec((pair, heads * dv), lambda j: (j // 2, j % 2))
    return gather_call(
        lambda *refs: gate_back_kernel(heads, *refs), "gate_back", 2, 4, own, [length, w_out, pg, o, gain],
        [
            pl.BlockSpec(memory_space=pltpu.SMEM),
            pl.BlockSpec((heads * dv, width), lambda j: (j % 2, 0)),
            by_head, by_head,
            pl.BlockSpec((1, dv), lambda j: (0, 0)),
        ],
        [by_head, by_head, pl.BlockSpec((1, dv), lambda j: (0, 0))],
        [
            jax.ShapeDtypeStruct(pg.shape, bf16),
            jax.ShapeDtypeStruct(pg.shape, bf16),
            jax.ShapeDtypeStruct((1, dv), f32),
        ],
        30_000_000_000, 30_000_000, "flip",
    )


def scatter_kernel(turned, count, *refs):
    lefts, rights, out = refs[:count], refs[count : 2 * count], refs[2 * count]
    far_own, leave, other, send_sem, recv_sem = refs[2 * count + 1 :]
    step = pl.program_id(0)
    parts = pl.num_programs(0) // 2
    rows = out.shape[0]
    place = lax.axis_index("tensor")
    beside, across = flipped(place, 1, 4), flipped(place, 2, 4)
    multiply = mm_nt if turned else mm
    CORNER, NEAR, ACROSS = 0, 1, 2

    def columns(part):
        return pl.ds(pl.multiple_of(part * COLUMNS, COLUMNS), COLUMNS)

    def copy(kind, part):
        return pltpu.make_async_remote_copy(
            src_ref=leave.at[kind, :, columns(part)],
            dst_ref=other.at[kind, :, columns(part)],
            send_sem=send_sem.at[kind, part],
            recv_sem=recv_sem.at[kind, part],
            device_id={"tensor": across if kind == ACROSS else beside},
            device_id_type=MESH,
        )

    def product():
        total = multiply(lefts[0][...], rights[0][...])
        for at in range(1, count):
            total = total + multiply(lefts[at][...], rights[at][...])
        return total

    def pass_on(part):
        copy(CORNER, part).wait_recv()
        both = far_own[:, columns(part)] + other[CORNER, :, columns(part)].astype(f32)
        leave[ACROSS, :, columns(part)] = both.astype(bf16)
        copy(ACROSS, part).start()

    @pl.when(step == 0)
    def _():
        barrier = pltpu.get_barrier_semaphore()
        for to in (beside, across):
            pl.semaphore_signal(barrier, inc=1, device_id={"tensor": to}, device_id_type=MESH)
        pl.semaphore_wait(barrier, 2)

    part = step % parts

    @pl.when(step < parts)
    def _():
        total = product()
        far_own[:, columns(part)] = total[:rows]
        leave[CORNER, :, columns(part)] = total[rows:].astype(bf16)
        copy(CORNER, part).start()

        @pl.when(step > 0)
        def _():
            pass_on(part - 1)

    @pl.when(step >= parts)
    def _():
        @pl.when(step == parts)
        def _():
            pass_on(parts - 1)

        total = product()
        out[:, columns(part)] = total[:rows]
        leave[NEAR, :, columns(part)] = total[rows:].astype(bf16)
        copy(NEAR, part).start()

    @pl.when(step == 2 * parts - 1)
    def _():
        def finish(part, carry):
            copy(NEAR, part).wait_recv()
            copy(ACROSS, part).wait_recv()
            where = columns(part)
            out[:, where] = (
                out[:, where] + other[NEAR, :, where].astype(f32) + other[ACROSS, :, where].astype(f32)
            )
            for kind in (CORNER, NEAR, ACROSS):
                copy(kind, part).wait_send()
            return carry

        lax.fori_loop(0, parts, finish, 0)


def scatter_products(lefts, rights, turned, collective):
    lefts = [left if isinstance(left, tuple) else (left, 0, left.shape[1]) for left in lefts]
    rows = lefts[0][0].shape[0] // 4
    width = rights[0].shape[0 if turned else 1]
    parts = width // COLUMNS
    total = sum(left[2] for left in lefts)
    flops = 8 * rows * width * total

    def left_spec(block, size):
        return pl.BlockSpec((2 * rows, size), lambda j: (1 - j // parts, block))

    def right_spec(right):
        if turned:
            return pl.BlockSpec((COLUMNS, right.shape[1]), lambda j: (j % parts, 0))
        return pl.BlockSpec((right.shape[0], COLUMNS), lambda j: (0, j % parts))

    return pl.pallas_call(
        lambda *refs: scatter_kernel(turned, len(lefts), *refs),
        name="scatter_products",
        grid=(2 * parts,),
        in_specs=[left_spec(block, size) for _, block, size in lefts] + [right_spec(right) for right in rights],
        out_specs=pl.BlockSpec((rows, width), lambda j: (0, 0)),
        out_shape=jax.ShapeDtypeStruct((rows, width), f32),
        scratch_shapes=[
            pltpu.VMEM((rows, width), f32),
            pltpu.VMEM((3, rows, width), bf16),
            pltpu.VMEM((3, rows, width), bf16),
            pltpu.SemaphoreType.DMA((3, parts)),
            pltpu.SemaphoreType.DMA((3, parts)),
        ],
        compiler_params=pltpu.CompilerParams(
            vmem_limit_bytes=VMEM_MOST, collective_id=collective, has_side_effects=True
        ),
        cost_estimate=pl.CostEstimate(flops=2 * flops, bytes_accessed=4 * total * width, transcendentals=0),
    )(*[left[0] for left in lefts], *rights)


def low_bit(chunk, groups):
    return groups if chunk == 0 else chunk & -chunk


def reduce_plan(groups, early, late):
    chunks = [chunk for chunk in group_order(groups) if chunk % 2 == 0]
    chunks.sort(key=lambda chunk: low_bit(chunk, groups))
    levels = max(groups.bit_length() - 2, 1)
    plan = []
    for at, tensor in enumerate(late):
        for position, chunk in enumerate(chunks):
            level = low_bit(chunk, groups).bit_length() - 2
            lag = 2.5 * level / levels if chunk == 0 else 0.5 * level
            plan.append((at * len(chunks) + position + lag, tensor, chunk))
    for at, tensor in enumerate(early):
        for position, chunk in enumerate(chunks):
            level = low_bit(chunk, groups).bit_length() - 2
            plan.append((2 * at - 1 + 2 * level + 0.01 * position, tensor, chunk))
    return [step[1:] for step in sorted(plan)], chunks


def reduce_kernel(groups, count, *refs):
    leaves, refs = refs[:count], refs[count:]
    small, gains, partial, resid, refs = refs[0], refs[1], refs[2], refs[3], refs[4:]
    outs, refs = refs[:count], refs[count:]
    small_out, gains_out, mixed, refs = refs[0], refs[1], refs[2], refs[3:]
    lands, refs = refs[:count], refs[count:]
    sends, refs = refs[:count], refs[count:]
    keeps, refs = refs[:count], refs[count:]
    small_land, gains_land, gains_first, rows_leave, rows_land = refs[:5]
    send_sem, recv_sem, sum_send, sum_recv, rows_send, rows_recv, keep_sem = refs[5:]
    place = lax.axis_index("dp")
    beside = lax.axis_index("tensor")
    order = group_order(groups)
    position = {chunk: at for at, chunk in enumerate(order)}
    bits = [1 << at for at in range(groups.bit_length() - 1)]
    each = outs[0].shape[0]
    across_core = {"tensor": flipped(beside, 1, 4)}
    across_chip = {"tensor": flipped(beside, 2, 4)}

    def rows(at):
        return pl.ds(at * each, each)

    def copy(tensor, chunk):
        source = (
            leaves[tensor].at[rows(position[chunk])] if chunk % 2 else sends[tensor].at[rows(chunk // 2 - 1)]
        )
        return pltpu.make_async_remote_copy(
            src_ref=source,
            dst_ref=lands[tensor].at[rows(chunk - 1)],
            send_sem=send_sem.at[tensor * groups + chunk],
            recv_sem=recv_sem.at[tensor * groups + chunk],
            device_id={"dp": flipped(place, low_bit(chunk, groups), groups)},
            device_id_type=MESH,
        )

    def keep_copy(tensor):
        return pltpu.make_async_copy(
            leaves[tensor].at[pl.ds(0, keeps[tensor].shape[0])], keeps[tensor], keep_sem.at[tensor]
        )

    for tensor in range(count):
        keep_copy(tensor).start()
    kept = set()
    partners = [{"dp": flipped(place, bit, groups)} for bit in bits] + [across_core, across_chip]
    barrier = pltpu.get_barrier_semaphore()
    for partner in partners:
        pl.semaphore_signal(barrier, inc=1, device_id=partner, device_id_type=MESH)
    pl.semaphore_wait(barrier, len(partners))

    plan, chunks = reduce_plan(groups, [], list(range(count)))
    pieces = [(tensor, chunk + 1) for tensor in range(count) for chunk in chunks]
    started = []

    def send_piece():
        if len(started) < len(pieces):
            copy(*pieces[len(started)]).start()
            started.append(1)

    for _ in range(3):
        send_piece()

    def plain_copy(source, land, sems, at, partner):
        return pltpu.make_async_remote_copy(
            src_ref=source, dst_ref=land, send_sem=sems[0].at[at], recv_sem=sems[1].at[at],
            device_id=partner, device_id_type=MESH,
        )

    quarter = mixed.shape[0]
    blocks = [pl.ds(at * quarter, quarter) for at in range(4)]
    row_sems = (rows_send, rows_recv)
    corner = plain_copy(partial.at[blocks[3]], rows_land.at[0], row_sems, 0, across_core)
    near = plain_copy(partial.at[blocks[1]], rows_land.at[1], row_sems, 1, across_core)
    far = plain_copy(rows_leave, rows_land.at[2], row_sems, 2, across_chip)
    corner.start()
    near.start()

    gains_first[0] = gains[...]
    small_land[0] = small[...]
    sum_sems = (sum_send, sum_recv)
    hops = [across_core, across_chip] + [{"dp": flipped(place, bit, groups)} for bit in bits]
    gains_copies = [
        plain_copy(gains_first.at[at], gains_land.at[at], sum_sems, at, partner)
        for at, partner in enumerate(hops)
    ]
    small_copies = [
        plain_copy(small_land.at[2 * at], small_land.at[2 * at + 1], sum_sems, len(hops) + at, partner)
        for at, partner in enumerate(hops[2:])
    ]
    gains_copies[0].start()
    small_copies[0].start()
    done = {"gains": 0, "small": 0}

    def next_sum():
        at = done["gains"]
        if at < len(gains_copies):
            gains_copies[at].wait_recv()
            total = gains_first[at] + gains_land[at]
            if at + 1 < len(gains_copies):
                gains_first[at + 1] = total
                gains_copies[at + 1].start()
            else:
                gains_out[...] = total
            done["gains"] += 1
        at = done["small"]
        if at < len(small_copies):
            small_copies[at].wait_recv()
            total = small_land[2 * at] + small_land[2 * at + 1]
            if at + 1 < len(small_copies):
                small_land[2 * at + 2] = total
                small_copies[at + 1].start()
            else:
                small_out[...] = total
            done["small"] += 1

    for index, (tensor, chunk) in enumerate(plan):
        if index == 1:
            corner.wait_recv()
            rows_leave[...] = (
                partial[blocks[2], :].astype(f32) + rows_land[0].astype(f32)
            ).astype(bf16)
            far.start()
        if tensor not in kept:
            keep_copy(tensor).wait()
            kept.add(tensor)
        total = keeps[tensor][rows(position[chunk]), :].astype(f32)
        for bit in bits:
            if bit >= low_bit(chunk, groups):
                break
            copy(tensor, chunk + bit).wait_recv()
            if bit == 1:
                send_piece()
            total = total + lands[tensor][rows(chunk + bit - 1), :].astype(f32)
        if chunk:
            sends[tensor][rows(chunk // 2 - 1), :] = total.astype(bf16)
            copy(tensor, chunk).start()
        else:
            outs[tensor][...] = total
        if index >= 2 and index % 2 == 0:
            next_sum()
        if index == 6:
            near.wait_recv()
            far.wait_recv()
            mixed[...] = (
                resid[...]
                + partial[blocks[0], :].astype(f32)
                + rows_land[1].astype(f32)
                + rows_land[2].astype(f32)
            ).astype(bf16)
    while done["gains"] < len(gains_copies):
        next_sum()
    for tensor in range(count):
        for chunk in range(1, groups):
            copy(tensor, chunk).wait_send()
    for sent in gains_copies + small_copies + [corner, near, far]:
        sent.wait_send()


def reduce_groups(grads, small, gains, partial, resid, collective):
    count = len(grads)
    groups = lax.axis_size("dp")
    bits = groups.bit_length() - 1
    each = grads[0].shape[0] // groups
    rows, width = resid.shape
    widths = [grad.shape[1] for grad in grads]
    vmem = pl.BlockSpec(memory_space=pltpu.VMEM)
    out_shape = [jax.ShapeDtypeStruct((each, size), f32) for size in widths]
    out_shape += [jax.ShapeDtypeStruct(small.shape, f32), jax.ShapeDtypeStruct(gains.shape, f32)]
    out_shape += [jax.ShapeDtypeStruct((rows, width), bf16)]
    return pl.pallas_call(
        lambda *refs: reduce_kernel(groups, count, *refs),
        name="reduce_groups",
        in_specs=[pl.BlockSpec(memory_space=pl.ANY)] * count + [vmem] * 4,
        out_specs=[vmem] * len(out_shape),
        out_shape=out_shape,
        scratch_shapes=[pltpu.VMEM(((groups - 1) * each, size), bf16) for size in widths]
        + [pltpu.VMEM(((groups // 2 - 1) * each, size), bf16) for size in widths]
        + [pltpu.VMEM((groups // 2 * each, size), bf16) for size in widths]
        + [
            pltpu.VMEM((2 * bits,) + small.shape, f32),
            pltpu.VMEM((bits + 2,) + gains.shape, f32),
            pltpu.VMEM((bits + 2,) + gains.shape, f32),
            pltpu.VMEM((rows, width), bf16),
            pltpu.VMEM((3, rows, width), bf16),
            pltpu.SemaphoreType.DMA((count * groups,)),
            pltpu.SemaphoreType.DMA((count * groups,)),
            pltpu.SemaphoreType.DMA((2 * bits + 2,)),
            pltpu.SemaphoreType.DMA((2 * bits + 2,)),
            pltpu.SemaphoreType.DMA((3,)),
            pltpu.SemaphoreType.DMA((3,)),
            pltpu.SemaphoreType.DMA((count,)),
        ],
        compiler_params=pltpu.CompilerParams(
            vmem_limit_bytes=VMEM_MOST, collective_id=collective, has_side_effects=True
        ),
        cost_estimate=pl.CostEstimate(flops=100_000_000_000, bytes_accessed=300_000_000, transcendentals=0),
    )(*grads, small, gains, partial, resid)


def product_nn(left, right):
    return jnp.dot(left, right, preferred_element_type=jnp.float32)


def tie(value, after):
    return lax.optimization_barrier((value, after))[0]


def together(*values):
    return lax.optimization_barrier(values)


def flip(array, axis, bit):
    size = lax.axis_size(axis)
    return lax.ppermute(array, axis, [(place, place ^ bit) for place in range(size)])


def in_order(array):
    groups = lax.axis_size("dp")
    place = lax.axis_index("dp").astype(jnp.int32)
    found = jnp.array(group_order(groups), jnp.int32)[jnp.arange(groups, dtype=jnp.int32) ^ place]
    return jnp.take(array.reshape(array.shape[0], groups, -1), found, axis=1)


def leaving(left, right):
    quarter = right.shape[1] // 4
    return [
        product_tn(left, right[:, at * quarter : (at + 1) * quarter]).astype(jnp.bfloat16) for at in (2, 3)
    ]


def settle(left, right, others):
    half = right.shape[1] // 2
    other = jnp.concatenate(others, axis=1).astype(jnp.float32)
    total = (product_tn(left, right[:, :half]) + other).astype(jnp.bfloat16)
    groups = lax.axis_size("dp")
    alike = [[place for place in range(groups) if place % 2 == bit] for bit in (0, 1)]
    return lax.psum_scatter(
        total, "dp", scatter_dimension=1, axis_index_groups=alike, tiled=True
    ).astype(jnp.float32)


def pack(parts):
    flat = jnp.concatenate([part.reshape(-1) for part in parts])
    return jnp.pad(flat, (0, -flat.shape[0] % 1024)).reshape(-1, 1024)


def unpack(flat, parts):
    flat, at, out = flat.reshape(-1), 0, []
    for part in parts:
        out.append(flat[at : at + part.size].reshape(part.shape))
        at += part.size
    return out


def per_device(
    tokens,
    norm1_gain,
    w_query,
    w_key,
    w_value,
    w_gate_out,
    w_decay,
    w_beta,
    conv_query,
    conv_key,
    conv_value,
    decay_log,
    decay_bias,
    head_gain,
    w_out,
    norm2_gain,
    w_gate,
    w_up,
    w_down,
    state_in,
    seq_blocks,
    seq_tail,
    cotangent,
):
    width = tokens.shape[1]
    heads = decay_log.shape[0]
    rows_in = tokens.astype(jnp.float32)
    scaled1, inverse1 = row_stats(rows_in)
    normed1 = (scaled1 * norm1_gain).astype(jnp.bfloat16)
    seq_length = (BLOCK * (seq_blocks - 1) + seq_tail).astype(jnp.int32)
    place = lax.axis_index("tensor").astype(jnp.int32)
    scal = jnp.stack([seq_length[0], place])
    gain_row, log_row, bias_row = head_gain[None], decay_log[None], decay_bias[None]
    w_small = jnp.concatenate([w_decay, w_beta], axis=1)
    weights1 = (w_query, w_key, w_value, w_gate_out, w_small)
    p_query, p_key, p_value, p_gate, p_small, gathered1 = project(normed1, weights1)
    cotangent = tie(cotangent, p_small)
    e_beside, e_across = flip(cotangent, "tensor", 1), flip(cotangent, "tensor", 2)
    gated, final, mixer_out, delta, states, inverse_t = mixer_forward(
        scal, p_query, p_key, p_value, p_gate, p_small,
        conv_query, conv_key, conv_value, log_row, bias_row, gain_row, state_in[0],
    )
    gated, e_across = together(gated, e_across)
    e_corner = flip(e_across, "tensor", 1)
    cot_full = jnp.concatenate([cotangent, e_beside, e_across, e_corner], axis=0)
    resid = rows_in + scatter_products([gated], [w_out], False, 3)
    scaled2, inverse2 = row_stats(resid)
    normed2 = (scaled2 * norm2_gain).astype(jnp.bfloat16)
    hidden, d_gate, d_up, cot_split, split2 = feed(normed2, cot_full, w_gate.T, w_up.T, w_down)
    down_one, down_two = leaving(hidden, cot_split)
    d_gate, d_up, down_one = together(d_gate, d_up, down_one)
    down_one = flip(down_one, "dp", 1)
    d_normed2 = scatter_products([d_gate, d_up], [w_gate.T, w_up.T], False, 4)
    d_normed2, down_one, d_gate, d_up = together(d_normed2, down_one, d_gate, d_up)
    d_resid_part, grad_norm2 = norm_back(scaled2, inverse2, norm2_gain, d_normed2)
    d_resid = (cotangent.astype(jnp.float32) + d_resid_part).astype(jnp.bfloat16)
    d_resid, down_two = together(d_resid, down_two)
    down_two = flip(down_two, "dp", 1)
    dp_gate, do, dgain, resid_full = gate_back(d_resid, seq_length, w_out, p_gate, mixer_out, gain_row)
    do, dp_gate, dgain, resid_full, down_two = together(do, dp_gate, dgain, resid_full, down_two)
    grad_down = settle(hidden, cot_split, (down_one, down_two))
    up_one, up_two = leaving(d_up, split2)
    do, up_one, up_two = together(do, up_one, up_two)
    up_one, up_two = flip(up_one, "dp", 1), flip(up_two, "dp", 1)
    mixer_grads = mixer_backward(
        scal, p_query, p_key, p_value, p_small, do, delta, states, inverse_t,
        conv_query, conv_key, conv_value, log_row, bias_row,
    )
    dp_pair, dp_value, dp_small, dc_query, dc_key, dc_value, ddecay, up_one, up_two = together(
        *mixer_grads, up_one, up_two
    )
    grad_up = settle(d_up, split2, (up_one, up_two))
    gate_one, gate_two = leaving(d_gate, split2)
    dp_small, gate_one, gate_two = together(dp_small, gate_one, gate_two)
    gate_one, gate_two = flip(gate_one, "dp", 1), flip(gate_two, "dp", 1)
    key_width = w_query.shape[1]
    d_normed1 = scatter_products(
        [(dp_pair, 0, key_width), (dp_pair, 1, key_width), dp_value, dp_gate, dp_small],
        weights1, True, 5,
    )
    grad_out = product_tn(resid_full, gated).astype(jnp.bfloat16)
    grad_gate_out = product_tn(gathered1, dp_gate).astype(jnp.bfloat16)
    grad_value = product_tn(gathered1, dp_value).astype(jnp.bfloat16)
    grad_pair = product_tn(gathered1, dp_pair).astype(jnp.bfloat16)
    grad_small = in_order(product_tn(dp_small, gathered1))
    d_normed1, gate_one, gate_two = together(d_normed1, gate_one, gate_two)
    grad_gate = settle(d_gate, split2, (gate_one, gate_two))
    d_tokens_part, grad_norm1 = norm_back(scaled1, inverse1, norm1_gain, d_normed1)
    tokens_grad = (d_resid.astype(jnp.float32) + d_tokens_part).astype(jnp.bfloat16)
    partial = product_nn(hidden, w_down).astype(jnp.bfloat16)
    small_parts = [dc_query, dc_key, dc_value, ddecay, grad_small]
    gain_parts = [grad_norm1, grad_norm2, dgain]
    grad_out, grad_gate_out, grad_value, grad_pair, small_sum, gain_sum, mixed = reduce_groups(
        [grad_out, grad_gate_out, grad_value, grad_pair],
        pack(small_parts), pack(gain_parts), partial, resid, 6,
    )
    dc_query, dc_key, dc_value, ddecay, grad_small = unpack(small_sum, small_parts)
    grad_norm1, grad_norm2, dgain = unpack(gain_sum, gain_parts)
    grad_small = lax.dynamic_index_in_dim(grad_small, lax.axis_index("dp"), 1, keepdims=False).T
    return (
        mixed,
        final[None],
        tokens_grad,
        grad_norm1,
        grad_pair[:, :key_width],
        grad_pair[:, key_width:],
        grad_value,
        grad_gate_out,
        grad_small[:, :heads],
        grad_small[:, heads:],
        dc_query,
        dc_key,
        dc_value,
        ddecay[0, :heads],
        ddecay[0, heads:],
        dgain[0],
        grad_out.T,
        grad_norm2,
        grad_gate.T,
        grad_up.T,
        grad_down,
    )


def solution(mesh):
    in_specs = (
        P(("dp", "tensor"), None),
        P(),
        P(None, "tensor"),
        P(None, "tensor"),
        P(None, "tensor"),
        P(None, "tensor"),
        P(None, "tensor"),
        P(None, "tensor"),
        P(None, "tensor"),
        P(None, "tensor"),
        P(None, "tensor"),
        P("tensor"),
        P("tensor"),
        P(),
        P("tensor", None),
        P(),
        P(None, "tensor"),
        P(None, "tensor"),
        P("tensor", None),
        P("dp", "tensor", None, None),
        P("dp"),
        P("dp"),
        P(("dp", "tensor"), None),
    )
    out_specs = (
        P(("dp", "tensor"), None),
        P("dp", "tensor", None, None),
        P(("dp", "tensor"), None),
        P(),
        P("dp", "tensor"),
        P("dp", "tensor"),
        P("dp", "tensor"),
        P("dp", "tensor"),
        P("dp", "tensor"),
        P("dp", "tensor"),
        P(None, "tensor"),
        P(None, "tensor"),
        P(None, "tensor"),
        P("tensor"),
        P("tensor"),
        P(),
        P("tensor", "dp"),
        P(),
        P("dp", "tensor"),
        P("dp", "tensor"),
        P("tensor", "dp"),
    )
    return jax.shard_map(
        per_device, mesh=mesh, in_specs=in_specs, out_specs=out_specs, check_vma=False
    )
```

time: 1360 us -> 695 us (0.51)
  waiting for transfers between devices: 902 us -> 10.7 us
  Pallas kernels: 68.1 us -> 515 us
  matrix products: 228 us -> 88.5 us
  blocking collectives: 78.2 us -> 0 us
  other arithmetic: 47 us -> 24.6 us
    reduce_scatter x12 -> x3, waiting for transfers between devices: 725 us -> 0.01 us  [settle(): lax.psum_scatter(total, 'dp', scatter_dimension=1, axis_index_groups=alik...]
    pallas_call x2 -> x9, Pallas kernels: 68.1 us -> 515 us  [the longest x1 223 us: reduce_groups(): pl.pallas_call(lambda *refs: reduce_kernel(groups, count, *refs), name='r...]
    dot_general x20 -> x1, matrix products: 153 us -> 11.1 us  [product_nn(): return jnp.dot(left, right, preferred_element_type=jnp.float32)]
    unnamed x20 -> x3, waiting for transfers between devices: 88.8 us -> 0.05 us
    all_gather x4 -> x0, waiting for transfers between devices: 88 us -> none  [the longest x1 35.9 us: per_device(): gathered1 = lax.all_gather(normed1, 'tensor', axis=0, tiled=True)]
    psum x2 -> x0, blocking collectives: 78.2 us -> none  [the longest x1 42.2 us: per_device(): lax.psum((grad_norm1, grad_norm2, mixer_grads[6]), ('dp', 'tensor'))]
    convert_element_type x19 -> x1, other arithmetic: 20.9 us -> 2.39 us  [settle(): return lax.psum_scatter(total, 'dp', scatter_dimension=1, axis_index_grou...]
    dot_general x9 -> x14, matrix products: 75 us -> 77.4 us  [product_tn(): lax.dot_general(left, right, (((0,), (0,)), ((), ())), preferred_element_...]
  transfers between devices with their start and end apart: 18 -> 12, of which waited for: 17 -> 2; matrix products, arithmetic and copies ran while one was open for 14% -> 15% of each run, Pallas kernels for 3% -> 62%
where the time goes in v2:
time: 695 us; the launch traced here: 686 us
  Pallas kernels  515 us (74%)
  matrix products  88.5 us (13%)
  other arithmetic  24.6 us (4%)
  local copies, waits for them, and re-layouts  23.7 us (3%)
  between operations  16.1 us (2%)
  waiting for transfers between devices  10.7 us (2%)
  starting transfers between devices  7.86 us (1%)
    pallas_call x1, Pallas kernels, reduce_groups(): pl.pallas_call(lambda *refs: reduce_kernel(groups, count, *refs), name='r...  223 us
    pallas_call x3, Pallas kernels, gather_call(): pl.pallas_call(body, name=name, grid=(steps,), in_specs=[pl.BlockSpec((ro...  122 us
    pallas_call x3, Pallas kernels, scatter_products(): pl.pallas_call(lambda *refs: scatter_kernel(turned, len(lefts), *refs), n...  99.5 us
    dot_general x14, matrix products, product_tn(): lax.dot_general(left, right, (((0,), (0,)), ((), ())), preferred_element_...  77.4 us
    pallas_call x1, Pallas kernels, mixer_backward(): pl.pallas_call(mixer_backward_kernel, grid_spec=pltpu.PrefetchScalarGridS...  36.8 us
    pallas_call x1, Pallas kernels, mixer_forward(): pl.pallas_call(mixer_forward_kernel, grid_spec=pltpu.PrefetchScalarGridSp...  33.6 us
  transfers between devices with their start and end apart: 12, of which 2 were waited for; matrix products, arithmetic and copies ran while one was open for 15% of the time, Pallas kernels for 62%

profile of v2, /device:TPU:0, one launch (start us, length us, event | category | flops | bytes accessed | tf_op | source)
XLA Modules:
  0.0 686.2 jit_solution(17994719888389620223)
XLA Ops:
  7.2 1.5 fusion.11
  8.8 0.8 pad_maximum_fusion.1
  9.5 1.0 copy.55.refs_4_.refs_9_
  10.5 2.5 fusion.4.own_ref
  13.1 43.9 %project.1 = (bf16[1024,512]{1,0:T(8,128)(2,1)}, bf16[1024,512]{1,0:T(8,128)(2,1)}, bf16[1024,1024]{1,0:T(8,128)(2,1)}, bf16[1024,1024]{1,0:T(8,128)(2,1)}, f32[...) custom-call(bf16[256,2048]{1,0:T(8,128)(2,1)} %fusion.4.own_ref, bf16[2048,512]{1,0:T(8,128)(2,1)} %refs_5_.1, ...), custom_call_target="tpu_custom_call" | custom-call | flops 40000000000 | bytes 40000000 | tf_op jit(solution)/shard_map/project/pallas_call | solution.py:611
  57.2 1.3 collective-permute-start.1
  59.9 1.2 copy-done.10
  61.1 1.2 copy-done.12
  62.3 1.0 copy-done.16
  63.4 33.6 %mixer_forward.1 = (bf16[1024,1024]{1,0:T(8,128)(2,1)}, f32[4,128,256]{2,1,0:T(8,128)}, bf16[1024,1024]{1,0:T(8,128)(2,1)}, bf16[1024,1024]{1,0:T(8,128)(2,1)}, ...) custom-call(s32[2]{0:T(128)S(1)} %pad_add_fusion.scal, bf16[1024,512]{1,0:T(8,128)(2,1)S(1)} %copy-done.10, ...), custom_call_target="tpu_custom_call" | custom-call | flops 20000000000 | bytes 24000000 | tf_op jit(solution)/shard_map/mixer_forward/pallas_call | solution.py:198
  96.9 1.0 copy-done.14
  97.9 0.6 gather_fusion
  98.6 0.6 pad_clamp_fusion
  99.7 31.0 %scatter_products.3 = f32[256,2048]{1,0:T(8,128)} custom-call(bf16[1024,1024]{1,0:T(8,128)(2,1)} %get-tuple-element.98.refs_0_, bf16[1024,2048]{1,0:T(8,128)(2,1)} %refs_1_.5), custom_call_target="tpu_custom_call" | custom-call | flops 8589934592 | bytes 8388608 | tf_op jit(solution)/shard_map/scatter_products/pallas_call | solution.py:879
  130.7 2.0 multiply_reduce_fusion.2
  132.7 1.5 multiply_convert_fusion.own_ref
  134.2 3.4 pad_maximum_fusion.refs_0_
  137.5 43.0 %feed.1 = (bf16[1024,1376]{1,0:T(8,128)(2,1)}, bf16[1024,1376]{1,0:T(8,128)(2,1)}, bf16[1024,1376]{1,0:T(8,128)(2,1)}, bf16[1024,2048]{1,0:T(8,128)(2,1)}, bf16[1024,2048]{1,0:T(8,128)(2,1)}) custom-call(bf16[256,2048]{1,0:T(8,128)(2,1)} %multiply_convert_fusion.own_ref, bf16[1024,2048]{1,0:T(8,128)(2,1)} %pad_maximum_fusion.refs_0_, ...), custom_call_target="tpu_custom_call" | custom-call | flops 40000000000 | bytes 40000000 | tf_op jit(solution)/shard_map/feed/pallas_call | solution.py:611
  180.5 5.0 convolution_convert_fusion.9
  185.5 4.0 convolution_convert_fusion.10
  189.5 1.5 collective-permute-start.3
  191.0 34.1 %scatter_products.4 = f32[256,2048]{1,0:T(8,128)} custom-call(bf16[1024,1376]{1,0:T(8,128)(2,1)} %get-tuple-element.141.refs_0_, bf16[1024,1376]{1,0:T(8,128)(2,1)} %get-tuple-element.119.refs_1_, bf16[1376,2048]{1,0:T(8,128)(2,1)} %bitcast.97, bf16[1376,2048]{1,0:T(8,128)(2,1)} %bitcast.99), custom_call_target="tpu_custom_call" | custom-call | flops 23085449216 | bytes 22544384 | tf_op jit(solution)/shard_map/scatter_products/pallas_call | solution.py:879
  225.1 11.1 %convolution_convert_fusion.refs_6_ = bf16[1024,2048]{1,0:T(8,128)(2,1)} fusion(bf16[1024,1376]{1,0:T(8,128)(2,1)} %get-tuple-element.102, bf16[1376,2048]{1,0:T(8,128)(2,1)} %refs_3_.3), kind=kOutput, calls=%fused_computation.6 | convolution fusion | flops 5773459456 | bytes 12648448 | tf_op jit(solution)/shard_map/dot_general | solution.py:1120
  236.8 1.6 add_convert_fusion.3.own_ref
  238.4 0.8 collective-permute-start.4
  239.2 34.7 %gate_back.1 = (bf16[1024,1024]{1,0:T(8,128)(2,1)}, bf16[1024,1024]{1,0:T(8,128)(2,1)}, f32[1,256]{1,0:T(1,128)}, bf16[1024,2048]{1,0:T(8,128)(2,1)}) custom-call(bf16[256,2048]{1,0:T(8,128)(2,1)} %add_convert_fusion.3.own_ref, s32[1]{0:T(128)S(6)} %add.78.refs_0_, bf16[1024,2048]{1,0:T(8,128)(2,1)} %refs_1_.5, ...), custom_call_target="tpu_custom_call" | custom-call | flops 30000001024 | bytes 30000000 | tf_op jit(solution)/shard_map/gate_back/pallas_call | solution.py:611
  273.9 4.0 convolution_convert_fusion.7
  277.9 4.2 convolution_convert_fusion.8
  282.0 5.1 add_convert_fusion
  287.3 5.0 convolution_convert_fusion.5
  292.3 2.8 convolution_convert_fusion.6
  295.1 1.6 collective-permute-start.5
  297.1 36.8 %mixer_backward.1 = (bf16[1024,1024]{1,0:T(8,128)(2,1)S(1)}, bf16[1024,1024]{1,0:T(8,128)(2,1)}, bf16[1024,8]{1,0:T(8,128)(2,1)S(1)}, f32[4,512]{1,0:T(4,128)S(1...) custom-call(s32[2]{0:T(128)S(1)} %pad_add_fusion.scal, bf16[1024,512]{1,0:T(8,128)(2,1)S(1)} %copy-done.11, ...), custom_call_target="tpu_custom_call" | custom-call | flops 22000001024 | bytes 28000000 | tf_op jit(solution)/shard_map/mixer_backward/pallas_call | solution.py:419
  334.0 9.3 %convolution_convert_fusion.4.refs_0_ = bf16[2048,1024]{1,0:T(8,128)(2,1)} fusion(bf16[1024,2048]{1,0:T(8,128)(2,1)} %get-tuple-element.115, bf16[1024,1024]{1,0:T(8,128)(2,1)S(1)} %copy-done.45), kind=kOutput, calls=%fused_computation.10 | convolution fusion | flops 4297064448 | bytes 10485760 | tf_op jit(solution)/shard_map/dot_general | solution.py:456
  343.3 6.3 convolution_convert_fusion.3.refs_1_
  349.6 9.0 %collective-permute-done.6 = bf16[1376,512]{1,0:T(8,128)(2,1)S(1)} collective-permute-done((bf16[1376,512]{1,0:T(8,128)(2,1)}, bf16[1376,512]{1,0:T(8,128)(2,1)S(1)}, u32[]{:S(2)}, u32[]{:S(2)}) %collective-permute-start.6) | collective-permute-done | bytes 1409056 | tf_op jit(solution)/shard_map/ppermute | solution.py:1133
  358.6 1.8 collective-permute-start.7
  360.6 5.1 add_convert_fusion.1
  365.8 8.4 %convolution_convert_fusion.1.refs_3_ = bf16[2048,1024]{1,0:T(8,128)(2,1)} fusion(bf16[1024,2048]{1,0:T(8,128)(2,1)} %get-tuple-element.116, bf16[1024,1024]{1,0:T(8,128)(2,1)S(1)} %get-tuple-element.135.refs_0_.refs_1_), kind=kOutput, calls=%fused_computation.7 | convolution fusion | flops 4297064448 | bytes 10485760 | tf_op jit(solution)/shard_map/dot_general | solution.py:456
  374.2 34.4 %scatter_products.5 = f32[256,2048]{1,0:T(8,128)} custom-call(bf16[1024,1024]{1,0:T(8,128)(2,1)} %copy-done.9, bf16[1024,1024]{1,0:T(8,128)(2,1)} %copy-done.9, bf16[1024,1024]{1,0:T(8,128)(2,1)} %get-tuple-element.134.refs_2_, bf16[1024,1024]{1,0:T(8,128)(2,1)} %get-tuple-element.117.refs_3_, bf16[1024,8]{1,0:T(8,128)(2,1)} %copy-done, ...), custom_call_target="tpu_custom_call" | custom-call | flops 25836912640 | bytes 25231360 | tf_op jit(solution)/shard_map/scatter_products/pallas_call | solution.py:879
  408.6 0.7 fusion.26
  409.3 0.7 gather_fusion.1
  410.3 0.7 reshape.163.refs_4_
  411.0 9.7 %convolution_convert_fusion.2.refs_2_ = bf16[2048,1024]{1,0:T(8,128)(2,1)} fusion(bf16[1024,2048]{1,0:T(8,128)(2,1)} %get-tuple-element.116, bf16[1024,1024]{1,0:T(8,128)(2,1)} %get-tuple-element.134.refs_2_), kind=kOutput, calls=%fused_computation.8 | convolution fusion | flops 4297064448 | bytes 10485760 | tf_op jit(solution)/shard_map/dot_general | solution.py:456
  420.7 1.7 collective-permute-done.8
  422.4 0.7 fusion.6
  423.1 0.6 reshape.165.refs_5_
  423.7 8.0 %add_convert_fusion.2 = bf16[1376,1024]{1,0:T(8,128)(2,1)} fusion(bf16[1024,1376]{1,0:T(8,128)(2,1)} %get-tuple-element.141.refs_0_, bf16[1376,512]{1,0:T(8,128)(2,1)} %collective-permute-done.8, bf16[1376,512]{1,0:T(8,128)(2,1)} %collective-permute-done.7, bf16[1024,2048]{1,0:T(8,128)(2,1)} %get-tuple-element.120), kind=kOutput, calls=%fused_computation.4 | convolution fusion | flops 2894135296 | bytes 10616832 | tf_op jit(solution)/shard_map/dot_general | solution.py:456
  431.7 223.3 %reduce_groups.1 = (f32[256,1024]{1,0:T(8,128)}, f32[256,1024]{1,0:T(8,128)}, f32[256,1024]{1,0:T(8,128)}, f32[256,1024]{1,0:T(8,128)}, f32[25,1024]{1,0:T(8,128...) custom-call(bf16[2048,1024]{1,0:T(8,128)(2,1)} %convolution_convert_fusion.4.refs_0_, ...), custom_call_target="tpu_custom_call" | custom-call | flops 99999997952 | bytes 300000000 | tf_op jit(solution)/shard_map/reduce_groups/pallas_call | solution.py:1089
  655.0 0.9 reshape.166
  655.9 1.4 slice.85
  657.3 2.5 copy.58
  660.0 0.8 fusion.24
  660.8 0.6 reshape.168
  661.4 0.6 reshape.169
  662.1 0.8 reshape.171
  665.2 2.2 fusion.23
  667.4 1.7 fusion.10
  669.2 2.4 convert_element_type.105
  671.5 2.4 convert_bitcast_fusion
  673.9 2.4 convert_bitcast_fusion.1
  676.3 1.0 copy.79
  677.3 1.0 copy.80
  678.3 1.0 copy.81
  (139 shorter events, 5.1 us)
Async XLA Ops:
  7.2 662.0 %reduce-scatter.8.cloned.1.call-start = ((), (), s32[]{:S(2)}) async-start(), calls=%async_computation.5 | async-start | bytes 3522560 | tf_op jit(solution)/shard_map/reduce_scatter | solution.py:1156
  8.8 1.8 copy-start.34
  13.0 43.9 %copy-start.27 = (bf16[256,2048]{1,0:T(8,128)(2,1)S(1)}, bf16[256,2048]{1,0:T(8,128)(2,1)}, u32[]{:S(2)}) copy-start(bf16[256,2048]{1,0:T(8,128)(2,1)} %param.46) | copy-start | bytes 3145732
  13.0 46.8 %copy-start.2 = (f32[1,4,128,256]{3,2,1,0:T(8,128)S(1)}, f32[1,4,128,256]{3,2,1,0:T(8,128)}, u32[]{:S(2)}) copy-start(f32[1,4,128,256]{3,2,1,0:T(8,128)} %param.43) | copy-start | bytes 1572868
  13.0 46.8 %copy-start.3 = (f32[4,1024]{1,0:T(4,128)S(1)}, f32[4,1024]{1,0:T(4,128)}, u32[]{:S(2)}) copy-start(f32[4,1024]{1,0:T(4,128)} %cv.3) | copy-start | bytes 49156
  13.0 46.8 %copy-start.4 = (f32[4,512]{1,0:T(4,128)S(1)}, f32[4,512]{1,0:T(4,128)}, u32[]{:S(2)}) copy-start(f32[4,512]{1,0:T(4,128)} %cq.3) | copy-start | bytes 24580
  13.1 46.8 %copy-start.5 = (f32[4,512]{1,0:T(4,128)S(1)}, f32[4,512]{1,0:T(4,128)}, u32[]{:S(2)}) copy-start(f32[4,512]{1,0:T(4,128)} %ck.3) | copy-start | bytes 24580
  13.1 46.8 %copy-start.6 = (f32[256]{0:T(256)S(1)}, f32[256]{0:T(256)}, u32[]{:S(2)}) copy-start(f32[256]{0:T(256)} %param.37) | copy-start | bytes 3076
  13.1 46.8 %copy-start.7 = (f32[4]{0:T(128)S(1)}, f32[4]{0:T(128)}, u32[]{:S(2)}) copy-start(f32[4]{0:T(128)} %param.35) | copy-start | bytes 52
  13.1 46.8 %copy-start.8 = (f32[4]{0:T(128)S(1)}, f32[4]{0:T(128)}, u32[]{:S(2)}) copy-start(f32[4]{0:T(128)} %param.36) | copy-start | bytes 52
  57.0 42.7 %collective-permute-start = (bf16[256,2048]{1,0:T(8,128)(2,1)S(1)}, bf16[256,2048]{1,0:T(8,128)(2,1)S(1)}, u32[]{:S(2)}, u32[]{:S(2)}) collective-permute-start(bf16[256,2048]{1,0:T(8,128)(2,1)S(1)} %copy-done.27), channel_id=1, source_target_pairs={{0,2},{1,3},{2,0},{3,1},{4,6},{5,7},{6,4},{7,5},{8,10},{9,11},{10,... | collective-permute-start | bytes 3145736 | tf_op jit(solution)/shard_map/ppermute | solution.py:1133
  57.2 77.0 %collective-permute-start.1 = (bf16[256,2048]{1,0:T(8,128)(2,1)S(1)}, bf16[256,2048]{1,0:T(8,128)(2,1)}, u32[]{:S(2)}, u32[]{:S(2)}) collective-permute-start(bf16[256,2048]{1,0:T(8,128)(2,1)S(1)} %copy-done.27), channel_id=1, source_target_pairs={{0,1},{1,0},{2,3},{3,2},{4,5},{5,4},{6,7},{7,6},{8,9},{9,8},{10,11... | collective-permute-start | bytes 3145736 | tf_op jit(solution)/shard_map/ppermute | solution.py:1133
  59.9 1.2 copy-start.10
  61.1 1.2 copy-start.12
  62.3 1.0 copy-start.16
  63.4 34.6 %copy-start.18 = (s32[8]{0:T(128)S(1)}, s32[8]{0:T(128)}, u32[]{:S(2)}) copy-start(s32[8]{0:T(128)} %constant.50.clone) | copy-start | bytes 100
  96.9 1.0 copy-start.14
  99.7 31.0 %copy-start.20 = (bf16[256,2048]{1,0:T(8,128)(2,1)S(1)}, bf16[256,2048]{1,0:T(8,128)(2,1)}, u32[]{:S(2)}) copy-start(bf16[256,2048]{1,0:T(8,128)(2,1)} %param.24) | copy-start | bytes 3145732
  99.7 34.5 %collective-permute-start.2 = (bf16[256,2048]{1,0:T(8,128)(2,1)S(1)}, bf16[256,2048]{1,0:T(8,128)(2,1)S(1)}, u32[]{:S(2)}, u32[]{:S(2)}) collective-permute-start(bf16[256,2048]{1,0:T(8,128)(2,1)S(1)} %collective-permute-done), channel_id=1, source_target_pairs={{0,1},{1,0},{2,3},{3,2},{4,5},{5,4},{6,7},{7,6},{8,9},{9,8},{10,11... | collective-permute-start | bytes 3145736 | tf_op jit(solution)/shard_map/ppermute | solution.py:1133
  130.7 2.0 copy-start.31
  132.7 104.1 %copy-start.19 = (f32[256,2048]{1,0:T(8,128)}, f32[256,2048]{1,0:T(8,128)S(1)}, u32[]{:S(2)}) copy-start(f32[256,2048]{1,0:T(8,128)S(1)} %get-tuple-element.250.refs_7_) | copy-start | bytes 6291460
  180.5 5.0 copy-start.43
  189.5 46.7 %collective-permute-start.3 = (bf16[1376,512]{1,0:T(8,128)(2,1)}, bf16[1376,512]{1,0:T(8,128)(2,1)S(1)}, u32[]{:S(2)}, u32[]{:S(2)}) collective-permute-start(bf16[1376,512]{1,0:T(8,128)(2,1)} %convolution_convert_fusion.10), channel_id=1, source_target_pairs={{0,4},{4,0},{8,12},{12,8},{16,20},{20,16},{24,28},{28,24},{1,5},{5... | collective-permute-start | bytes 4227080 | tf_op jit(solution)/shard_map/ppermute | solution.py:1133
  225.1 11.1 %copy-start.22 = (f32[256,2048]{1,0:T(8,128)S(1)}, f32[256,2048]{1,0:T(8,128)}, u32[]{:S(2)}) copy-start(f32[256,2048]{1,0:T(8,128)} %scatter_products.4) | copy-start | bytes 6291460
  238.4 43.6 %collective-permute-start.4 = (bf16[1376,512]{1,0:T(8,128)(2,1)}, bf16[1376,512]{1,0:T(8,128)(2,1)S(1)}, u32[]{:S(2)}, u32[]{:S(2)}) collective-permute-start(bf16[1376,512]{1,0:T(8,128)(2,1)} %convolution_convert_fusion.9), channel_id=1, source_target_pairs={{0,4},{4,0},{8,12},{12,8},{16,20},{20,16},{24,28},{28,24},{1,5},{5... | collective-permute-start | bytes 4227080 | tf_op jit(solution)/shard_map/ppermute | solution.py:1133
  239.2 34.7 %copy-start.41 = (bf16[1024,1376]{1,0:T(8,128)(2,1)S(1)}, bf16[1024,1376]{1,0:T(8,128)(2,1)}, u32[]{:S(2)}) copy-start(bf16[1024,1376]{1,0:T(8,128)(2,1)} %get-tuple-element.119.refs_1_) | copy-start | bytes 8454148
  277.9 4.2 copy-start.39
  277.9 4.2 copy-start.44
  287.2 5.1 copy-start.40
  287.2 384.3 %reduce-scatter.6.cloned.1.call-start = ((), (), s32[]{:S(2)}) async-start(), calls=%async_computation.4 | async-start | bytes 3522560 | tf_op jit(solution)/shard_map/reduce_scatter | solution.py:1156
  287.2 5.0 copy-start.38
  292.3 4.8 copy-start.11
  292.3 4.8 copy-start.13
  292.3 4.8 copy-start.15
  292.3 4.8 copy-start.17
  295.1 54.5 %collective-permute-start.5 = (bf16[1376,512]{1,0:T(8,128)(2,1)}, bf16[1376,512]{1,0:T(8,128)(2,1)S(1)}, u32[]{:S(2)}, u32[]{:S(2)}) collective-permute-start(bf16[1376,512]{1,0:T(8,128)(2,1)} %convolution_convert_fusion.8), channel_id=1, source_target_pairs={{0,4},{4,0},{8,12},{12,8},{16,20},{20,16},{24,28},{28,24},{1,5},{5... | collective-permute-start | bytes 4227080 | tf_op jit(solution)/shard_map/ppermute | solution.py:1133
  296.7 61.9 %collective-permute-start.6 = (bf16[1376,512]{1,0:T(8,128)(2,1)}, bf16[1376,512]{1,0:T(8,128)(2,1)S(1)}, u32[]{:S(2)}, u32[]{:S(2)}) collective-permute-start(bf16[1376,512]{1,0:T(8,128)(2,1)} %convolution_convert_fusion.7), channel_id=1, source_target_pairs={{0,4},{4,0},{8,12},{12,8},{16,20},{20,16},{24,28},{28,24},{1,5},{5... | collective-permute-start | bytes 4227080 | tf_op jit(solution)/shard_map/ppermute | solution.py:1133
  297.1 36.8 %copy-start.45 = (bf16[1024,1024]{1,0:T(8,128)(2,1)S(1)}, bf16[1024,1024]{1,0:T(8,128)(2,1)}, u32[]{:S(2)}) copy-start(bf16[1024,1024]{1,0:T(8,128)(2,1)} %get-tuple-element.98.refs_0_) | copy-start | bytes 6291460
  333.9 9.3 %copy-start = (bf16[1024,8]{1,0:T(8,128)(2,1)}, bf16[1024,8]{1,0:T(8,128)(2,1)S(1)}, u32[]{:S(2)}) copy-start(bf16[1024,8]{1,0:T(8,128)(2,1)S(1)} %get-tuple-element.142.refs_4_) | copy-start | bytes 49156
  333.9 31.9 %copy-start.9 = (bf16[1024,1024]{1,0:T(8,128)(2,1)}, bf16[1024,1024]{1,0:T(8,128)(2,1)S(1)}, u32[]{:S(2)}) copy-start(bf16[1024,1024]{1,0:T(8,128)(2,1)S(1)} %get-tuple-element.135.refs_0_.refs_1_) | copy-start | bytes 6291460
  333.9 9.3 %copy-start.24 = (bf16[1024,2048]{1,0:T(8,128)(2,1)S(1)}, bf16[1024,2048]{1,0:T(8,128)(2,1)}, u32[]{:S(2)}) copy-start(bf16[1024,2048]{1,0:T(8,128)(2,1)} %get-tuple-element.116) | copy-start | bytes 12582916
  334.0 9.3 %copy-start.46 = (bf16[1024,1024]{1,0:T(8,128)(2,1)S(1)}, bf16[1024,1024]{1,0:T(8,128)(2,1)}, u32[]{:S(2)}) copy-start(bf16[1024,1024]{1,0:T(8,128)(2,1)} %get-tuple-element.117.refs_3_) | copy-start | bytes 6291460
  343.3 17.4 %copy-start.42 = (bf16[1024,1376]{1,0:T(8,128)(2,1)S(1)}, bf16[1024,1376]{1,0:T(8,128)(2,1)}, u32[]{:S(2)}) copy-start(bf16[1024,1376]{1,0:T(8,128)(2,1)} %get-tuple-element.119.refs_1_) | copy-start | bytes 8454148
  358.6 62.1 %collective-permute-start.7 = (bf16[1376,512]{1,0:T(8,128)(2,1)}, bf16[1376,512]{1,0:T(8,128)(2,1)}, u32[]{:S(2)}, u32[]{:S(2)}) collective-permute-start(bf16[1376,512]{1,0:T(8,128)(2,1)} %convolution_convert_fusion.6), channel_id=1, source_target_pairs={{0,4},{4,0},{8,12},{12,8},{16,20},{20,16},{24,28},{28,24},{1,5},{5... | collective-permute-start | bytes 4227080 | tf_op jit(solution)/shard_map/ppermute | solution.py:1133
  360.4 61.9 %collective-permute-start.8 = (bf16[1376,512]{1,0:T(8,128)(2,1)}, bf16[1376,512]{1,0:T(8,128)(2,1)}, u32[]{:S(2)}, u32[]{:S(2)}) collective-permute-start(bf16[1376,512]{1,0:T(8,128)(2,1)} %convolution_convert_fusion.5), channel_id=1, source_target_pairs={{0,4},{4,0},{8,12},{12,8},{16,20},{20,16},{24,28},{28,24},{1,5},{5... | collective-permute-start | bytes 4227080 | tf_op jit(solution)/shard_map/ppermute | solution.py:1133
  365.8 308.2 %reduce-scatter.4.cloned.1.call-start = ((), (), s32[]{:S(2)}) async-start(), calls=%async_computation.3 | async-start | bytes 3522560 | tf_op jit(solution)/shard_map/reduce_scatter | solution.py:1156
  374.2 34.4 %copy-start.1 = (bf16[1024,8]{1,0:T(8,128)(2,1)S(1)}, bf16[1024,8]{1,0:T(8,128)(2,1)}, u32[]{:S(2)}) copy-start(bf16[1024,8]{1,0:T(8,128)(2,1)} %copy-done) | copy-start | bytes 49156
  374.2 34.4 %copy-start.25 = (bf16[1024,2048]{1,0:T(8,128)(2,1)S(1)}, bf16[1024,2048]{1,0:T(8,128)(2,1)}, u32[]{:S(2)}) copy-start(bf16[1024,2048]{1,0:T(8,128)(2,1)} %get-tuple-element.116) | copy-start | bytes 12582916
  408.6 1.4 copy-start.37
  411.0 11.3 %copy-start.21 = (bf16[256,2048]{1,0:T(8,128)(2,1)S(1)}, bf16[256,2048]{1,0:T(8,128)(2,1)}, u32[]{:S(2)}) copy-start(bf16[256,2048]{1,0:T(8,128)(2,1)} %param.24) | copy-start | bytes 3145732
  411.0 11.3 %copy-start.23 = (f32[256,2048]{1,0:T(8,128)S(1)}, f32[256,2048]{1,0:T(8,128)}, u32[]{:S(2)}) copy-start(f32[256,2048]{1,0:T(8,128)} %scatter_products.5) | copy-start | bytes 6291460
  411.0 11.3 %copy-start.32 = (f32[2048]{0:T(1024)S(1)}, f32[2048]{0:T(1024)}, u32[]{:S(2)}) copy-start(f32[2048]{0:T(1024)} %param.25) | copy-start | bytes 24580
  411.0 11.3 %copy-start.35 = (f32[256]{0:T(256)S(1)}, f32[256]{0:T(256)}, u32[]{:S(2)}) copy-start(f32[256]{0:T(256)} %copy-done.34) | copy-start | bytes 3076
  420.7 2.4 copy-start.36
  655.0 9.6 %copy-start.33 = (f32[5,1024]{1,0:T(8,128)S(1)}, f32[5,1024]{1,0:T(8,128)}, u32[]{:S(2)}) copy-start(f32[5,1024]{1,0:T(8,128)} %get-tuple-element.149) | copy-start | bytes 61444
  662.8 4.6 copy-start.26
  669.2 7.2 %copy-start.30 = (bf16[256,2048]{1,0:T(8,128)(2,1)S(1)}, bf16[256,2048]{1,0:T(8,128)(2,1)}, u32[]{:S(2)}) copy-start(bf16[256,2048]{1,0:T(8,128)(2,1)} %get-tuple-element.284) | copy-start | bytes 3145732
  671.5 5.8 copy-start.29
  673.9 4.3 copy-start.28
Sparse Core Ops, SparseCore 0:
  287.3 57.1 reduce-scatter.7
  365.9 56.0 reduce-scatter.5
  431.8 78.2 reduce-scatter.3

commit v3 on v2

--- a/solution.py
+++ b/solution.py
@@ -8,6 +8,7 @@
 BLOCK = 64
 
 CHUNK = 128
+LITTLE = pl.CostEstimate(flops=1, bytes_accessed=1, transcendentals=0)
 f32 = jnp.float32
 bf16 = jnp.bfloat16
 
@@ -222,16 +223,16 @@
             jax.ShapeDtypeStruct((chunks, heads, dk, dv), bf16),
             jax.ShapeDtypeStruct((chunks, heads, CHUNK, CHUNK), bf16),
         ],
-        compiler_params=pltpu.CompilerParams(vmem_limit_bytes=48 * 1024 * 1024),
-        cost_estimate=pl.CostEstimate(flops=20_000_000_000, bytes_accessed=24_000_000, transcendentals=4_000_000),
+        compiler_params=pltpu.CompilerParams(vmem_limit_bytes=56 * 1024 * 1024),
+        cost_estimate=LITTLE,
         name="mixer_forward",
     )(scal, pq, pk, pv, pg, small, cq, ck, cv, dlog, dbias, gain, s0)
 
 
 def mixer_backward_kernel(
     scal, pq, pk, pv, pq16, pk16, pv16, small, do_in, delta_in, s_in, tt_in,
-    cq, ck, cv, dlog_in, dbias_in,
-    dpqk, dpv, dsmall, dcq, dck, dcv, ddecay,
+    cq, ck, cv, dlog_in, dbias_in, left_one, right_one, left_two, right_two, left_three, right_three,
+    dpqk, dpv, dsmall, dcq, dck, dcv, ddecay, product_one, product_two, product_three,
     dstate, nq, nk, nv,
 ):
     step = pl.program_id(0)
@@ -244,6 +245,9 @@
         for ref in (dstate, nq, nk, nv, dcq, dck, dcv, ddecay):
             ref[...] = jnp.zeros_like(ref)
 
+    product_one[...] = mm_tn(left_one[...], right_one[...]).astype(bf16)
+    product_two[...] = mm_tn(left_two[...], right_two[...]).astype(bf16)
+    product_three[...] = mm(left_three[...], right_three[...]).astype(bf16)
     down, across = chunk_masks()
     lower = down > across
     full = down >= across
@@ -393,12 +397,15 @@
     ddecay[...] += jnp.sum(along, axis=0, keepdims=True)
 
 
-def mixer_backward(scal, pq, pk, pv, small, do, delta, s, tt, cq, ck, cv, dlog, dbias):
+def mixer_backward(scal, pq, pk, pv, small, do, delta, s, tt, cq, ck, cv, dlog, dbias, one, two, three):
     rows = pq.shape[0]
     chunks, heads, dk, dv = s.shape
     kw, vw = heads * dk, heads * dv
     per = chunks // 4
     fine = CHUNK // 16
+    (left_one, right_one), (left_two, right_two), (left_three, right_three) = one, two, three
+    width = left_one.shape[1]
+    each_one, each_two = width // chunks, width // 2 // chunks
 
     def by_rows(width):
         return pl.BlockSpec((CHUNK, width), lambda c, s: (block_place(chunks - 1 - c, s[1], per), 0))
@@ -427,10 +434,16 @@
                 by_rows(2 * heads), by_rows(vw), by_rows(vw),
                 by_chunk(heads, dk, dv), by_chunk(heads, CHUNK, CHUNK),
                 whole(4, kw), whole(4, kw), whole(4, vw), whole(1, heads), whole(1, heads),
+                pl.BlockSpec((rows, each_one), lambda c, s: (0, c)), whole(*right_one.shape),
+                pl.BlockSpec((rows, each_two), lambda c, s: (0, chunks + c)), whole(*right_two.shape),
+                pl.BlockSpec((CHUNK, left_three.shape[1]), lambda c, s: (c, 0)), whole(*right_three.shape),
             ],
             out_specs=[
                 by_rows(2 * kw), by_rows(vw), by_rows(2 * heads),
                 whole(4, kw), whole(4, kw), whole(4, vw), whole(1, 2 * heads),
+                pl.BlockSpec((each_one, right_one.shape[1]), lambda c, s: (c, 0)),
+                pl.BlockSpec((each_two, right_two.shape[1]), lambda c, s: (c, 0)),
+                pl.BlockSpec((CHUNK, right_three.shape[1]), lambda c, s: (c, 0)),
             ],
             scratch_shapes=[
                 pltpu.VMEM((heads, dk, dv), f32),
@@ -445,11 +458,17 @@
             jax.ShapeDtypeStruct((4, kw), f32),
             jax.ShapeDtypeStruct((4, vw), f32),
             jax.ShapeDtypeStruct((1, 2 * heads), f32),
+            jax.ShapeDtypeStruct((width, right_one.shape[1]), bf16),
+            jax.ShapeDtypeStruct((width // 2, right_two.shape[1]), bf16),
+            jax.ShapeDtypeStruct((rows, right_three.shape[1]), bf16),
         ],
-        compiler_params=pltpu.CompilerParams(vmem_limit_bytes=48 * 1024 * 1024),
-        cost_estimate=pl.CostEstimate(flops=22_000_000_000, bytes_accessed=28_000_000, transcendentals=6_000_000),
+        compiler_params=pltpu.CompilerParams(vmem_limit_bytes=56 * 1024 * 1024),
+        cost_estimate=LITTLE,
         name="mixer_backward",
-    )(scal, pq, pk, pv, pq, pk, pv, small, do, delta, s, tt, cq, ck, cv, dlog, dbias)
+    )(
+        scal, pq, pk, pv, pq, pk, pv, small, do, delta, s, tt, cq, ck, cv, dlog, dbias,
+        left_one, right_one, left_two, right_two, left_three, right_three,
+    )
 
 
 def product_tn(left, right):
@@ -566,7 +585,9 @@
         to_beside, to_across, _ = self.copies()
         to_across.start()
         to_beside.start()
-        to_beside.wait_recv()
+
+    def near(self):
+        self.copies()[0].wait_recv()
 
     def second(self):
         _, to_across, forward = self.copies()
@@ -583,7 +604,11 @@
             copy.wait()
 
     def at(self, step, steps):
-        pl.when(step == 0)(self.begin)
+        @pl.when(step == 0)
+        def _():
+            self.begin()
+            self.near()
+
         pl.when(step == steps // 2)(self.second)
 
     def rows(self, half):
@@ -591,28 +616,37 @@
         return self.held[pl.ds(pl.multiple_of(half * count, count), count), :]
 
 
-def gather_call(kernel, name, collective, steps, own, operands, in_specs, out_specs, out_shape, flops, nbytes, kind, more=()):
+def column_groups(width):
+    groups = lax.axis_size("dp")
+    return 1 if (width // groups) % 128 else groups
+
+
+def gather_call(kernel, name, collective, own, operands, in_specs, out_specs, out_shape, cost, kind, more=(), grid=None):
     rows, width = own.shape
-    groups = lax.axis_size("dp")
-    if (width // groups) % 128:
-        groups = 1
+    groups = column_groups(width)
+    count, made = len(operands), len(out_shape)
 
     def body(own_ref, *refs):
-        count = len(operands)
-        outs = refs[count : count + len(out_shape)]
-        whole, held, send_sem, recv_sem, out_sem = refs[count + len(out_shape) :][:5]
+        outs = refs[count : count + made]
+        whole, held, send_sem, recv_sem, out_sem = refs[count + made : count + made + 5]
         gather = Gather(own_ref, held, whole, send_sem, recv_sem, out_sem, groups, kind)
-        outs = outs + refs[count + len(out_shape) + 5 :]
+        rest = refs[count + made + 5 :]
+        if grid is None:
+            kernel(gather, *refs[:count], *outs, *rest)
+            return
         step = pl.program_id(0)
-        gather.at(step, steps)
-        kernel(step, gather, *refs[:count], *outs)
-        pl.when(step == steps - 1)(gather.end)
-
+        gather.at(step, grid)
+        kernel(step, gather, *refs[:count], *outs, *rest)
+        pl.when(step == grid - 1)(gather.end)
+
+    own_spec = pl.BlockSpec(memory_space=pltpu.VMEM)
+    if grid is not None:
+        own_spec = pl.BlockSpec((rows, width), lambda j: (0, 0))
     outs = pl.pallas_call(
         body,
         name=name,
-        grid=(steps,),
-        in_specs=[pl.BlockSpec((rows, width), lambda j: (0, 0))] + in_specs,
+        grid=() if grid is None else (grid,),
+        in_specs=[own_spec] + in_specs,
         out_specs=out_specs + [pl.BlockSpec(memory_space=pl.ANY)],
         out_shape=out_shape + [jax.ShapeDtypeStruct((4 * rows, width), own.dtype)],
         scratch_shapes=[
@@ -625,105 +659,163 @@
         compiler_params=pltpu.CompilerParams(
             vmem_limit_bytes=VMEM_MOST, collective_id=collective, has_side_effects=True
         ),
-        cost_estimate=pl.CostEstimate(flops=flops, bytes_accessed=nbytes, transcendentals=0),
+        cost_estimate=LITTLE,
     )(own, *operands)
-    if groups == 1:
+    if kind is not None and groups == 1:
         outs = list(outs[:-1]) + [take_columns(outs[-1], kind)]
     return outs
 
 
-def project_kernel(step, gather, wq, wk, wv, wg, ws, pq, pk, pv, pg, small):
-    steps = [(wq, pq), (wk, pk), (wv, pv), (wv, pv), (wg, pg), (wg, pg)]
-    half = step // 6
-
-    def run(weight, out):
-        out[...] = mm(gather.rows(half), weight[...]).astype(bf16)
-
-    for at, (weight, out) in enumerate(steps):
-        pl.when(step % 6 == at)(lambda weight=weight, out=out: run(weight, out))
-
-    @pl.when(step % 6 == 0)
-    def _():
-        small[...] = mm(gather.rows(half), ws[...])
+def project_kernel(gather, wq, wk, wv, wg, ws, pq, pk, pv, pg, small, held_w, stage, w_sem, o_sem):
+    pair = 2 * gather.own.shape[0]
+    pieces = []
+    for weight, out in ((wq, pq), (wk, pk), (wv, pv), (wg, pg)):
+        for start in range(0, weight.shape[1], COLUMNS):
+            pieces.append((weight, out, start))
+
+    def block(at):
+        return pl.ds(at * COLUMNS, COLUMNS)
+
+    def load(at):
+        weight, _, start = pieces[at]
+        return pltpu.make_async_copy(
+            weight.at[:, pl.ds(start, COLUMNS)], held_w.at[:, block(at)], w_sem.at[at]
+        )
+
+    def store(half, at):
+        _, out, start = pieces[at]
+        rows = pl.ds(half * pair, pair)
+        return pltpu.make_async_copy(
+            stage.at[rows, block(at)], out.at[rows, pl.ds(start, COLUMNS)], o_sem.at[half * len(pieces) + at]
+        )
+
+    load(0).start()
+    gather.begin()
+    for at in range(1, len(pieces)):
+        load(at).start()
+    gather.near()
+    for half in range(2):
+        if half:
+            gather.second()
+        rows = pl.ds(half * pair, pair)
+        for at in range(len(pieces)):
+            if half == 0:
+                load(at).wait()
+            stage[rows, block(at)] = mm(gather.held[rows, :], held_w[:, block(at)]).astype(bf16)
+            store(half, at).start()
+        small[rows, :] = mm_nt(gather.held[rows, :], ws[...])
+    for half in range(2):
+        for at in range(len(pieces)):
+            store(half, at).wait()
+    gather.end()
 
 
 def project(own, weights):
     rows, width = own.shape
-    pair = 2 * rows
-    n_small = weights[4].shape[1]
-    places = [
-        lambda j: 0,
-        lambda j: 0,
-        lambda j: jnp.clip(j % 6 - 2, 0, 1),
-        lambda j: jnp.clip(j % 6 - 4, 0, 1),
-    ]
-    in_specs = [pl.BlockSpec((width, COLUMNS), lambda j, place=place: (0, place(j))) for place in places]
-    in_specs.append(pl.BlockSpec((width, n_small), lambda j: (0, 0)))
-    out_specs = [pl.BlockSpec((pair, COLUMNS), lambda j, place=place: (j // 6, place(j))) for place in places]
-    out_specs.append(pl.BlockSpec((pair, n_small), lambda j: (j // 6, 0)))
-    out_shape = [jax.ShapeDtypeStruct((2 * pair, weight.shape[1]), bf16) for weight in weights[:4]]
-    out_shape.append(jax.ShapeDtypeStruct((2 * pair, n_small), f32))
+    total = sum(weight.shape[1] for weight in weights[:4])
+    blocks = total // COLUMNS
+    hbm, vmem = pl.BlockSpec(memory_space=pl.ANY), pl.BlockSpec(memory_space=pltpu.VMEM)
+    out_shape = [jax.ShapeDtypeStruct((4 * rows, weight.shape[1]), bf16) for weight in weights[:4]]
+    out_shape.append(jax.ShapeDtypeStruct((4 * rows, weights[4].shape[0]), f32))
     return gather_call(
-        project_kernel, "project", 0, 12, own, weights, in_specs, out_specs, out_shape,
-        40_000_000_000, 40_000_000, "flip",
-    )
-
-
-def feed_kernel(blocks, step, gather, e, wg, wu, wd, hidden, d_gate, d_up, e_split, e_sem):
-    groups = e_sem.shape[0]
-    half = step // blocks
-    count = e.shape[0] // 2
-
-    def copies():
-        if groups == 1:
-            return [pltpu.make_async_copy(e, e_split, e_sem.at[0])]
-        return column_copies("split", groups, e, e_split, e_sem)
-
-    @pl.when(step == 0)
-    def _():
-        for copy in copies():
-            copy.start()
-
-    x = gather.rows(half)
-    gate = mm_nt(x, wg[...])
-    up = mm_nt(x, wu[...])
-    back = mm_nt(e[pl.ds(pl.multiple_of(half * count, count), count), :], wd[...])
-    sig = sigmoid(gate)
-    act = gate * sig
-    hidden[...] = (act * up).astype(bf16)
-    d_gate[...] = (back * up * (sig + act * (1.0 - sig))).astype(bf16)
-    d_up[...] = (back * act).astype(bf16)
-
-    @pl.when(step == 2 * blocks - 1)
-    def _():
-        for copy in copies():
-            copy.wait()
-
-
-def feed(own, e, wg, wu, wd):
+        project_kernel, "project", 0, own, weights, [hbm] * 4 + [vmem], [hbm] * 4 + [vmem], out_shape,
+        (40_000_000_000, 40_000_000), "flip",
+        [
+            pltpu.VMEM((width, total), bf16),
+            pltpu.VMEM((4 * rows, total), bf16),
+            pltpu.SemaphoreType.DMA((blocks,)),
+            pltpu.SemaphoreType.DMA((2 * blocks,)),
+        ],
+    )
+
+
+def feed_kernel(
+    gather, e0, e1, e2, e3, wg, wu, wd, hidden, d_gate, d_up, e_out,
+    e, held_g, held_u, held_d, stage, e_sem, w_sem, o_sem,
+):
+    count = gather.own.shape[0]
+    pair = 2 * count
+    units = wg.shape[0]
+    blocks = [(start, min(COLUMNS, units - start)) for start in range(0, units, COLUMNS)]
+    outs = (hidden, d_gate, d_up)
+
+    def load_rows(at):
+        return pltpu.make_async_copy((e0, e1, e2, e3)[at], e.at[pl.ds(at * count, count)], e_sem.at[at])
+
+    def save_rows():
+        return pltpu.make_async_copy(e, e_out, e_sem.at[4])
+
+    def load(at, which):
+        where = pl.ds(*blocks[at])
+        return pltpu.make_async_copy(
+            (wg, wu, wd)[which].at[where], (held_g, held_u, held_d)[which].at[where], w_sem.at[3 * at + which]
+        )
+
+    def store(half, which):
+        rows = pl.ds(half * pair, pair)
+        return pltpu.make_async_copy(stage.at[which, rows], outs[which].at[rows], o_sem.at[3 * half + which])
+
+    load(0, 0).start()
+    gather.begin()
+    for at in range(len(blocks)):
+        for which in range(3):
+            if at or which:
+                load(at, which).start()
+        if at == 0:
+            for part in range(4):
+                load_rows(part).start()
+    gather.near()
+    for part in range(4):
+        load_rows(part).wait()
+    save_rows().start()
+    for half in range(2):
+        if half:
+            gather.second()
+        rows = pl.ds(half * pair, pair)
+        for at, (start, size) in enumerate(blocks):
+            where = pl.ds(start, size)
+            if half == 0:
+                for which in range(3):
+                    load(at, which).wait()
+            gate = mm_nt(gather.held[rows, :], held_g[where, :])
+            up = mm_nt(gather.held[rows, :], held_u[where, :])
+            back = mm_nt(e[rows, :], held_d[where, :])
+            sig = sigmoid(gate)
+            act = gate * sig
+            stage[0, rows, where] = (act * up).astype(bf16)
+            stage[1, rows, where] = (back * up * (sig + act * (1.0 - sig))).astype(bf16)
+            stage[2, rows, where] = (back * act).astype(bf16)
+        for which in range(3):
+            store(half, which).start()
+    for half in range(2):
+        for which in range(3):
+            store(half, which).wait()
+    save_rows().wait()
+    gather.end()
+
+
+def feed(own, e_blocks, wg, wu, wd):
     rows, width = own.shape
-    pair = 2 * rows
     units = wd.shape[0]
     blocks = pl.cdiv(units, COLUMNS)
-    groups = lax.axis_size("dp")
-    if (width // groups) % 128:
-        groups = 1
-    by_rows = pl.BlockSpec((COLUMNS, width), lambda j: (j % blocks, 0))
-    outs = gather_call(
-        lambda *refs: feed_kernel(blocks, *refs), "feed", 1, 2 * blocks, own, [e, wg, wu, wd],
-        [pl.BlockSpec((2 * pair, width), lambda j: (0, 0)), by_rows, by_rows, by_rows],
-        [pl.BlockSpec((pair, COLUMNS), lambda j: (j // blocks, j % blocks))] * 3
-        + [pl.BlockSpec(memory_space=pl.ANY)],
-        [jax.ShapeDtypeStruct((2 * pair, units), bf16)] * 3
-        + [jax.ShapeDtypeStruct((2 * pair, width), bf16)],
-        40_000_000_000, 40_000_000, "split", [pltpu.SemaphoreType.DMA((groups,))],
-    )
-    if groups == 1:
-        outs[3] = take_columns(outs[3], "split")
-    return outs
-
-
-def gate_back_kernel(heads, step, gather, length, w, pg, o_in, gain, dpg, do, dgain):
+    hbm = pl.BlockSpec(memory_space=pl.ANY)
+    return gather_call(
+        feed_kernel, "feed", 1, own, list(e_blocks) + [wg, wu, wd], [hbm] * 7, [hbm] * 4,
+        [jax.ShapeDtypeStruct((4 * rows, units), bf16)] * 3
+        + [jax.ShapeDtypeStruct((4 * rows, width), bf16)],
+        (40_000_000_000, 40_000_000), "split",
+        [pltpu.VMEM((4 * rows, width), bf16)]
+        + [pltpu.VMEM((units, width), bf16)] * 3
+        + [
+            pltpu.VMEM((3, 4 * rows, units), bf16),
+            pltpu.SemaphoreType.DMA((5,)),
+            pltpu.SemaphoreType.DMA((3 * blocks,)),
+            pltpu.SemaphoreType.DMA((6,)),
+        ],
+    )
+
+
+def gate_back_kernel(heads, step, gather, length, w, pg, o_in, gain, left, right, dpg, do, dgain, leave):
     pair = 2 * gather.own.shape[0]
     each = pair // 2
     dv = gain.shape[1]
@@ -752,34 +844,52 @@
         dn = dg * gain[...] * act
         do[:, where] = (inv * (dn - norm * jnp.mean(dn * norm, axis=-1, keepdims=True))).astype(bf16)
 
-
-def gate_back(own, length, w_out, pg, o, gain):
+    @pl.when(step == 1)
+    def _():
+        units = leave.shape[0]
+        for start in range(0, units, COLUMNS):
+            where = slice(start, min(start + COLUMNS, units))
+            leave[where, :] = mm_tn(left[:, where], right[...]).astype(bf16)
+
+
+def gate_back(own, length, w_out, pg, o, gain, left, right):
     rows, width = own.shape
     pair = 2 * rows
     dv = gain.shape[1]
     heads = w_out.shape[0] // dv // 2
     by_head = pl.BlockSpec((pair, heads * dv), lambda j: (j // 2, j % 2))
     return gather_call(
-        lambda *refs: gate_back_kernel(heads, *refs), "gate_back", 2, 4, own, [length, w_out, pg, o, gain],
+        lambda *refs: gate_back_kernel(heads, *refs), "gate_back", 2, own, [length, w_out, pg, o, gain, left, right],
         [
             pl.BlockSpec(memory_space=pltpu.SMEM),
             pl.BlockSpec((heads * dv, width), lambda j: (j % 2, 0)),
             by_head, by_head,
             pl.BlockSpec((1, dv), lambda j: (0, 0)),
+            pl.BlockSpec(left.shape, lambda j: (0, 0)),
+            pl.BlockSpec((right.shape[0], right.shape[1] // 2), lambda j: (0, 1)),
         ],
-        [by_head, by_head, pl.BlockSpec((1, dv), lambda j: (0, 0))],
+        [
+            by_head, by_head,
+            pl.BlockSpec((1, dv), lambda j: (0, 0)),
+            pl.BlockSpec((left.shape[1], right.shape[1] // 2), lambda j: (0, 0)),
+        ],
         [
             jax.ShapeDtypeStruct(pg.shape, bf16),
             jax.ShapeDtypeStruct(pg.shape, bf16),
             jax.ShapeDtypeStruct((1, dv), f32),
+            jax.ShapeDtypeStruct((left.shape[1], right.shape[1] // 2), bf16),
         ],
-        30_000_000_000, 30_000_000, "flip",
-    )
-
-
-def scatter_kernel(turned, count, *refs):
-    lefts, rights, out = refs[:count], refs[count : 2 * count], refs[2 * count]
-    far_own, leave, other, send_sem, recv_sem = refs[2 * count + 1 :]
+        (30_000_000_000, 30_000_000), "flip", grid=4,
+    )
+
+
+def scatter_kernel(turned, count, filled, *refs):
+    lefts, rights, refs = refs[:count], refs[count : 2 * count], refs[2 * count :]
+    if filled:
+        (fill_left, fill_right, out, fill), refs = refs[:4], refs[4:]
+    else:
+        out, refs = refs[0], refs[1:]
+    far_own, leave, other, send_sem, recv_sem = refs
     step = pl.program_id(0)
     parts = pl.num_programs(0) // 2
     rows = out.shape[0]
@@ -846,6 +956,11 @@
 
     @pl.when(step == 2 * parts - 1)
     def _():
+        if filled:
+            for start in range(0, fill.shape[0], COLUMNS):
+                where = slice(start, start + COLUMNS)
+                fill[where, :] = mm_tn(fill_left[:, where], fill_right[...]).astype(bf16)
+
         def finish(part, carry):
             copy(NEAR, part).wait_recv()
             copy(ACROSS, part).wait_recv()
@@ -860,7 +975,7 @@
         lax.fori_loop(0, parts, finish, 0)
 
 
-def scatter_products(lefts, rights, turned, collective):
+def scatter_products(lefts, rights, turned, collective, fill=None):
     lefts = [left if isinstance(left, tuple) else (left, 0, left.shape[1]) for left in lefts]
     rows = lefts[0][0].shape[0] // 4
     width = rights[0].shape[0 if turned else 1]
@@ -876,13 +991,21 @@
             return pl.BlockSpec((COLUMNS, right.shape[1]), lambda j: (j % parts, 0))
         return pl.BlockSpec((right.shape[0], COLUMNS), lambda j: (0, j % parts))
 
-    return pl.pallas_call(
-        lambda *refs: scatter_kernel(turned, len(lefts), *refs),
+    in_specs = [left_spec(block, size) for _, block, size in lefts] + [right_spec(right) for right in rights]
+    out_specs = [pl.BlockSpec((rows, width), lambda j: (0, 0))]
+    out_shape = [jax.ShapeDtypeStruct((rows, width), f32)]
+    if fill is not None:
+        made = (fill[0].shape[1], fill[1].shape[1])
+        in_specs += [pl.BlockSpec(part.shape, lambda j: (0, 0)) for part in fill]
+        out_specs.append(pl.BlockSpec(made, lambda j: (0, 0)))
+        out_shape.append(jax.ShapeDtypeStruct(made, bf16))
+    outs = pl.pallas_call(
+        lambda *refs: scatter_kernel(turned, len(lefts), fill is not None, *refs),
         name="scatter_products",
         grid=(2 * parts,),
-        in_specs=[left_spec(block, size) for _, block, size in lefts] + [right_spec(right) for right in rights],
-        out_specs=pl.BlockSpec((rows, width), lambda j: (0, 0)),
-        out_shape=jax.ShapeDtypeStruct((rows, width), f32),
+        in_specs=in_specs,
+        out_specs=out_specs,
+        out_shape=out_shape,
         scratch_shapes=[
             pltpu.VMEM((rows, width), f32),
             pltpu.VMEM((3, rows, width), bf16),
@@ -893,8 +1016,39 @@
         compiler_params=pltpu.CompilerParams(
             vmem_limit_bytes=VMEM_MOST, collective_id=collective, has_side_effects=True
         ),
-        cost_estimate=pl.CostEstimate(flops=2 * flops, bytes_accessed=4 * total * width, transcendentals=0),
-    )(*[left[0] for left in lefts], *rights)
+        cost_estimate=LITTLE,
+    )(*[left[0] for left in lefts], *rights, *(fill or ()))
+    return outs[0] if fill is None else outs
+
+
+def turned_kernel(added, left, right, *refs):
+    total = mm_tn(left[...], right[...])
+    if added:
+        total = total + refs[0][...].astype(f32)
+    refs[-1][...] = total.astype(bf16)
+
+
+def turned_product(left, right, left_half=None, right_half=None, other=None):
+    rows = left.shape[0]
+    count = left.shape[1] if left_half is None else left.shape[1] // 2
+    width = right.shape[1] if right_half is None else right.shape[1] // 2
+    skip = (left_half or 0) * (count // COLUMNS)
+    out = pl.BlockSpec((COLUMNS, width), lambda j: (j, 0))
+    more = [] if other is None else [other]
+    return pl.pallas_call(
+        lambda *refs: turned_kernel(len(more), *refs),
+        name="turned_product",
+        grid=(pl.cdiv(count, COLUMNS),),
+        in_specs=[
+            pl.BlockSpec((rows, COLUMNS), lambda j: (0, skip + j)),
+            pl.BlockSpec((rows, width), lambda j: (0, right_half or 0)),
+        ]
+        + [out] * len(more),
+        out_specs=out,
+        out_shape=jax.ShapeDtypeStruct((count, width), bf16),
+        compiler_params=pltpu.CompilerParams(vmem_limit_bytes=VMEM_MOST),
+        cost_estimate=LITTLE,
+    )(left, right, *more)
 
 
 def low_bit(chunk, groups):
@@ -909,46 +1063,68 @@
     for at, tensor in enumerate(late):
         for position, chunk in enumerate(chunks):
             level = low_bit(chunk, groups).bit_length() - 2
-            lag = 2.5 * level / levels if chunk == 0 else 0.5 * level
+            lag = LAST * level / levels if chunk == 0 else NEXT * level
             plan.append((at * len(chunks) + position + lag, tensor, chunk))
     for at, tensor in enumerate(early):
         for position, chunk in enumerate(chunks):
             level = low_bit(chunk, groups).bit_length() - 2
-            plan.append((2 * at - 1 + 2 * level + 0.01 * position, tensor, chunk))
+            plan.append((EARLY[0] * at - 1 + EARLY[1] * level + 0.01 * position, tensor, chunk))
     return [step[1:] for step in sorted(plan)], chunks
 
 
-def reduce_kernel(groups, count, *refs):
+PARTS = 2
+AHEAD = 4
+EARLY = (2, 6)
+LAST, NEXT = 2.5, 0.5
+
+
+def reduce_kernel(groups, early, shapes, *refs):
+    count = len(shapes)
+    late = list(range(len(early), count))
     leaves, refs = refs[:count], refs[count:]
-    small, gains, partial, resid, refs = refs[0], refs[1], refs[2], refs[3], refs[4:]
-    outs, refs = refs[:count], refs[count:]
-    small_out, gains_out, mixed, refs = refs[0], refs[1], refs[2], refs[3:]
+    (taps_q, taps_k, taps_v, decay, thin, gain_one, gain_two, gain_head, partial_in, resid), refs = (
+        refs[:10], refs[10:],
+    )
+    outs = []
+    for shape in shapes:
+        outs.append(refs[: len(shape)])
+        refs = refs[len(shape) :]
+    (out_q, out_k, out_v, out_decay, out_thin, out_one, out_two, out_head, mixed), refs = refs[:9], refs[9:]
     lands, refs = refs[:count], refs[count:]
     sends, refs = refs[:count], refs[count:]
     keeps, refs = refs[:count], refs[count:]
-    small_land, gains_land, gains_first, rows_leave, rows_land = refs[:5]
-    send_sem, recv_sem, sum_send, sum_recv, rows_send, rows_recv, keep_sem = refs[5:]
+    small_land, gains_land, gains_first, rows_leave, rows_land, partial = refs[:6]
+    send_sem, recv_sem, sum_send, sum_recv, rows_send, rows_recv, keep_sem, load_sem = refs[6:]
     place = lax.axis_index("dp")
     beside = lax.axis_index("tensor")
     order = group_order(groups)
     position = {chunk: at for at, chunk in enumerate(order)}
     bits = [1 << at for at in range(groups.bit_length() - 1)]
-    each = outs[0].shape[0]
+    each = sends[0].shape[0] // (groups // 2 - 1)
     across_core = {"tensor": flipped(beside, 1, 4)}
     across_chip = {"tensor": flipped(beside, 2, 4)}
 
-    def rows(at):
-        return pl.ds(at * each, each)
-
-    def copy(tensor, chunk):
-        source = (
-            leaves[tensor].at[rows(position[chunk])] if chunk % 2 else sends[tensor].at[rows(chunk // 2 - 1)]
-        )
+    size = each // PARTS
+
+    def rows(at, part):
+        return pl.ds(at * each + part * size, size)
+
+    def slot(unit, chunk):
+        tensor, part = unit
+        return rows(chunk // 2 - 1 if tensor in early else chunk - 1, part)
+
+    def copy(unit, chunk):
+        tensor, part = unit
+        if chunk % 2:
+            source = leaves[tensor].at[rows(position[chunk], part)]
+        else:
+            source = sends[tensor].at[rows(chunk // 2 - 1, part)]
+        at = (tensor * PARTS + part) * groups + chunk
         return pltpu.make_async_remote_copy(
             src_ref=source,
-            dst_ref=lands[tensor].at[rows(chunk - 1)],
-            send_sem=send_sem.at[tensor * groups + chunk],
-            recv_sem=recv_sem.at[tensor * groups + chunk],
+            dst_ref=lands[tensor].at[slot(unit, chunk)],
+            send_sem=send_sem.at[at],
+            recv_sem=recv_sem.at[at],
             device_id={"dp": flipped(place, low_bit(chunk, groups), groups)},
             device_id_type=MESH,
         )
@@ -967,8 +1143,10 @@
         pl.semaphore_signal(barrier, inc=1, device_id=partner, device_id_type=MESH)
     pl.semaphore_wait(barrier, len(partners))
 
-    plan, chunks = reduce_plan(groups, [], list(range(count)))
-    pieces = [(tensor, chunk + 1) for tensor in range(count) for chunk in chunks]
+    early_units = [(tensor, part) for tensor in early for part in range(PARTS)]
+    late_units = [(tensor, part) for tensor in late for part in range(PARTS)]
+    plan, chunks = reduce_plan(groups, early_units, late_units)
+    pieces = [(unit, chunk + 1) for unit in late_units for chunk in chunks]
     started = []
 
     def send_piece():
@@ -976,7 +1154,7 @@
             copy(*pieces[len(started)]).start()
             started.append(1)
 
-    for _ in range(3):
+    for _ in range(AHEAD):
         send_piece()
 
     def plain_copy(source, land, sems, at, partner):
@@ -991,11 +1169,23 @@
     corner = plain_copy(partial.at[blocks[3]], rows_land.at[0], row_sems, 0, across_core)
     near = plain_copy(partial.at[blocks[1]], rows_land.at[1], row_sems, 1, across_core)
     far = plain_copy(rows_leave, rows_land.at[2], row_sems, 2, across_chip)
-    corner.start()
-    near.start()
-
-    gains_first[0] = gains[...]
-    small_land[0] = small[...]
+    load = pltpu.make_async_copy(partial_in, partial, load_sem.at[0])
+    load.start()
+
+    kw, line = taps_q.shape[1], taps_v.shape[1]
+    lines = gain_one.shape[1] // line
+    gains_first[0] = jnp.zeros(gains_first.shape[1:], f32)
+    small_land[0] = jnp.zeros(small_land.shape[1:], f32)
+    small_land[0, 0:4, :] = taps_v[...]
+    small_land[0, 4:8, :kw] = taps_q[...]
+    small_land[0, 4:8, kw:] = taps_k[...]
+    for at in range(lines):
+        where = slice(at * line, (at + 1) * line)
+        small_land[0, 8 + 8 * at : 16 + 8 * at, :] = thin[:, where]
+        gains_first[0, at : at + 1, :] = gain_one[:, where]
+        gains_first[0, lines + at : lines + at + 1, :] = gain_two[:, where]
+    small_land[0, 8 + 8 * lines : 9 + 8 * lines, : decay.shape[1]] = decay[...]
+    gains_first[0, 2 * lines : 2 * lines + 1, : gain_head.shape[1]] = gain_head[...]
     sum_sems = (sum_send, sum_recv)
     hops = [across_core, across_chip] + [{"dp": flipped(place, bit, groups)} for bit in bits]
     gains_copies = [
@@ -1019,7 +1209,11 @@
                 gains_first[at + 1] = total
                 gains_copies[at + 1].start()
             else:
-                gains_out[...] = total
+                for row in range(lines):
+                    where = slice(row * line, (row + 1) * line)
+                    out_one[:, where] = total[row : row + 1, :]
+                    out_two[:, where] = total[lines + row : lines + row + 1, :]
+                out_head[...] = total[2 * lines : 2 * lines + 1, : gain_head.shape[1]]
             done["gains"] += 1
         at = done["small"]
         if at < len(small_copies):
@@ -1029,11 +1223,30 @@
                 small_land[2 * at + 2] = total
                 small_copies[at + 1].start()
             else:
-                small_out[...] = total
+                out_v[...] = total[0:4]
+                out_q[...] = total[4:8, :kw]
+                out_k[...] = total[4:8, kw:]
+                for row in range(lines):
+                    out_thin[:, row * line : (row + 1) * line] = total[8 + 8 * row : 16 + 8 * row]
+                out_decay[...] = total[8 + 8 * lines : 9 + 8 * lines, : decay.shape[1]]
             done["small"] += 1
 
-    for index, (tensor, chunk) in enumerate(plan):
-        if index == 1:
+    def finish(tensor, part, total):
+        where = slice(part * size, (part + 1) * size)
+        for out, (start, count, turned) in zip(outs[tensor], shapes[tensor]):
+            piece = total[:, start : start + count]
+            if turned:
+                out[:, where] = jnp.transpose(piece)
+            else:
+                out[where, :] = piece
+
+    for index, (unit, chunk) in enumerate(plan):
+        tensor, part = unit
+        if index == 8:
+            load.wait()
+            corner.start()
+            near.start()
+        if index == 8:
             corner.wait_recv()
             rows_leave[...] = (
                 partial[blocks[2], :].astype(f32) + rows_land[0].astype(f32)
@@ -1042,22 +1255,24 @@
         if tensor not in kept:
             keep_copy(tensor).wait()
             kept.add(tensor)
-        total = keeps[tensor][rows(position[chunk]), :].astype(f32)
+        total = keeps[tensor][rows(position[chunk], part), :].astype(f32)
         for bit in bits:
             if bit >= low_bit(chunk, groups):
                 break
-            copy(tensor, chunk + bit).wait_recv()
+            if bit == 1 and tensor in early:
+                continue
+            copy(unit, chunk + bit).wait_recv()
             if bit == 1:
                 send_piece()
-            total = total + lands[tensor][rows(chunk + bit - 1), :].astype(f32)
+            total = total + lands[tensor][slot(unit, chunk + bit), :].astype(f32)
         if chunk:
-            sends[tensor][rows(chunk // 2 - 1), :] = total.astype(bf16)
-            copy(tensor, chunk).start()
+            sends[tensor][rows(chunk // 2 - 1, part), :] = total.astype(bf16)
+            copy(unit, chunk).start()
         else:
-            outs[tensor][...] = total
-        if index >= 2 and index % 2 == 0:
+            finish(tensor, part, total)
+        if index >= 4 and index % 4 == 0:
             next_sum()
-        if index == 6:
+        if index == 20:
             near.wait_recv()
             far.wait_recv()
             mixed[...] = (
@@ -1068,52 +1283,64 @@
             ).astype(bf16)
     while done["gains"] < len(gains_copies):
         next_sum()
-    for tensor in range(count):
+    for unit in early_units + late_units:
         for chunk in range(1, groups):
-            copy(tensor, chunk).wait_send()
+            if chunk % 2 == 0 or unit[0] in late:
+                copy(unit, chunk).wait_send()
     for sent in gains_copies + small_copies + [corner, near, far]:
         sent.wait_send()
 
 
-def reduce_groups(grads, small, gains, partial, resid, collective):
-    count = len(grads)
+def reduce_groups(early_grads, late_grads, shapes, small, partial, resid, collective):
+    grads = list(early_grads) + list(late_grads)
+    early = list(range(len(early_grads)))
     groups = lax.axis_size("dp")
     bits = groups.bit_length() - 1
-    each = grads[0].shape[0] // groups
+    each = late_grads[0].shape[0] // groups
     rows, width = resid.shape
     widths = [grad.shape[1] for grad in grads]
     vmem = pl.BlockSpec(memory_space=pltpu.VMEM)
-    out_shape = [jax.ShapeDtypeStruct((each, size), f32) for size in widths]
-    out_shape += [jax.ShapeDtypeStruct(small.shape, f32), jax.ShapeDtypeStruct(gains.shape, f32)]
+    out_shape = []
+    for shape in shapes:
+        for _, size, turned in shape:
+            out_shape.append(jax.ShapeDtypeStruct((size, each) if turned else (each, size), f32))
+    out_shape += [jax.ShapeDtypeStruct(part.shape, f32) for part in small]
     out_shape += [jax.ShapeDtypeStruct((rows, width), bf16)]
+    line = small[2].shape[1]
+    lines = width // line
+    small_shape, gains_shape = (16 + 8 * lines, line), (8 * pl.cdiv(2 * lines + 1, 8), line)
+    landed = [(groups // 2 if at in early else groups) - 1 for at in range(len(grads))]
     return pl.pallas_call(
-        lambda *refs: reduce_kernel(groups, count, *refs),
+        lambda *refs: reduce_kernel(groups, early, shapes, *refs),
         name="reduce_groups",
-        in_specs=[pl.BlockSpec(memory_space=pl.ANY)] * count + [vmem] * 4,
+        in_specs=[pl.BlockSpec(memory_space=pl.ANY)] * len(grads) + [vmem] * len(small)
+        + [pl.BlockSpec(memory_space=pl.ANY), vmem],
         out_specs=[vmem] * len(out_shape),
         out_shape=out_shape,
-        scratch_shapes=[pltpu.VMEM(((groups - 1) * each, size), bf16) for size in widths]
+        scratch_shapes=[pltpu.VMEM((chunks * each, size), bf16) for chunks, size in zip(landed, widths)]
         + [pltpu.VMEM(((groups // 2 - 1) * each, size), bf16) for size in widths]
         + [pltpu.VMEM((groups // 2 * each, size), bf16) for size in widths]
         + [
-            pltpu.VMEM((2 * bits,) + small.shape, f32),
-            pltpu.VMEM((bits + 2,) + gains.shape, f32),
-            pltpu.VMEM((bits + 2,) + gains.shape, f32),
+            pltpu.VMEM((2 * bits,) + small_shape, f32),
+            pltpu.VMEM((bits + 2,) + gains_shape, f32),
+            pltpu.VMEM((bits + 2,) + gains_shape, f32),
             pltpu.VMEM((rows, width), bf16),
             pltpu.VMEM((3, rows, width), bf16),
-            pltpu.SemaphoreType.DMA((count * groups,)),
-            pltpu.SemaphoreType.DMA((count * groups,)),
+            pltpu.VMEM((4 * rows, width), bf16),
+            pltpu.SemaphoreType.DMA((len(grads) * PARTS * groups,)),
+            pltpu.SemaphoreType.DMA((len(grads) * PARTS * groups,)),
             pltpu.SemaphoreType.DMA((2 * bits + 2,)),
             pltpu.SemaphoreType.DMA((2 * bits + 2,)),
             pltpu.SemaphoreType.DMA((3,)),
             pltpu.SemaphoreType.DMA((3,)),
-            pltpu.SemaphoreType.DMA((count,)),
+            pltpu.SemaphoreType.DMA((len(grads),)),
+            pltpu.SemaphoreType.DMA((1,)),
         ],
         compiler_params=pltpu.CompilerParams(
             vmem_limit_bytes=VMEM_MOST, collective_id=collective, has_side_effects=True
         ),
-        cost_estimate=pl.CostEstimate(flops=100_000_000_000, bytes_accessed=300_000_000, transcendentals=0),
-    )(*grads, small, gains, partial, resid)
+        cost_estimate=LITTLE,
+    )(*grads, *small, partial, resid)
 
 
 def product_nn(left, right):
@@ -1140,35 +1367,12 @@
     return jnp.take(array.reshape(array.shape[0], groups, -1), found, axis=1)
 
 
-def leaving(left, right):
-    quarter = right.shape[1] // 4
-    return [
-        product_tn(left, right[:, at * quarter : (at + 1) * quarter]).astype(jnp.bfloat16) for at in (2, 3)
-    ]
-
-
-def settle(left, right, others):
-    half = right.shape[1] // 2
-    other = jnp.concatenate(others, axis=1).astype(jnp.float32)
-    total = (product_tn(left, right[:, :half]) + other).astype(jnp.bfloat16)
+def scatter_far(total):
     groups = lax.axis_size("dp")
     alike = [[place for place in range(groups) if place % 2 == bit] for bit in (0, 1)]
     return lax.psum_scatter(
         total, "dp", scatter_dimension=1, axis_index_groups=alike, tiled=True
     ).astype(jnp.float32)
-
-
-def pack(parts):
-    flat = jnp.concatenate([part.reshape(-1) for part in parts])
-    return jnp.pad(flat, (0, -flat.shape[0] % 1024)).reshape(-1, 1024)
-
-
-def unpack(flat, parts):
-    flat, at, out = flat.reshape(-1), 0, []
-    for part in parts:
-        out.append(flat[at : at + part.size].reshape(part.shape))
-        at += part.size
-    return out
 
 
 def per_device(
@@ -1205,7 +1409,7 @@
     place = lax.axis_index("tensor").astype(jnp.int32)
     scal = jnp.stack([seq_length[0], place])
     gain_row, log_row, bias_row = head_gain[None], decay_log[None], decay_bias[None]
-    w_small = jnp.concatenate([w_decay, w_beta], axis=1)
+    w_small = jnp.concatenate([w_decay.T, w_beta.T], axis=0)
     weights1 = (w_query, w_key, w_value, w_gate_out, w_small)
     p_query, p_key, p_value, p_gate, p_small, gathered1 = project(normed1, weights1)
     cotangent = tie(cotangent, p_small)
@@ -1216,68 +1420,80 @@
     )
     gated, e_across = together(gated, e_across)
     e_corner = flip(e_across, "tensor", 1)
-    cot_full = jnp.concatenate([cotangent, e_beside, e_across, e_corner], axis=0)
     resid = rows_in + scatter_products([gated], [w_out], False, 3)
     scaled2, inverse2 = row_stats(resid)
     normed2 = (scaled2 * norm2_gain).astype(jnp.bfloat16)
-    hidden, d_gate, d_up, cot_split, split2 = feed(normed2, cot_full, w_gate.T, w_up.T, w_down)
-    down_one, down_two = leaving(hidden, cot_split)
-    d_gate, d_up, down_one = together(d_gate, d_up, down_one)
-    down_one = flip(down_one, "dp", 1)
+    hidden, d_gate, d_up, cot_full, split2 = feed(
+        normed2, (cotangent, e_beside, e_across, e_corner), w_gate.T, w_up.T, w_down
+    )
+    grad_down = product_tn(hidden, cot_full).astype(jnp.bfloat16)
+    half = width // 2
+    up_other = product_tn(d_up, split2[:, half:]).astype(jnp.bfloat16)
+    d_gate, d_up, grad_down, up_other = together(d_gate, d_up, grad_down, up_other)
+    grad_down = lax.psum_scatter(grad_down, "dp", scatter_dimension=1, tiled=True).astype(jnp.float32)
+    up_other = flip(up_other, "dp", 1)
     d_normed2 = scatter_products([d_gate, d_up], [w_gate.T, w_up.T], False, 4)
-    d_normed2, down_one, d_gate, d_up = together(d_normed2, down_one, d_gate, d_up)
     d_resid_part, grad_norm2 = norm_back(scaled2, inverse2, norm2_gain, d_normed2)
     d_resid = (cotangent.astype(jnp.float32) + d_resid_part).astype(jnp.bfloat16)
-    d_resid, down_two = together(d_resid, down_two)
-    down_two = flip(down_two, "dp", 1)
-    dp_gate, do, dgain, resid_full = gate_back(d_resid, seq_length, w_out, p_gate, mixer_out, gain_row)
-    do, dp_gate, dgain, resid_full, down_two = together(do, dp_gate, dgain, resid_full, down_two)
-    grad_down = settle(hidden, cot_split, (down_one, down_two))
-    up_one, up_two = leaving(d_up, split2)
-    do, up_one, up_two = together(do, up_one, up_two)
-    up_one, up_two = flip(up_one, "dp", 1), flip(up_two, "dp", 1)
+    dp_gate, do, dgain, gate_other, resid_full = gate_back(
+        d_resid, seq_length, w_out, p_gate, mixer_out, gain_row, d_gate, split2
+    )
+    do, dp_gate, dgain, resid_full, gate_other, up_other = together(
+        do, dp_gate, dgain, resid_full, gate_other, up_other
+    )
+    gate_other = flip(gate_other, "dp", 1)
+    up_kept = turned_product(d_up, split2, right_half=0, other=up_other)
+    do, up_kept = together(do, up_kept)
+    grad_up = scatter_far(up_kept)
     mixer_grads = mixer_backward(
         scal, p_query, p_key, p_value, p_small, do, delta, states, inverse_t,
-        conv_query, conv_key, conv_value, log_row, bias_row,
-    )
-    dp_pair, dp_value, dp_small, dc_query, dc_key, dc_value, ddecay, up_one, up_two = together(
-        *mixer_grads, up_one, up_two
-    )
-    grad_up = settle(d_up, split2, (up_one, up_two))
-    gate_one, gate_two = leaving(d_gate, split2)
-    dp_small, gate_one, gate_two = together(dp_small, gate_one, gate_two)
-    gate_one, gate_two = flip(gate_one, "dp", 1), flip(gate_two, "dp", 1)
+        conv_query, conv_key, conv_value, log_row, bias_row, (gathered1, dp_gate), (resid_full, gated),
+        (hidden, w_down),
+    )
+    (
+        dp_pair, dp_value, dp_small, dc_query, dc_key, dc_value, ddecay, grad_gate_out, out_other, partial,
+        grad_down, gate_other,
+    ) = together(*mixer_grads, grad_down, gate_other)
+    out_other = flip(out_other, "dp", 1)
+    grad_gate = scatter_far(turned_product(d_gate, split2, right_half=0, other=gate_other))
+    grad_value = turned_product(gathered1, dp_value)
+    dp_value, grad_value = together(dp_value, grad_value)
     key_width = w_query.shape[1]
-    d_normed1 = scatter_products(
+    d_normed1, grad_pair = scatter_products(
         [(dp_pair, 0, key_width), (dp_pair, 1, key_width), dp_value, dp_gate, dp_small],
-        weights1, True, 5,
-    )
-    grad_out = product_tn(resid_full, gated).astype(jnp.bfloat16)
-    grad_gate_out = product_tn(gathered1, dp_gate).astype(jnp.bfloat16)
-    grad_value = product_tn(gathered1, dp_value).astype(jnp.bfloat16)
-    grad_pair = product_tn(gathered1, dp_pair).astype(jnp.bfloat16)
+        weights1[:4] + (w_small.T,), True, 5, (gathered1, dp_pair),
+    )
+    d_normed1, out_other = together(d_normed1, out_other)
+    out_keep = turned_product(resid_full, gated, left_half=0, other=out_other)
     grad_small = in_order(product_tn(dp_small, gathered1))
-    d_normed1, gate_one, gate_two = together(d_normed1, gate_one, gate_two)
-    grad_gate = settle(d_gate, split2, (gate_one, gate_two))
     d_tokens_part, grad_norm1 = norm_back(scaled1, inverse1, norm1_gain, d_normed1)
     tokens_grad = (d_resid.astype(jnp.float32) + d_tokens_part).astype(jnp.bfloat16)
-    partial = product_nn(hidden, w_down).astype(jnp.bfloat16)
-    small_parts = [dc_query, dc_key, dc_value, ddecay, grad_small]
-    gain_parts = [grad_norm1, grad_norm2, dgain]
-    grad_out, grad_gate_out, grad_value, grad_pair, small_sum, gain_sum, mixed = reduce_groups(
-        [grad_out, grad_gate_out, grad_value, grad_pair],
-        pack(small_parts), pack(gain_parts), partial, resid, 6,
-    )
-    dc_query, dc_key, dc_value, ddecay, grad_small = unpack(small_sum, small_parts)
-    grad_norm1, grad_norm2, dgain = unpack(gain_sum, gain_parts)
-    grad_small = lax.dynamic_index_in_dim(grad_small, lax.axis_index("dp"), 1, keepdims=False).T
+    value_width = w_value.shape[1]
+    turn = (width // lax.axis_size("dp")) % 128 == 0
+    thin = grad_small.reshape(grad_small.shape[0], width)
+    small = [dc_query, dc_key, dc_value, ddecay, thin, grad_norm1[None], grad_norm2[None], dgain]
+    (
+        grad_out, grad_gate_out, grad_value, grad_query, grad_key,
+        dc_query, dc_key, dc_value, ddecay, thin, grad_norm1, grad_norm2, dgain, mixed,
+    ) = reduce_groups(
+        [out_keep], [grad_gate_out, grad_value, grad_pair],
+        [
+            [(0, value_width, turn)],
+            [(0, value_width, False)],
+            [(0, value_width, False)],
+            [(0, key_width, False), (key_width, key_width, False)],
+        ],
+        small, partial, resid, 6,
+    )
+    each = width // lax.axis_size("dp")
+    grad_small = lax.dynamic_slice_in_dim(thin, lax.axis_index("dp") * each, each, 1).T
     return (
         mixed,
         final[None],
         tokens_grad,
-        grad_norm1,
-        grad_pair[:, :key_width],
-        grad_pair[:, key_width:],
+        grad_norm1[0],
+        grad_query,
+        grad_key,
         grad_value,
         grad_gate_out,
         grad_small[:, :heads],
@@ -1288,8 +1504,8 @@
         ddecay[0, :heads],
         ddecay[0, heads:],
         dgain[0],
-        grad_out.T,
-        grad_norm2,
+        grad_out if turn else grad_out.T,
+        grad_norm2[0],
         grad_gate.T,
         grad_up.T,
         grad_down,

time: 695 us -> 626 us (0.901)
  matrix products: 88.5 us -> 16 us
  waiting for transfers between devices: 10.7 us -> 35.6 us
  Pallas kernels: 515 us -> 498 us
    dot_general x14 -> x3, matrix products: 77.4 us -> 16 us  [product_tn(): lax.dot_general(left, right, (((0,), (0,)), ((), ())), preferred_element_...]
    pallas_call x7 -> x11, Pallas kernels: 444 us -> 411 us  [the longest x1 159 us: reduce_groups(): pl.pallas_call(lambda *refs: reduce_kernel(groups, early, shapes, *refs),...]
    ppermute x9 -> x6, waiting for transfers between devices: 10.7 us -> 28.7 us  [flip(): lax.ppermute(array, axis, [(place, place ^ bit) for place in range(size)])]
    pallas_call x1, Pallas kernels: 36.8 us -> 52.8 us  [mixer_backward(): pl.pallas_call(mixer_backward_kernel, grid_spec=pltpu.PrefetchScalarGridS...]
    dot_general x1 -> x0, matrix products: 11.1 us -> none  [product_nn(): return jnp.dot(left, right, preferred_element_type=jnp.float32)]
  transfers between devices with their start and end apart: 12 -> 9, of which waited for: 2 -> 3; matrix products, arithmetic and copies ran while one was open for 15% -> 4% of each run, Pallas kernels for 62% -> 68%
where the time goes in v3:
time: 626 us; the launch traced here: 616 us
  Pallas kernels  498 us (80%)
  waiting for transfers between devices  35.6 us (6%)
  other arithmetic  25.7 us (4%)
  local copies, waits for them, and re-layouts  18.6 us (3%)
  matrix products  16 us (3%)
  between operations  15.6 us (2%)
  starting transfers between devices  6.6 us (1%)
    pallas_call x1, Pallas kernels, reduce_groups(): pl.pallas_call(lambda *refs: reduce_kernel(groups, early, shapes, *refs),...  159 us
    pallas_call x3, Pallas kernels, gather_call(): pl.pallas_call(body, name=name, grid=() if grid is None else (grid,), in_...  118 us
    pallas_call x3, Pallas kernels, scatter_products(): pl.pallas_call(lambda *refs: scatter_kernel(turned, len(lefts), fill is n...  104 us
    pallas_call x1, Pallas kernels, mixer_backward(): pl.pallas_call(mixer_backward_kernel, grid_spec=pltpu.PrefetchScalarGridS...  52.8 us
    pallas_call x1, Pallas kernels, mixer_forward(): pl.pallas_call(mixer_forward_kernel, grid_spec=pltpu.PrefetchScalarGridSp...  35.1 us
    pallas_call x4, Pallas kernels, turned_product(): pl.pallas_call(lambda *refs: turned_kernel(len(more), *refs), name='turne...  30 us
    ppermute x6, waiting for transfers between devices, flip(): lax.ppermute(array, axis, [(place, place ^ bit) for place in range(size)])  28.7 us
    dot_general x3, matrix products, product_tn(): lax.dot_general(left, right, (((0,), (0,)), ((), ())), preferred_element_...  16 us
  transfers between devices with their start and end apart: 9, of which 3 were waited for; matrix products, arithmetic and copies ran while one was open for 4% of the time, Pallas kernels for 68%

profile of v3, /device:TPU:0, one launch (start us, length us, event | category | flops | bytes accessed | tf_op | source)
XLA Modules:
  0.0 616.5 jit_solution(12812558488578547833)
XLA Ops:
  7.2 1.5 fusion.11
  8.8 1.4 pad_maximum_fusion.refs_4_
  10.1 2.5 fusion.4.own_ref
  12.6 39.3 %project.1 = (bf16[1024,512]{1,0:T(8,128)(2,1)}, bf16[1024,512]{1,0:T(8,128)(2,1)}, bf16[1024,1024]{1,0:T(8,128)(2,1)}, bf16[1024,1024]{1,0:T(8,128)(2,1)}, f32[...) custom-call(bf16[256,2048]{1,0:T(8,128)(2,1)} %fusion.4.own_ref, bf16[2048,512]{1,0:T(8,128)(2,1)} %refs_5_.1, ...), custom_call_target="tpu_custom_call" | custom-call | flops 1 | bytes 1 | tf_op jit(solution)/shard_map/project/pallas_call | solution.py:645
  52.0 0.2 collective-permute-start
  52.1 1.3 collective-permute-start.1
  54.7 0.6 pad_add_fusion.scal
  55.3 35.1 %mixer_forward.1 = (bf16[1024,1024]{1,0:T(8,128)(2,1)}, f32[4,128,256]{2,1,0:T(8,128)}, bf16[1024,1024]{1,0:T(8,128)(2,1)}, bf16[1024,1024]{1,0:T(8,128)(2,1)}, ...) custom-call(s32[2]{0:T(128)} %pad_add_fusion.scal, bf16[1024,512]{1,0:T(8,128)(2,1)} %get-tuple-element.102.pq.pq16, ...), custom_call_target="tpu_custom_call" | custom-call | flops 1 | bytes 1 | tf_op jit(solution)/shard_map/mixer_forward/pallas_call | solution.py:199
  90.4 0.1 collective-permute-start.2
  90.5 31.0 %scatter_products.3 = f32[256,2048]{1,0:T(8,128)} custom-call(bf16[1024,1024]{1,0:T(8,128)(2,1)} %get-tuple-element.107.refs_0_.right_two.refs_1_, bf16[1024,2048]{1,0:T(8,128)(2,1)} %refs_1_.5), custom_call_target="tpu_custom_call" | custom-call | flops 1 | bytes 1 | tf_op jit(solution)/shard_map/scatter_products/pallas_call | solution.py:1002
  121.5 2.0 multiply_reduce_fusion.2
  123.5 1.4 multiply_convert_fusion.own_ref
  124.9 1.0 copy-done.15
  125.9 40.5 %feed.1 = (bf16[1024,1376]{1,0:T(8,128)(2,1)}, bf16[1024,1376]{1,0:T(8,128)(2,1)}, bf16[1024,1376]{1,0:T(8,128)(2,1)}, bf16[1024,2048]{1,0:T(8,128)(2,1)}, bf16[1024,2048]{1,0:T(8,128)(2,1)}) custom-call(bf16[256,2048]{1,0:T(8,128)(2,1)} %multiply_convert_fusion.own_ref, bf16[256,2048]{1,0:T(8,128)(2,1)} %refs_0_.2, ...), custom_call_target="tpu_custom_call" | custom-call | flops 1 | bytes 1 | tf_op jit(solution)/shard_map/feed/pallas_call | solution.py:645
  166.4 7.2 %convolution_convert_fusion.1 = bf16[1376,1024]{1,0:T(8,128)(2,1)} fusion(bf16[1024,1376]{1,0:T(8,128)(2,1)} %get-tuple-element.115.refs_1_.refs_0_, bf16[1024,2048]{1,0:T(8,128)(2,1)} %get-tuple-element.113.refs_6_.refs_1_), kind=kOutput, calls=%fused_computation.3 | convolution fusion | flops 2887090176 | bytes 7798784 | tf_op jit(solution)/shard_map/dot_general | solution.py:475
  173.7 8.0 %convolution_convert_fusion = bf16[1376,2048]{1,0:T(8,128)(2,1)} fusion(bf16[1024,1376]{1,0:T(8,128)(2,1)S(1)} %copy-done.7, bf16[1024,2048]{1,0:T(8,128)(2,1)S(1)} %copy-done.27), kind=kOutput, calls=%fused_computation.2 | convolution fusion | flops 5774180352 | bytes 12648448 | tf_op jit(solution)/shard_map/dot_general | solution.py:475
  181.7 0.0 reduce-scatter.8.cloned.1.call-start
  181.8 1.5 collective-permute-start.3
  183.3 34.3 %scatter_products.4 = f32[256,2048]{1,0:T(8,128)} custom-call(bf16[1024,1376]{1,0:T(8,128)(2,1)} %get-tuple-element.114.refs_0_.refs_5_, bf16[1024,1376]{1,0:T(8,128)(2,1)} %get-tuple-element.115.refs_1_.refs_0_, bf16[1376,2048]{1,0:T(8,128)(2,1)} %bitcast.42, bf16[1376,2048]{1,0:T(8,128)(2,1)} %bitcast.44), custom_call_target="tpu_custom_call" | custom-call | flops 1 | bytes 1 | tf_op jit(solution)/shard_map/scatter_products/pallas_call | solution.py:1002
  217.6 2.9 multiply_reduce_fusion
  220.6 2.9 add_convert_fusion.own_ref
  223.4 37.8 %gate_back.1 = (bf16[1024,1024]{1,0:T(8,128)(2,1)}, bf16[1024,1024]{1,0:T(8,128)(2,1)}, f32[1,256]{1,0:T(1,128)}, bf16[1376,1024]{1,0:T(8,128)(2,1)}, bf16[1024,2048]{1,0:T(8,128)(2,1)}) custom-call(bf16[256,2048]{1,0:T(8,128)(2,1)} %add_convert_fusion.own_ref, s32[1]{0:T(128)S(6)} %add.64.refs_0_, bf16[1024,2048]{1,0:T(8,128)(2,1)} %refs_1_.5, ...), custom_call_target="tpu_custom_call" | custom-call | flops 1 | bytes 1 | tf_op jit(solution)/shard_map/gate_back/pallas_call | solution.py:645
  261.2 13.9 %collective-permute-done.3.refs_2_ = bf16[1376,1024]{1,0:T(8,128)(2,1)S(1)} collective-permute-done((bf16[1376,1024]{1,0:T(8,128)(2,1)}, bf16[1376,1024]{1,0:T(8,128)(2,1)S(1)}, u32[]{:S(2)}, u32[]{:S(2)}) %collective-permute-start.3) | collective-permute-done | bytes 2818080 | tf_op jit(solution)/shard_map/ppermute | solution.py:1360
  275.1 1.5 copy-done.8
  276.6 7.5 %turned_product.4 = bf16[1376,1024]{1,0:T(8,128)(2,1)} custom-call(bf16[1024,1376]{1,0:T(8,128)(2,1)} %get-tuple-element.115.refs_1_.refs_0_, bf16[1024,2048]{1,0:T(8,128)(2,1)} %get-tuple-element.113.refs_6_.refs_1_, bf16[1376,1024]{1,0:T(8,128)(2,1)} %copy-done.8), custom_call_target="tpu_custom_call" | custom-call | flops 1 | bytes 1 | tf_op jit(solution)/shard_map/turned_product/pallas_call | solution.py:1038
  284.2 0.0 reduce-scatter.6.cloned.1.call-start
  284.2 1.8 collective-permute-start.4
  286.0 52.8 %mixer_backward.1 = (bf16[1024,1024]{1,0:T(8,128)(2,1)}, bf16[1024,1024]{1,0:T(8,128)(2,1)}, bf16[1024,8]{1,0:T(8,128)(2,1)}, f32[4,512]{1,0:T(4,128)}, f32[4,51...) custom-call(s32[2]{0:T(128)} %pad_add_fusion.scal, ...), custom_call_target="tpu_custom_call" | custom-call | flops 1 | bytes 1 | tf_op jit(solution)/shard_map/mixer_backward/pallas_call | solution.py:426
  338.8 2.3 convert_element_type.39
  341.1 14.8 %collective-permute-done.4.refs_2_ = bf16[1376,1024]{1,0:T(8,128)(2,1)} collective-permute-done((bf16[1376,1024]{1,0:T(8,128)(2,1)}, bf16[1376,1024]{1,0:T(8,128)(2,1)}, u32[]{:S(2)}, u32[]{:S(2)}) %collective-permute-start.4) | collective-permute-done | bytes 2818080 | tf_op jit(solution)/shard_map/ppermute | solution.py:1360
  355.9 7.5 %turned_product.7 = bf16[1376,1024]{1,0:T(8,128)(2,1)} custom-call(bf16[1024,1376]{1,0:T(8,128)(2,1)} %get-tuple-element.114.refs_0_.refs_5_, bf16[1024,2048]{1,0:T(8,128)(2,1)} %get-tuple-element.113.refs_6_.refs_1_, bf16[1376,1024]{1,0:T(8,128)(2,1)} %collective-permute-done.4.refs_2_), custom_call_target="tpu_custom_call" | custom-call | flops 1 | bytes 1 | tf_op jit(solution)/shard_map/turned_product/pallas_call | solution.py:1038
  363.4 0.7 copy-done.18
  364.1 1.0 copy.51
  365.1 1.7 collective-permute-start.5
  366.8 0.6 gather_fusion
  367.5 0.1 broadcast_in_dim.44
  367.6 6.8 %reduce-scatter.8.cloned.1.call-done = bf16[1376,256]{1,0:T(8,128)(2,1)} async-done(((bf16[1376,1024]{1,0:T(8,128)(2,1)}), bf16[1376,256]{1,0:T(8,128)(2,1)}) %reduce-scatter.8.cloned.1.call-update) | async-done | bytes 704528 | tf_op jit(solution)/shard_map/reduce_scatter | solution.py:1373
  374.4 2.3 convert_bitcast_fusion
  376.7 8.6 %turned_product.5.refs_2_ = bf16[2048,1024]{1,0:T(8,128)(2,1)} custom-call(bf16[1024,2048]{1,0:T(8,128)(2,1)} %get-tuple-element.130.left_one.refs_0_.refs_10_, bf16[1024,1024]{1,0:T(8,128)(2,1)} %get-tuple-element.146.refs_1_.refs_2_), custom_call_target="tpu_custom_call" | custom-call | flops 1 | bytes 1 | tf_op jit(solution)/shard_map/turned_product/pallas_call | solution.py:1038
  385.3 38.4 %scatter_products.5 = (f32[256,2048]{1,0:T(8,128)}, bf16[2048,1024]{1,0:T(8,128)(2,1)}) custom-call(bf16[1024,1024]{1,0:T(8,128)(2,1)} %get-tuple-element.144.refs_0_.refs_1_.refs_11_, bf16[1024,1024]{1,0:T(8,128)(2,1)} %get-tuple-element.144.refs_0_.refs_1_.refs_11_, bf16[1024,1024]{1,0:T(8,128)(2,1)} %get-tuple-element.146.refs_1_.refs_2_, ...), custom_call_target="tpu_custom_call" | custom-call | flops 1 | bytes 1 | tf_op jit(solution)/shard_map/scatter_products/pallas_call | solution.py:1002
  423.7 0.7 fusion.16
  424.4 0.6 gather_fusion.1
  424.9 0.6 broadcast_select_fusion.refs_8_
  425.6 1.3 copy-done.9
  426.9 6.5 %turned_product.6.refs_0_ = bf16[1024,1024]{1,0:T(8,128)(2,1)} custom-call(bf16[1024,2048]{1,0:T(8,128)(2,1)} %get-tuple-element.123.left_two.refs_0_, bf16[1024,1024]{1,0:T(8,128)(2,1)} %get-tuple-element.107.refs_0_.right_two.refs_1_, bf16[1024,1024]{1,0:T(8,128)(2,1)} %copy-done.9), custom_call_target="tpu_custom_call" | custom-call | flops 1 | bytes 1 | tf_op jit(solution)/shard_map/turned_product/pallas_call | solution.py:1038
  433.4 1.2 fusion.6
  434.6 159.3 %reduce_groups.1 = (f32[1024,256]{1,0:T(8,128)}, f32[256,1024]{1,0:T(8,128)}, f32[256,1024]{1,0:T(8,128)}, f32[256,512]{1,0:T(8,128)}, f32[256,512]{1,0:T(8,128)...) custom-call(bf16[1024,1024]{1,0:T(8,128)(2,1)} %turned_product.6.ref, ...), custom_call_target="tpu_custom_call" | custom-call | flops 1 | bytes 1 | tf_op jit(solution)/shard_map/reduce_groups/pallas_call | solution.py:1313
  593.9 0.7 dynamic-slice_bitcast_fusion
  594.7 1.3 slice_bitcast_fusion
  596.0 0.6 fusion.15
  596.6 1.7 fusion.10
  598.2 2.4 convert_bitcast_fusion.1
  600.7 1.0 copy.66
  601.6 0.6 copy.67
  602.2 0.8 copy.68
  603.0 0.8 copy.69
  603.9 1.0 copy.70
  604.8 1.0 copy.71
  605.8 0.6 copy.72
  606.4 0.6 copy.73
  607.0 0.6 copy.74
  607.6 0.6 copy.75
  608.2 1.0 copy.76
  609.2 0.6 copy.77
  (72 shorter events, 0.3 us)
Async XLA Ops:
  7.2 331.6 %reduce-scatter.4.cloned.1.call-start = ((), (), s32[]{:S(2)}) async-start(), calls=%async_computation.3 | async-start | bytes 6340608 | tf_op jit(solution)/shard_map/reduce_scatter | solution.py:1433
  52.0 38.4 %collective-permute-start = (bf16[256,2048]{1,0:T(8,128)(2,1)}, bf16[256,2048]{1,0:T(8,128)(2,1)}, u32[]{:S(2)}, u32[]{:S(2)}) collective-permute-start(bf16[256,2048]{1,0:T(8,128)(2,1)} %refs_0_.2), channel_id=1, source_target_pairs={{0,2},{1,3},{2,0},{3,1},{4,6},{5,7},{6,4},{7,5},{8,10},{9,11},{10,... | collective-permute-start | bytes 3145736 | tf_op jit(solution)/shard_map/ppermute | solution.py:1360
  52.1 72.8 %collective-permute-start.1 = (bf16[256,2048]{1,0:T(8,128)(2,1)}, bf16[256,2048]{1,0:T(8,128)(2,1)}, u32[]{:S(2)}, u32[]{:S(2)}) collective-permute-start(bf16[256,2048]{1,0:T(8,128)(2,1)} %refs_0_.2), channel_id=1, source_target_pairs={{0,1},{1,0},{2,3},{3,2},{4,5},{5,4},{6,7},{7,6},{8,9},{9,8},{10,11... | collective-permute-start | bytes 3145736 | tf_op jit(solution)/shard_map/ppermute | solution.py:1360
  90.4 31.1 %copy-start.3 = (bf16[256,2048]{1,0:T(8,128)(2,1)S(1)}, bf16[256,2048]{1,0:T(8,128)(2,1)}, u32[]{:S(2)}) copy-start(bf16[256,2048]{1,0:T(8,128)(2,1)} %param.24) | copy-start | bytes 3145732
  90.4 34.5 %collective-permute-start.2 = (bf16[256,2048]{1,0:T(8,128)(2,1)}, bf16[256,2048]{1,0:T(8,128)(2,1)S(1)}, u32[]{:S(2)}, u32[]{:S(2)}) collective-permute-start(bf16[256,2048]{1,0:T(8,128)(2,1)} %collective-permute-done.refs_2_), channel_id=1, source_target_pairs={{0,1},{1,0},{2,3},{3,2},{4,5},{5,4},{6,7},{7,6},{8,9},{9,8},{10,11... | collective-permute-start | bytes 3145736 | tf_op jit(solution)/shard_map/ppermute | solution.py:1360
  121.5 2.0 copy-start.19
  123.4 97.1 %copy-start.2 = (f32[256,2048]{1,0:T(8,128)}, f32[256,2048]{1,0:T(8,128)S(1)}, u32[]{:S(2)}) copy-start(f32[256,2048]{1,0:T(8,128)S(1)} %get-tuple-element.184.refs_13_) | copy-start | bytes 6291460
  124.9 1.0 copy-start.15
  166.4 7.3 %copy-start.7 = (bf16[1024,1376]{1,0:T(8,128)(2,1)S(1)}, bf16[1024,1376]{1,0:T(8,128)(2,1)}, u32[]{:S(2)}) copy-start(bf16[1024,1376]{1,0:T(8,128)(2,1)} %get-tuple-element.111.left_three) | copy-start | bytes 8454148
  166.4 7.3 %copy-start.27 = (bf16[1024,2048]{1,0:T(8,128)(2,1)S(1)}, bf16[1024,2048]{1,0:T(8,128)(2,1)}, u32[]{:S(2)}) copy-start(bf16[1024,2048]{1,0:T(8,128)(2,1)} %get-tuple-element.112) | copy-start | bytes 12582916
  181.7 192.7 %reduce-scatter.8.cloned.1.call-start = ((), (), s32[]{:S(2)}) async-start(), calls=%async_computation.5 | async-start | bytes 3522560 | tf_op jit(solution)/shard_map/reduce_scatter | solution.py:1373
  181.8 93.4 %collective-permute-start.3 = (bf16[1376,1024]{1,0:T(8,128)(2,1)}, bf16[1376,1024]{1,0:T(8,128)(2,1)S(1)}, u32[]{:S(2)}, u32[]{:S(2)}) collective-permute-start(bf16[1376,1024]{1,0:T(8,128)(2,1)} %convolution_convert_fusion.1), channel_id=1, source_target_pairs={{0,4},{4,0},{8,12},{12,8},{16,20},{20,16},{24,28},{28,24},{1,5},{5... | collective-permute-start | bytes 8454152 | tf_op jit(solution)/shard_map/ppermute | solution.py:1360
  217.6 3.0 copy-start.4
  275.1 1.5 copy-start.8
  284.2 314.1 %reduce-scatter.6.cloned.1.call-start = ((), (), s32[]{:S(2)}) async-start(), calls=%async_computation.4 | async-start | bytes 3522560 | tf_op jit(solution)/shard_map/reduce_scatter | solution.py:1373
  284.2 71.7 %collective-permute-start.4 = (bf16[1376,1024]{1,0:T(8,128)(2,1)}, bf16[1376,1024]{1,0:T(8,128)(2,1)}, u32[]{:S(2)}, u32[]{:S(2)}) collective-permute-start(bf16[1376,1024]{1,0:T(8,128)(2,1)} %get-tuple-element.143), channel_id=1, source_target_pairs={{0,4},{4,0},{8,12},{12,8},{16,20},{20,16},{24,28},{28,24},{1,5},{5... | collective-permute-start | bytes 8454152 | tf_op jit(solution)/shard_map/ppermute | solution.py:1360
  363.4 0.8 copy-start.18
  363.4 3.4 copy-start
  365.1 60.5 %collective-permute-start.5 = (bf16[1024,1024]{1,0:T(8,128)(2,1)}, bf16[1024,1024]{1,0:T(8,128)(2,1)S(1)}, u32[]{:S(2)}, u32[]{:S(2)}) collective-permute-start(bf16[1024,1024]{1,0:T(8,128)(2,1)} %get-tuple-element.149), channel_id=1, source_target_pairs={{0,4},{4,0},{8,12},{12,8},{16,20},{20,16},{24,28},{28,24},{1,5},{5... | collective-permute-start | bytes 6291464 | tf_op jit(solution)/shard_map/ppermute | solution.py:1360
  385.3 38.4 %copy-start.1 = (bf16[1024,2048]{1,0:T(8,128)(2,1)S(1)}, bf16[1024,2048]{1,0:T(8,128)(2,1)}, u32[]{:S(2)}) copy-start(bf16[1024,2048]{1,0:T(8,128)(2,1)} %get-tuple-element.130.left_one.refs_0_.refs_10_) | copy-start | bytes 12582916
  385.3 38.4 %copy-start.10 = (bf16[1024,8]{1,0:T(8,128)(2,1)S(1)}, bf16[1024,8]{1,0:T(8,128)(2,1)}, u32[]{:S(2)}) copy-start(bf16[1024,8]{1,0:T(8,128)(2,1)} %get-tuple-element.147.refs_4_) | copy-start | bytes 49156
  425.6 1.4 copy-start.9
  426.9 6.5 %copy-start.6 = (f32[256,2048]{1,0:T(8,128)S(1)}, f32[256,2048]{1,0:T(8,128)}, u32[]{:S(2)}) copy-start(f32[256,2048]{1,0:T(8,128)} %get-tuple-element.158) | copy-start | bytes 6291460
  426.9 6.5 %copy-start.20 = (f32[2048]{0:T(1024)S(1)}, f32[2048]{0:T(1024)}, u32[]{:S(2)}) copy-start(f32[2048]{0:T(1024)} %param.25) | copy-start | bytes 24580
  434.6 161.9 %copy-start.5 = (bf16[256,2048]{1,0:T(8,128)(2,1)S(1)}, bf16[256,2048]{1,0:T(8,128)(2,1)}, u32[]{:S(2)}) copy-start(bf16[256,2048]{1,0:T(8,128)(2,1)} %add_convert_fusion.own_ref) | copy-start | bytes 3145732
  598.2 2.4 copy-start.14
  598.2 3.4 copy-start.25
  598.2 4.0 copy-start.17
  600.7 2.4 copy-start.16
  600.7 3.2 copy-start.13
  602.2 2.6 copy-start.12
  603.8 2.0 copy-start.24
  603.8 2.6 copy-start.23
  603.8 3.2 copy-start.21
  603.8 3.8 copy-start.26
  603.9 4.3 copy-start.11
  604.8 4.3 copy-start.22
Sparse Core Ops, SparseCore 0:
  181.8 136.3 reduce-scatter.3
  320.5 53.8 reduce-scatter.7
  376.9 54.9 reduce-scatter.5

commit v4 on v3

--- a/solution.py
+++ b/solution.py
@@ -102,78 +102,102 @@
     kslice = [slice(h * dk, (h + 1) * dk) for h in every]
     vslice = [slice(h * dv, (h + 1) * dv) for h in every]
 
-    row_at = chunk * CHUNK + lax.broadcasted_iota(jnp.int32, (CHUNK, 1), 0)
-    valid = jnp.where(row_at < scal[0], 1.0, 0.0)
+    subs = range(pq.shape[0] // CHUNK)
+    units = [(sub, h) for sub in subs for h in every]
+    parts = range(len(units))
     tri = jnp.where(full, 1.0, 0.0)
-    gcol, grow = decay_terms(small[...], dlog[...], dbias[...], valid, tri)
+    valid, gcol, grow = [], [], []
+    for sub in subs:
+        row_at = (chunk * len(subs) + sub) * CHUNK + lax.broadcasted_iota(jnp.int32, (CHUNK, 1), 0)
+        valid.append(jnp.where(row_at < scal[0], 1.0, 0.0))
+        cols, rows = decay_terms(
+            small[sub * CHUNK : (sub + 1) * CHUNK, :], dlog[...], dbias[...], valid[sub], tri
+        )
+        gcol.append(cols)
+        grow.append(rows)
 
     def activated(ref, tail, taps, where):
         pre = conv_rows(ref[:, where].astype(f32), tail[:, where], taps[:, where])
         return pre * sigmoid(pre)
 
-    keys, queries, values = [], [], []
+    def cut(array, sub):
+        return array[sub * CHUNK : (sub + 1) * CHUNK]
+
+    all_keys, all_queries, all_values = [], [], []
     for h in every:
         u = activated(pk, tk, ck, kslice[h])
-        keys.append((u * unit_factor(u)).astype(bf16))
+        all_keys.append((u * unit_factor(u)).astype(bf16))
     for h in every:
         u = activated(pq, tq, cq, kslice[h])
-        queries.append((u * (unit_factor(u) * dk ** (-0.5))).astype(bf16))
-    gc = [gcol[:, h : h + 1] for h in every]
-    bc = [gcol[:, heads + h : heads + h + 1] for h in every]
-    products = [mm_nt(jnp.concatenate([keys[h], queries[h]], axis=0), keys[h]) for h in every]
-    gam = [jnp.exp(jnp.where(full, gc[h] - grow[h : h + 1, :], -1e30)) for h in every]
-    system = [jnp.where(lower, products[h][:CHUNK] * gam[h] * bc[h], 0.0) for h in every]
-    attend = [(products[h][CHUNK:] * gam[h]).astype(bf16) for h in every]
-    system_low = [system[h].astype(bf16) for h in every]
+        all_queries.append((u * (unit_factor(u) * dk ** (-0.5))).astype(bf16))
+    keys = [cut(all_keys[h], sub) for sub, h in units]
+    queries = [cut(all_queries[h], sub) for sub, h in units]
+    gc = [gcol[sub][:, h : h + 1] for sub, h in units]
+    bc = [gcol[sub][:, heads + h : heads + h + 1] for sub, h in units]
+    products = [mm_nt(jnp.concatenate([keys[u], queries[u]], axis=0), keys[u]) for u in parts]
+    gam = [
+        jnp.exp(jnp.where(full, gc[u] - grow[sub][h : h + 1, :], -1e30))
+        for u, (sub, h) in enumerate(units)
+    ]
+    system = [jnp.where(lower, products[u][:CHUNK] * gam[u] * bc[u], 0.0) for u in parts]
+    attend = [(products[u][CHUNK:] * gam[u]).astype(bf16) for u in parts]
+    system_low = [system[u].astype(bf16) for u in parts]
     first = jnp.where(level == 1, 1.0, 0.0).astype(bf16)
-    inverse = [eye_low - system_low[h] * first for h in every]
+    inverse = [eye_low - system_low[u] * first for u in parts]
     size = 2
     while size < CHUNK:
         mask = jnp.where((level >= size) & (level < 2 * size), 1.0, 0.0).astype(bf16)
-        inner = [mm(system_low[h] * mask, inverse[h]).astype(bf16) for h in every]
-        inverse = [inverse[h] - mm(inverse[h], inner[h]).astype(bf16) for h in every]
+        inner = [mm(system_low[u] * mask, inverse[u]).astype(bf16) for u in parts]
+        inverse = [inverse[u] - mm(inverse[u], inner[u]).astype(bf16) for u in parts]
         size *= 2
     left_over = [
-        (eye - inverse[h].astype(f32))
-        - mm(system_low[h], inverse[h])
-        - mm((system[h] - system_low[h].astype(f32)).astype(bf16), inverse[h])
-        for h in every
+        (eye - inverse[u].astype(f32))
+        - mm(system_low[u], inverse[u])
+        - mm((system[u] - system_low[u].astype(f32)).astype(bf16), inverse[u])
+        for u in parts
     ]
-    inverse = [(inverse[h].astype(f32) + mm(inverse[h], left_over[h])) for h in every]
+    inverse = [(inverse[u].astype(f32) + mm(inverse[u], left_over[u])) for u in parts]
+    for u, (sub, h) in enumerate(units):
+        tt_out[sub, h] = jnp.transpose(inverse[u]).astype(bf16)
+    inverse = [inverse[u].astype(bf16) for u in parts]
     for h in every:
-        tt_out[0, h] = jnp.transpose(inverse[h]).astype(bf16)
-    inverse = [inverse[h].astype(bf16) for h in every]
-    for h in every:
-        values.append(activated(pv, tv, cv, vslice[h]))
+        all_values.append(activated(pv, tv, cv, vslice[h]))
     for ref, tail in ((pq, tq), (pk, tk), (pv, tv)):
-        tail[...] = ref[CHUNK - 16 :, :].astype(f32)[8:]
-    growth = [jnp.exp(gc[h]) for h in every]
-    keys_f = [keys[h].astype(f32) for h in every]
+        tail[...] = ref[ref.shape[0] - 16 :, :].astype(f32)[8:]
+    growth = [jnp.exp(gc[u]) for u in parts]
+    keys_f = [keys[u].astype(f32) for u in parts]
     pair = [
         jnp.concatenate(
-            [(keys_f[h] * growth[h]).astype(bf16), (queries[h].astype(f32) * growth[h]).astype(bf16)], axis=0
+            [(keys_f[u] * growth[u]).astype(bf16), (queries[u].astype(f32) * growth[u]).astype(bf16)], axis=0
         )
-        for h in every
+        for u in parts
     ]
+    now = [state[h] for h in every]
+    for sub in subs:
+        mine = [sub * heads + h for h in every]
+        for h in every:
+            s_out[sub, h] = now[h].astype(bf16)
+        carried = [mm(pair[u], now[h]) for h, u in enumerate(mine)]
+        delta = [
+            mm(inverse[u], bc[u] * (cut(all_values[h], sub) - carried[h][:CHUNK])).astype(bf16)
+            for h, u in enumerate(mine)
+        ]
+        out = [carried[h][CHUNK:] + mm(attend[u], delta[h]) for h, u in enumerate(mine)]
+        for h, u in enumerate(mine):
+            last = gc[u][CHUNK - 1 : CHUNK]
+            late = (keys_f[u] * jnp.exp(last - gc[u])).astype(bf16)
+            now[h] = jnp.exp(last) * now[h] + mm_tn(late, delta[h])
+        here = slice(sub * CHUNK, (sub + 1) * CHUNK)
+        for h in every:
+            delta_out[here, vslice[h]] = delta[h]
+            o_out[here, vslice[h]] = out[h].astype(bf16)
+            inv = lax.rsqrt(jnp.mean(out[h] * out[h], axis=-1, keepdims=True) + 1e-05)
+            gate = pg[here, vslice[h]].astype(f32)
+            gated_out[here, vslice[h]] = (
+                out[h] * (inv * valid[sub]) * gain[...] * (gate * sigmoid(gate))
+            ).astype(bf16)
     for h in every:
-        s_out[0, h] = state[h].astype(bf16)
-    carried = [mm(pair[h], state[h]) for h in every]
-    delta = [
-        mm(inverse[h], bc[h] * (values[h] - carried[h][:CHUNK])).astype(bf16) for h in every
-    ]
-    out = [carried[h][CHUNK:] + mm(attend[h], delta[h]) for h in every]
-    for h in every:
-        last = gc[h][CHUNK - 1 : CHUNK]
-        late = (keys_f[h] * jnp.exp(last - gc[h])).astype(bf16)
-        state[h] = jnp.exp(last) * state[h] + mm_tn(late, delta[h])
-    for h in every:
-        delta_out[:, vslice[h]] = delta[h]
-        o_out[:, vslice[h]] = out[h].astype(bf16)
-        inv = lax.rsqrt(jnp.mean(out[h] * out[h], axis=-1, keepdims=True) + 1e-05)
-        gate = pg[:, vslice[h]].astype(f32)
-        gated_out[:, vslice[h]] = (
-            out[h] * (inv * valid) * gain[...] * (gate * sigmoid(gate))
-        ).astype(bf16)
+        state[h] = now[h]
 
     @pl.when(chunk == pl.num_programs(0) - 1)
     def _():
@@ -185,22 +209,25 @@
     heads, dk, dv = s0.shape
     chunks = rows // CHUNK
     per = chunks // 4
+    joined = 2 if per % 2 == 0 else 1
 
     def by_rows(width):
-        return pl.BlockSpec((CHUNK, width), lambda c, s: (block_place(c, s[1], per), 0))
+        return pl.BlockSpec(
+            (joined * CHUNK, width), lambda c, s: (block_place(c, s[1], per // joined), 0)
+        )
 
     def whole(*shape):
         return pl.BlockSpec(shape, lambda c, s: (0,) * len(shape))
 
     def by_chunk(*shape):
-        return pl.BlockSpec((1,) + shape, lambda c, s: (c,) + (0,) * len(shape))
+        return pl.BlockSpec((joined,) + shape, lambda c, s: (c,) + (0,) * len(shape))
 
     kw, vw = heads * dk, heads * dv
     return pl.pallas_call(
         mixer_forward_kernel,
         grid_spec=pltpu.PrefetchScalarGridSpec(
             num_scalar_prefetch=1,
-            grid=(chunks,),
+            grid=(chunks // joined,),
             in_specs=[
                 by_rows(kw), by_rows(kw), by_rows(vw), by_rows(vw), by_rows(2 * heads),
                 whole(4, kw), whole(4, kw), whole(4, vw), whole(1, heads), whole(1, heads),
@@ -230,7 +257,7 @@
 
 
 def mixer_backward_kernel(
-    scal, pq, pk, pv, pq16, pk16, pv16, small, do_in, delta_in, s_in, tt_in,
+    pieces, scal, pq, pk, pv, pq16, pk16, pv16, small, do_in, delta_in, s_in, tt_in,
     cq, ck, cv, dlog_in, dbias_in, left_one, right_one, left_two, right_two, left_three, right_three,
     dpqk, dpv, dsmall, dcq, dck, dcv, ddecay, product_one, product_two, product_three,
     dstate, nq, nk, nv,
@@ -247,7 +274,11 @@
 
     product_one[...] = mm_tn(left_one[...], right_one[...]).astype(bf16)
     product_two[...] = mm_tn(left_two[...], right_two[...]).astype(bf16)
-    product_three[...] = mm(left_three[...], right_three[...]).astype(bf16)
+
+    @pl.when(step < pieces)
+    def _():
+        product_three[...] = mm_tn(left_three[...], right_three[...]).astype(bf16)
+
     down, across = chunk_masks()
     lower = down > across
     full = down >= across
@@ -404,6 +435,8 @@
     per = chunks // 4
     fine = CHUNK // 16
     (left_one, right_one), (left_two, right_two), (left_three, right_three) = one, two, three
+    units, piece = left_three.shape[1], 512
+    pieces = pl.cdiv(units, piece)
     width = left_one.shape[1]
     each_one, each_two = width // chunks, width // 2 // chunks
 
@@ -423,8 +456,11 @@
     def by_chunk(*shape):
         return pl.BlockSpec((1,) + shape, lambda c, s: (chunks - 1 - c,) + (0,) * len(shape))
 
+    def at_piece(c):
+        return jnp.minimum(c, pieces - 1)
+
     return pl.pallas_call(
-        mixer_backward_kernel,
+        lambda *refs: mixer_backward_kernel(pieces, *refs),
         grid_spec=pltpu.PrefetchScalarGridSpec(
             num_scalar_prefetch=1,
             grid=(chunks,),
@@ -436,14 +472,14 @@
                 whole(4, kw), whole(4, kw), whole(4, vw), whole(1, heads), whole(1, heads),
                 pl.BlockSpec((rows, each_one), lambda c, s: (0, c)), whole(*right_one.shape),
                 pl.BlockSpec((rows, each_two), lambda c, s: (0, chunks + c)), whole(*right_two.shape),
-                pl.BlockSpec((CHUNK, left_three.shape[1]), lambda c, s: (c, 0)), whole(*right_three.shape),
+                pl.BlockSpec((rows, piece), lambda c, s: (0, at_piece(c))), whole(rows, width // 2),
             ],
             out_specs=[
                 by_rows(2 * kw), by_rows(vw), by_rows(2 * heads),
                 whole(4, kw), whole(4, kw), whole(4, vw), whole(1, 2 * heads),
                 pl.BlockSpec((each_one, right_one.shape[1]), lambda c, s: (c, 0)),
                 pl.BlockSpec((each_two, right_two.shape[1]), lambda c, s: (c, 0)),
-                pl.BlockSpec((CHUNK, right_three.shape[1]), lambda c, s: (c, 0)),
+                pl.BlockSpec((piece, width // 2), lambda c, s: (at_piece(c), 0)),
             ],
             scratch_shapes=[
                 pltpu.VMEM((heads, dk, dv), f32),
@@ -460,7 +496,7 @@
             jax.ShapeDtypeStruct((1, 2 * heads), f32),
             jax.ShapeDtypeStruct((width, right_one.shape[1]), bf16),
             jax.ShapeDtypeStruct((width // 2, right_two.shape[1]), bf16),
-            jax.ShapeDtypeStruct((rows, right_three.shape[1]), bf16),
+            jax.ShapeDtypeStruct((units, width // 2), bf16),
         ],
         compiler_params=pltpu.CompilerParams(vmem_limit_bytes=56 * 1024 * 1024),
         cost_estimate=LITTLE,
@@ -885,11 +921,11 @@
 
 def scatter_kernel(turned, count, filled, *refs):
     lefts, rights, refs = refs[:count], refs[count : 2 * count], refs[2 * count :]
-    if filled:
-        (fill_left, fill_right, out, fill), refs = refs[:4], refs[4:]
-    else:
-        out, refs = refs[0], refs[1:]
-    far_own, leave, other, send_sem, recv_sem = refs
+    sources, refs = refs[: filled + 1 if filled else 0], refs[filled + 1 if filled else 0 :]
+    out, fills, refs = refs[0], refs[1 : 1 + filled], refs[1 + filled :]
+    far_own, leave, other, send_sem, recv_sem, fill_sem = refs[:6]
+    held = refs[6:]
+    loads = [pltpu.make_async_copy(source, kept, fill_sem.at[at]) for at, (source, kept) in enumerate(zip(sources, held))]
     step = pl.program_id(0)
     parts = pl.num_programs(0) // 2
     rows = out.shape[0]
@@ -929,6 +965,8 @@
         for to in (beside, across):
             pl.semaphore_signal(barrier, inc=1, device_id={"tensor": to}, device_id_type=MESH)
         pl.semaphore_wait(barrier, 2)
+        for load in loads:
+            load.start()
 
     part = step % parts
 
@@ -956,10 +994,12 @@
 
     @pl.when(step == 2 * parts - 1)
     def _():
-        if filled:
+        for load in loads:
+            load.wait()
+        for fill, source in zip(fills, held[1:]):
             for start in range(0, fill.shape[0], COLUMNS):
                 where = slice(start, start + COLUMNS)
-                fill[where, :] = mm_tn(fill_left[:, where], fill_right[...]).astype(bf16)
+                fill[where, :] = mm_tn(held[0][:, where], source[...]).astype(bf16)
 
         def finish(part, carry):
             copy(NEAR, part).wait_recv()
@@ -994,13 +1034,14 @@
     in_specs = [left_spec(block, size) for _, block, size in lefts] + [right_spec(right) for right in rights]
     out_specs = [pl.BlockSpec((rows, width), lambda j: (0, 0))]
     out_shape = [jax.ShapeDtypeStruct((rows, width), f32)]
-    if fill is not None:
-        made = (fill[0].shape[1], fill[1].shape[1])
-        in_specs += [pl.BlockSpec(part.shape, lambda j: (0, 0)) for part in fill]
+    fill = list(fill or ())
+    in_specs += [pl.BlockSpec(memory_space=pl.ANY)] * len(fill)
+    for part in fill[1:]:
+        made = (fill[0].shape[1], part.shape[1])
         out_specs.append(pl.BlockSpec(made, lambda j: (0, 0)))
         out_shape.append(jax.ShapeDtypeStruct(made, bf16))
     outs = pl.pallas_call(
-        lambda *refs: scatter_kernel(turned, len(lefts), fill is not None, *refs),
+        lambda *refs: scatter_kernel(turned, len(lefts), max(len(fill) - 1, 0), *refs),
         name="scatter_products",
         grid=(2 * parts,),
         in_specs=in_specs,
@@ -1012,13 +1053,15 @@
             pltpu.VMEM((3, rows, width), bf16),
             pltpu.SemaphoreType.DMA((3, parts)),
             pltpu.SemaphoreType.DMA((3, parts)),
-        ],
+            pltpu.SemaphoreType.DMA((max(len(fill), 1),)),
+        ]
+        + [pltpu.VMEM(part.shape, bf16) for part in fill],
         compiler_params=pltpu.CompilerParams(
             vmem_limit_bytes=VMEM_MOST, collective_id=collective, has_side_effects=True
         ),
         cost_estimate=LITTLE,
-    )(*[left[0] for left in lefts], *rights, *(fill or ()))
-    return outs[0] if fill is None else outs
+    )(*[left[0] for left in lefts], *rights, *fill)
+    return outs if fill else outs[0]
 
 
 def turned_kernel(added, left, right, *refs):
@@ -1082,8 +1125,9 @@
     count = len(shapes)
     late = list(range(len(early), count))
     leaves, refs = refs[:count], refs[count:]
-    (taps_q, taps_k, taps_v, decay, thin, gain_one, gain_two, gain_head, partial_in, resid), refs = (
-        refs[:10], refs[10:],
+    given, refs = refs[: len(early)], refs[len(early) :]
+    (taps_q, taps_k, taps_v, decay, thin, gain_one, gain_two, gain_head, hidden_in, down_in, resid), refs = (
+        refs[:11], refs[11:],
     )
     outs = []
     for shape in shapes:
@@ -1093,8 +1137,8 @@
     lands, refs = refs[:count], refs[count:]
     sends, refs = refs[:count], refs[count:]
     keeps, refs = refs[:count], refs[count:]
-    small_land, gains_land, gains_first, rows_leave, rows_land, partial = refs[:6]
-    send_sem, recv_sem, sum_send, sum_recv, rows_send, rows_recv, keep_sem, load_sem = refs[6:]
+    small_land, gains_land, gains_first, rows_leave, rows_land, hidden, down, partial = refs[:8]
+    send_sem, recv_sem, sum_send, sum_recv, rows_send, rows_recv, keep_sem, load_sem = refs[8:]
     place = lax.axis_index("dp")
     beside = lax.axis_index("tensor")
     order = group_order(groups)
@@ -1164,13 +1208,18 @@
         )
 
     quarter = mixed.shape[0]
+    quarter_width = mixed.shape[1] // 4
     blocks = [pl.ds(at * quarter, quarter) for at in range(4)]
     row_sems = (rows_send, rows_recv)
     corner = plain_copy(partial.at[blocks[3]], rows_land.at[0], row_sems, 0, across_core)
     near = plain_copy(partial.at[blocks[1]], rows_land.at[1], row_sems, 1, across_core)
     far = plain_copy(rows_leave, rows_land.at[2], row_sems, 2, across_chip)
-    load = pltpu.make_async_copy(partial_in, partial, load_sem.at[0])
-    load.start()
+    loads = [
+        pltpu.make_async_copy(hidden_in, hidden, load_sem.at[0]),
+        pltpu.make_async_copy(down_in, down, load_sem.at[1]),
+    ]
+    for load in loads:
+        load.start()
 
     kw, line = taps_q.shape[1], taps_v.shape[1]
     lines = gain_one.shape[1] // line
@@ -1242,11 +1291,16 @@
 
     for index, (unit, chunk) in enumerate(plan):
         tensor, part = unit
+        if index == 3:
+            for load in loads:
+                load.wait()
+        if 4 <= index < 8:
+            where = pl.ds((index - 4) * quarter_width, quarter_width)
+            partial[:, where] = mm(hidden[...], down[:, where]).astype(bf16)
         if index == 8:
-            load.wait()
             corner.start()
             near.start()
-        if index == 8:
+        if index == 12:
             corner.wait_recv()
             rows_leave[...] = (
                 partial[blocks[2], :].astype(f32) + rows_land[0].astype(f32)
@@ -1260,6 +1314,7 @@
             if bit >= low_bit(chunk, groups):
                 break
             if bit == 1 and tensor in early:
+                total = total + given[tensor][rows(position[chunk], part), :].astype(f32)
                 continue
             copy(unit, chunk + bit).wait_recv()
             if bit == 1:
@@ -1291,7 +1346,7 @@
         sent.wait_send()
 
 
-def reduce_groups(early_grads, late_grads, shapes, small, partial, resid, collective):
+def reduce_groups(early_grads, given, late_grads, shapes, small, hidden, down, resid, collective):
     grads = list(early_grads) + list(late_grads)
     early = list(range(len(early_grads)))
     groups = lax.axis_size("dp")
@@ -1313,8 +1368,9 @@
     return pl.pallas_call(
         lambda *refs: reduce_kernel(groups, early, shapes, *refs),
         name="reduce_groups",
-        in_specs=[pl.BlockSpec(memory_space=pl.ANY)] * len(grads) + [vmem] * len(small)
-        + [pl.BlockSpec(memory_space=pl.ANY), vmem],
+        in_specs=[pl.BlockSpec(memory_space=pl.ANY)] * len(grads)
+        + [vmem] * (len(given) + len(small))
+        + [pl.BlockSpec(memory_space=pl.ANY)] * 2 + [vmem],
         out_specs=[vmem] * len(out_shape),
         out_shape=out_shape,
         scratch_shapes=[pltpu.VMEM((chunks * each, size), bf16) for chunks, size in zip(landed, widths)]
@@ -1326,6 +1382,8 @@
             pltpu.VMEM((bits + 2,) + gains_shape, f32),
             pltpu.VMEM((rows, width), bf16),
             pltpu.VMEM((3, rows, width), bf16),
+            pltpu.VMEM(hidden.shape, bf16),
+            pltpu.VMEM(down.shape, bf16),
             pltpu.VMEM((4 * rows, width), bf16),
             pltpu.SemaphoreType.DMA((len(grads) * PARTS * groups,)),
             pltpu.SemaphoreType.DMA((len(grads) * PARTS * groups,)),
@@ -1334,13 +1392,13 @@
             pltpu.SemaphoreType.DMA((3,)),
             pltpu.SemaphoreType.DMA((3,)),
             pltpu.SemaphoreType.DMA((len(grads),)),
-            pltpu.SemaphoreType.DMA((1,)),
+            pltpu.SemaphoreType.DMA((2,)),
         ],
         compiler_params=pltpu.CompilerParams(
             vmem_limit_bytes=VMEM_MOST, collective_id=collective, has_side_effects=True
         ),
         cost_estimate=LITTLE,
-    )(*grads, *small, partial, resid)
+    )(*grads, *given, *small, hidden, down, resid)
 
 
 def product_nn(left, right):
@@ -1370,9 +1428,7 @@
 def scatter_far(total):
     groups = lax.axis_size("dp")
     alike = [[place for place in range(groups) if place % 2 == bit] for bit in (0, 1)]
-    return lax.psum_scatter(
-        total, "dp", scatter_dimension=1, axis_index_groups=alike, tiled=True
-    ).astype(jnp.float32)
+    return lax.psum_scatter(total, "dp", scatter_dimension=1, axis_index_groups=alike, tiled=True)
 
 
 def per_device(
@@ -1430,7 +1486,7 @@
     half = width // 2
     up_other = product_tn(d_up, split2[:, half:]).astype(jnp.bfloat16)
     d_gate, d_up, grad_down, up_other = together(d_gate, d_up, grad_down, up_other)
-    grad_down = lax.psum_scatter(grad_down, "dp", scatter_dimension=1, tiled=True).astype(jnp.float32)
+    grad_down = scatter_far(grad_down)
     up_other = flip(up_other, "dp", 1)
     d_normed2 = scatter_products([d_gate, d_up], [w_gate.T, w_up.T], False, 4)
     d_resid_part, grad_norm2 = norm_back(scaled2, inverse2, norm2_gain, d_normed2)
@@ -1448,23 +1504,28 @@
     mixer_grads = mixer_backward(
         scal, p_query, p_key, p_value, p_small, do, delta, states, inverse_t,
         conv_query, conv_key, conv_value, log_row, bias_row, (gathered1, dp_gate), (resid_full, gated),
-        (hidden, w_down),
+        (d_gate, split2),
     )
     (
-        dp_pair, dp_value, dp_small, dc_query, dc_key, dc_value, ddecay, grad_gate_out, out_other, partial,
+        dp_pair, dp_value, dp_small, dc_query, dc_key, dc_value, ddecay, grad_gate_out, out_other, gate_kept,
         grad_down, gate_other,
     ) = together(*mixer_grads, grad_down, gate_other)
-    out_other = flip(out_other, "dp", 1)
-    grad_gate = scatter_far(turned_product(d_gate, split2, right_half=0, other=gate_other))
-    grad_value = turned_product(gathered1, dp_value)
-    dp_value, grad_value = together(dp_value, grad_value)
+    each = width // lax.axis_size("dp")
+    bit = lax.axis_index("dp") % 2
+    down_keep = lax.dynamic_slice_in_dim(grad_down, bit * each, each, 1)
+    down_other = lax.dynamic_slice_in_dim(grad_down, (1 - bit) * each, each, 1)
+    out_other, down_other = together(out_other, down_other)
+    out_other, down_other = flip(out_other, "dp", 1), flip(down_other, "dp", 1)
+    gate_kept = gate_kept.astype(jnp.float32) + gate_other.astype(jnp.float32)
+    grad_gate = scatter_far(gate_kept.astype(jnp.bfloat16))
     key_width = w_query.shape[1]
-    d_normed1, grad_pair = scatter_products(
+    d_normed1, grad_value, grad_pair = scatter_products(
         [(dp_pair, 0, key_width), (dp_pair, 1, key_width), dp_value, dp_gate, dp_small],
-        weights1[:4] + (w_small.T,), True, 5, (gathered1, dp_pair),
-    )
-    d_normed1, out_other = together(d_normed1, out_other)
-    out_keep = turned_product(resid_full, gated, left_half=0, other=out_other)
+        weights1[:4] + (w_small.T,), True, 5, (gathered1, dp_value, dp_pair),
+    )
+    out_keep = turned_product(resid_full, gated, left_half=0)
+    d_normed1, out_keep, out_other, down_other = together(d_normed1, out_keep, out_other, down_other)
+    grad_down = down_keep.astype(jnp.float32) + down_other.astype(jnp.float32)
     grad_small = in_order(product_tn(dp_small, gathered1))
     d_tokens_part, grad_norm1 = norm_back(scaled1, inverse1, norm1_gain, d_normed1)
     tokens_grad = (d_resid.astype(jnp.float32) + d_tokens_part).astype(jnp.bfloat16)
@@ -1476,16 +1537,17 @@
         grad_out, grad_gate_out, grad_value, grad_query, grad_key,
         dc_query, dc_key, dc_value, ddecay, thin, grad_norm1, grad_norm2, dgain, mixed,
     ) = reduce_groups(
-        [out_keep], [grad_gate_out, grad_value, grad_pair],
+        [out_keep], [out_other], [grad_gate_out, grad_value, grad_pair],
         [
             [(0, value_width, turn)],
             [(0, value_width, False)],
             [(0, value_width, False)],
             [(0, key_width, False), (key_width, key_width, False)],
         ],
-        small, partial, resid, 6,
-    )
-    each = width // lax.axis_size("dp")
+        small, hidden, w_down, resid, 6,
+    )
+    mixed, grad_up = together(mixed, grad_up)
+    grad_up, grad_gate = grad_up.astype(jnp.float32), grad_gate.astype(jnp.float32)
     grad_small = lax.dynamic_slice_in_dim(thin, lax.axis_index("dp") * each, each, 1).T
     return (
         mixed,

time: 626 us -> 601 us (0.960); the launches traced: 616 us -> 599 us
  Pallas kernels: 498 us -> 485 us
  waiting for transfers between devices: 35.6 us -> 26.8 us
    pallas_call x4 -> x2, Pallas kernels: 30 us -> 13 us  [turned_product(): pl.pallas_call(lambda *refs: turned_kernel(len(more), *refs), name='turne...]
    reduce_scatter x2 -> x3, waiting for transfers between devices: 6.83 us -> 0.02 us  [scatter_far(): lax.psum_scatter(total, 'dp', scatter_dimension=1, axis_index_groups=alik...]
    ppermute x6 -> x7, waiting for transfers between devices: 28.7 us -> 26.7 us  [flip(): lax.ppermute(array, axis, [(place, place ^ bit) for place in range(size)])]
    unnamed x68 -> x70, local copies, waits for them, and re-layouts: 13.7 us -> 13 us
  transfers between devices with their start and end apart: 9 -> 10, of which waited for: 3 -> 2; matrix products, arithmetic and copies ran while one was open for 4% -> 5% of each run, Pallas kernels for 68% -> 68%
where the time goes in v4:
time: 601 us; the launch traced here: 599 us
  Pallas kernels  485 us (81%)
  other arithmetic  31.4 us (5%)
  waiting for transfers between devices  26.8 us (4%)
  local copies, waits for them, and re-layouts  18.9 us (3%)
  matrix products  16 us (3%)
  between operations  15.6 us (3%)
    pallas_call x1, Pallas kernels, reduce_groups(): pl.pallas_call(lambda *refs: reduce_kernel(groups, early, shapes, *refs),...  160 us
    pallas_call x3, Pallas kernels, gather_call(): pl.pallas_call(body, name=name, grid=() if grid is None else (grid,), in_...  118 us
    pallas_call x3, Pallas kernels, scatter_products(): pl.pallas_call(lambda *refs: scatter_kernel(turned, len(lefts), max(len(f...  102 us
    pallas_call x1, Pallas kernels, mixer_backward(): pl.pallas_call(lambda *refs: mixer_backward_kernel(pieces, *refs), grid_s...  52.1 us
    pallas_call x1, Pallas kernels, mixer_forward(): pl.pallas_call(mixer_forward_kernel, grid_spec=pltpu.PrefetchScalarGridSp...  40.1 us
    ppermute x7, waiting for transfers between devices, flip(): lax.ppermute(array, axis, [(place, place ^ bit) for place in range(size)])  26.7 us
    dot_general x3, matrix products, product_tn(): lax.dot_general(left, right, (((0,), (0,)), ((), ())), preferred_element_...  16 us
    pallas_call x2, Pallas kernels, turned_product(): pl.pallas_call(lambda *refs: turned_kernel(len(more), *refs), name='turne...  13 us
  transfers between devices with their start and end apart: 10, of which 2 were waited for; matrix products, arithmetic and copies ran while one was open for 5% of the time, Pallas kernels for 68%

profile of v4, /device:TPU:0, one launch (start us, length us, event | category | flops | bytes accessed | tf_op | source)
XLA Modules:
  0.0 598.8 jit_solution(14288220578072921071)
XLA Ops:
  7.2 0.0 reduce-scatter.4.cloned.1.call-start
  7.2 1.5 fusion.11
  8.8 1.4 pad_maximum_fusion.refs_4_
  10.1 2.5 fusion.4.own_ref
  12.6 39.3 %project.1 = (bf16[1024,512]{1,0:T(8,128)(2,1)}, bf16[1024,512]{1,0:T(8,128)(2,1)}, bf16[1024,1024]{1,0:T(8,128)(2,1)}, bf16[1024,1024]{1,0:T(8,128)(2,1)}, f32[...) custom-call(bf16[256,2048]{1,0:T(8,128)(2,1)} %fusion.4.own_ref, bf16[2048,512]{1,0:T(8,128)(2,1)} %refs_5_.1, ...), custom_call_target="tpu_custom_call" | custom-call | flops 1 | bytes 1 | tf_op jit(solution)/shard_map/project/pallas_call | solution.py:681
  51.9 0.2 collective-permute-start
  52.1 1.3 collective-permute-start.1
  54.7 0.6 pad_add_fusion.scal.refs_0_
  55.3 40.1 %mixer_forward.1 = (bf16[1024,1024]{1,0:T(8,128)(2,1)}, f32[4,128,256]{2,1,0:T(8,128)}, bf16[1024,1024]{1,0:T(8,128)(2,1)}, bf16[1024,1024]{1,0:T(8,128)(2,1)}, ...) custom-call(s32[2]{0:T(128)} %pad_add_fusion.scal.refs_0_, ...), custom_call_target="tpu_custom_call" | custom-call | flops 1 | bytes 1 | tf_op jit(solution)/shard_map/mixer_forward/pallas_call | solution.py:226
  95.4 0.1 collective-permute-start.2
  95.5 30.9 %scatter_products.3 = f32[256,2048]{1,0:T(8,128)} custom-call(bf16[1024,1024]{1,0:T(8,128)(2,1)} %get-tuple-element.112.refs_0_.refs_20_.refs_1_, bf16[1024,2048]{1,0:T(8,128)(2,1)} %refs_1_.5), custom_call_target="tpu_custom_call" | custom-call | flops 1 | bytes 1 | tf_op jit(solution)/shard_map/scatter_products/pallas_call | solution.py:1043
  126.4 2.0 multiply_reduce_fusion.2
  128.4 1.4 multiply_convert_fusion.own_ref
  129.8 1.0 copy-done.16
  130.8 40.6 %feed.1 = (bf16[1024,1376]{1,0:T(8,128)(2,1)}, bf16[1024,1376]{1,0:T(8,128)(2,1)}, bf16[1024,1376]{1,0:T(8,128)(2,1)}, bf16[1024,2048]{1,0:T(8,128)(2,1)}, bf16[1024,2048]{1,0:T(8,128)(2,1)}) custom-call(bf16[256,2048]{1,0:T(8,128)(2,1)} %multiply_convert_fusion.own_ref, bf16[256,2048]{1,0:T(8,128)(2,1)} %refs_0_.2, ...), custom_call_target="tpu_custom_call" | custom-call | flops 1 | bytes 1 | tf_op jit(solution)/shard_map/feed/pallas_call | solution.py:681
  171.4 7.3 %convolution_convert_fusion.1 = bf16[1376,1024]{1,0:T(8,128)(2,1)} fusion(bf16[1024,1376]{1,0:T(8,128)(2,1)} %get-tuple-element.120.refs_1_.refs_0_, bf16[1024,2048]{1,0:T(8,128)(2,1)} %get-tuple-element.118.refs_6_.refs_1_.refs_22_), kind=kOutput, calls=%fused_computation.4 | convolution fusion | flops 2887090176 | bytes 7798784 | tf_op jit(solution)/shard_map/dot_general | solution.py:511
  178.7 8.0 %convolution_convert_fusion = bf16[1376,2048]{1,0:T(8,128)(2,1)} fusion(bf16[1024,1376]{1,0:T(8,128)(2,1)S(1)} %copy-done.7, bf16[1024,2048]{1,0:T(8,128)(2,1)S(1)} %copy-done.28), kind=kOutput, calls=%fused_computation.2 | convolution fusion | flops 5774180352 | bytes 12648448 | tf_op jit(solution)/shard_map/dot_general | solution.py:511
  186.8 0.0 reduce-scatter.6.cloned.1.call-start
  186.8 1.6 collective-permute-start.3
  188.4 34.2 %scatter_products.4 = f32[256,2048]{1,0:T(8,128)} custom-call(bf16[1024,1376]{1,0:T(8,128)(2,1)} %get-tuple-element.119.refs_0_.refs_5_.refs_21_, bf16[1024,1376]{1,0:T(8,128)(2,1)} %get-tuple-element.120.refs_1_.refs_0_, bf16[1376,2048]{1,0:T(8,128)(2,1)} %bitcast.42, bf16[1376,2048]{1,0:T(8,128)(2,1)} %bitcast.44), custom_call_target="tpu_custom_call" | custom-call | flops 1 | bytes 1 | tf_op jit(solution)/shard_map/scatter_products/pallas_call | solution.py:1043
  222.6 2.9 multiply_reduce_fusion
  225.5 2.9 add_convert_fusion.1.own_ref
  228.4 37.9 %gate_back.1 = (bf16[1024,1024]{1,0:T(8,128)(2,1)}, bf16[1024,1024]{1,0:T(8,128)(2,1)}, f32[1,256]{1,0:T(1,128)}, bf16[1376,1024]{1,0:T(8,128)(2,1)}, bf16[1024,2048]{1,0:T(8,128)(2,1)}) custom-call(bf16[256,2048]{1,0:T(8,128)(2,1)} %add_convert_fusion.1.own_ref, s32[1]{0:T(128)S(6)} %add.79.refs_0_, bf16[1024,2048]{1,0:T(8,128)(2,1)} %refs_1_.5, ...), custom_call_target="tpu_custom_call" | custom-call | flops 1 | bytes 1 | tf_op jit(solution)/shard_map/gate_back/pallas_call | solution.py:681
  266.3 1.6 copy-done.8
  267.9 7.5 %turned_product.2 = bf16[1376,1024]{1,0:T(8,128)(2,1)} custom-call(bf16[1024,1376]{1,0:T(8,128)(2,1)} %get-tuple-element.120.refs_1_.refs_0_, bf16[1024,2048]{1,0:T(8,128)(2,1)} %get-tuple-element.118.refs_6_.refs_1_.refs_22_, bf16[1376,1024]{1,0:T(8,128)(2,1)} %copy-done.8), custom_call_target="tpu_custom_call" | custom-call | flops 1 | bytes 1 | tf_op jit(solution)/shard_map/turned_product/pallas_call | solution.py:1081
  275.3 0.0 reduce-scatter.8.cloned.1.call-start
  275.4 0.4 collective-permute-start.4
  275.8 52.1 %mixer_backward.1 = (bf16[1024,1024]{1,0:T(8,128)(2,1)}, bf16[1024,1024]{1,0:T(8,128)(2,1)}, bf16[1024,8]{1,0:T(8,128)(2,1)}, f32[4,512]{1,0:T(4,128)}, f32[4,51...) custom-call(s32[2]{0:T(128)} %pad_add_fusion.scal.refs_0_, ...), custom_call_target="tpu_custom_call" | custom-call | flops 1 | bytes 1 | tf_op jit(solution)/shard_map/mixer_backward/pallas_call | solution.py:462
  327.9 11.8 %collective-permute-done.4 = bf16[1376,1024]{1,0:T(8,128)(2,1)} collective-permute-done((bf16[1376,1024]{1,0:T(8,128)(2,1)}, bf16[1376,1024]{1,0:T(8,128)(2,1)}, u32[]{:S(2)}, u32[]{:S(2)}) %collective-permute-start.4) | collective-permute-done | bytes 2818080 | tf_op jit(solution)/shard_map/ppermute | solution.py:1418
  339.7 5.6 add_convert_fusion
  345.3 1.3 copy-done.9
  346.6 0.9 constant_dynamic-slice_fusion
  347.5 0.3 collective-permute-start.5
  347.9 1.0 copy.51
  348.9 0.6 gather_fusion
  349.6 0.1 broadcast_in_dim.44
  349.7 5.6 turned_product.3.refs_0_
  355.3 1.7 collective-permute-start.6
  357.0 36.8 %scatter_products.5 = (f32[256,2048]{1,0:T(8,128)}, bf16[2048,1024]{1,0:T(8,128)(2,1)}, bf16[2048,1024]{1,0:T(8,128)(2,1)}) custom-call(bf16[1024,1024]{1,0:T(8,128)(2,1)} %get-tuple-element.149.refs_0_.refs_1_.refs_12_, bf16[1024,1024]{1,0:T(8,128)(2,1)} %get-tuple-element.149.refs_0_.refs_1_.refs_12_, ...), custom_call_target="tpu_custom_call" | custom-call | flops 1 | bytes 1 | tf_op jit(solution)/shard_map/scatter_products/pallas_call | solution.py:1043
  393.8 0.7 fusion.16
  394.5 0.6 gather_fusion.1
  395.1 0.6 broadcast_select_fusion.refs_9_
  395.7 14.9 %collective-permute-done.6 = bf16[1376,256]{1,0:T(8,128)(2,1)} collective-permute-done((bf16[1376,256]{1,0:T(8,128)(2,1)}, bf16[1376,256]{1,0:T(8,128)(2,1)}, u32[]{:S(2)}, u32[]{:S(2)}) %collective-permute-start.6) | collective-permute-done | bytes 704544 | tf_op jit(solution)/shard_map/ppermute | solution.py:1418
  410.6 1.2 fusion.6
  411.8 159.6 %reduce_groups.1 = (f32[1024,256]{1,0:T(8,128)}, f32[256,1024]{1,0:T(8,128)}, f32[256,1024]{1,0:T(8,128)}, f32[256,512]{1,0:T(8,128)}, f32[256,512]{1,0:T(8,128)...) custom-call(bf16[1024,1024]{1,0:T(8,128)(2,1)} %turned_product.3.ref, ...), custom_call_target="tpu_custom_call" | custom-call | flops 1 | bytes 1 | tf_op jit(solution)/shard_map/reduce_groups/pallas_call | solution.py:1368
  571.4 0.8 dynamic-slice_bitcast_fusion
  572.2 1.3 slice_bitcast_fusion
  573.5 0.6 fusion.15
  574.1 2.4 convert_bitcast_fusion
  576.5 2.3 convert_add_fusion.1
  578.8 1.7 fusion.10
  580.5 2.4 convert_bitcast_fusion.1
  583.0 1.0 copy.66
  583.9 0.6 copy.67
  584.5 0.8 copy.68
  585.3 0.8 copy.69
  586.2 1.0 copy.70
  587.1 1.0 copy.71
  588.1 0.6 copy.72
  588.7 0.6 copy.73
  589.3 0.6 copy.74
  589.9 0.6 copy.75
  590.5 1.0 copy.76
  591.5 0.6 copy.77
  (76 shorter events, 0.3 us)
Async XLA Ops:
  7.2 332.5 %reduce-scatter.4.cloned.1.call-start = ((), (), s32[]{:S(2)}) async-start(), calls=%async_computation.3 | async-start | bytes 7045120 | tf_op jit(solution)/shard_map/reduce_scatter | solution.py:1431
  51.9 43.5 %collective-permute-start = (bf16[256,2048]{1,0:T(8,128)(2,1)}, bf16[256,2048]{1,0:T(8,128)(2,1)}, u32[]{:S(2)}, u32[]{:S(2)}) collective-permute-start(bf16[256,2048]{1,0:T(8,128)(2,1)} %refs_0_.2), channel_id=1, source_target_pairs={{0,2},{1,3},{2,0},{3,1},{4,6},{5,7},{6,4},{7,5},{8,10},{9,11},{10,... | collective-permute-start | bytes 3145736 | tf_op jit(solution)/shard_map/ppermute | solution.py:1418
  52.1 77.7 %collective-permute-start.1 = (bf16[256,2048]{1,0:T(8,128)(2,1)}, bf16[256,2048]{1,0:T(8,128)(2,1)}, u32[]{:S(2)}, u32[]{:S(2)}) collective-permute-start(bf16[256,2048]{1,0:T(8,128)(2,1)} %refs_0_.2), channel_id=1, source_target_pairs={{0,1},{1,0},{2,3},{3,2},{4,5},{5,4},{6,7},{7,6},{8,9},{9,8},{10,11... | collective-permute-start | bytes 3145736 | tf_op jit(solution)/shard_map/ppermute | solution.py:1418
  95.4 31.0 %copy-start.3 = (bf16[256,2048]{1,0:T(8,128)(2,1)S(1)}, bf16[256,2048]{1,0:T(8,128)(2,1)}, u32[]{:S(2)}) copy-start(bf16[256,2048]{1,0:T(8,128)(2,1)} %param.24) | copy-start | bytes 3145732
  95.4 34.4 %collective-permute-start.2 = (bf16[256,2048]{1,0:T(8,128)(2,1)}, bf16[256,2048]{1,0:T(8,128)(2,1)S(1)}, u32[]{:S(2)}, u32[]{:S(2)}) collective-permute-start(bf16[256,2048]{1,0:T(8,128)(2,1)} %collective-permute-done.refs_2_), channel_id=1, source_target_pairs={{0,1},{1,0},{2,3},{3,2},{4,5},{5,4},{6,7},{7,6},{8,9},{9,8},{10,11... | collective-permute-start | bytes 3145736 | tf_op jit(solution)/shard_map/ppermute | solution.py:1418
  126.4 2.0 copy-start.20
  128.4 97.1 %copy-start.1 = (f32[256,2048]{1,0:T(8,128)}, f32[256,2048]{1,0:T(8,128)S(1)}, u32[]{:S(2)}) copy-start(f32[256,2048]{1,0:T(8,128)S(1)} %get-tuple-element.194.refs_15_) | copy-start | bytes 6291460
  129.8 1.0 copy-start.16
  171.4 7.4 %copy-start.7 = (bf16[1024,1376]{1,0:T(8,128)(2,1)S(1)}, bf16[1024,1376]{1,0:T(8,128)(2,1)}, u32[]{:S(2)}) copy-start(bf16[1024,1376]{1,0:T(8,128)(2,1)} %get-tuple-element.116.refs_13_) | copy-start | bytes 8454148
  171.4 7.4 %copy-start.28 = (bf16[1024,2048]{1,0:T(8,128)(2,1)S(1)}, bf16[1024,2048]{1,0:T(8,128)(2,1)}, u32[]{:S(2)}) copy-start(bf16[1024,2048]{1,0:T(8,128)(2,1)} %get-tuple-element.117) | copy-start | bytes 12582916
  186.8 384.6 %reduce-scatter.6.cloned.1.call-start = ((), (), s32[]{:S(2)}) async-start(), calls=%async_computation.4 | async-start | bytes 3522560 | tf_op jit(solution)/shard_map/reduce_scatter | solution.py:1431
  186.8 79.4 %collective-permute-start.3 = (bf16[1376,1024]{1,0:T(8,128)(2,1)}, bf16[1376,1024]{1,0:T(8,128)(2,1)S(1)}, u32[]{:S(2)}, u32[]{:S(2)}) collective-permute-start(bf16[1376,1024]{1,0:T(8,128)(2,1)} %convolution_convert_fusion.1), channel_id=1, source_target_pairs={{0,4},{4,0},{8,12},{12,8},{16,20},{20,16},{24,28},{28,24},{1,5},{5... | collective-permute-start | bytes 8454152 | tf_op jit(solution)/shard_map/ppermute | solution.py:1418
  222.6 2.9 copy-start.4
  266.3 1.6 copy-start.8
  275.3 305.2 %reduce-scatter.8.cloned.1.call-start = ((), (), s32[]{:S(2)}) async-start(), calls=%async_computation.5 | async-start | bytes 3522560 | tf_op jit(solution)/shard_map/reduce_scatter | solution.py:1431
  275.4 64.3 %collective-permute-start.4 = (bf16[1376,1024]{1,0:T(8,128)(2,1)}, bf16[1376,1024]{1,0:T(8,128)(2,1)}, u32[]{:S(2)}, u32[]{:S(2)}) collective-permute-start(bf16[1376,1024]{1,0:T(8,128)(2,1)} %get-tuple-element.148), channel_id=1, source_target_pairs={{0,4},{4,0},{8,12},{12,8},{16,20},{20,16},{24,28},{28,24},{1,5},{5... | collective-permute-start | bytes 8454152 | tf_op jit(solution)/shard_map/ppermute | solution.py:1418
  345.3 1.4 copy-start.9
  345.3 2.6 copy-start.19
  345.3 3.6 copy-start
  347.5 63.0 %collective-permute-start.5 = (bf16[1024,1024]{1,0:T(8,128)(2,1)}, bf16[1024,1024]{1,0:T(8,128)(2,1)}, u32[]{:S(2)}, u32[]{:S(2)}) collective-permute-start(bf16[1024,1024]{1,0:T(8,128)(2,1)} %get-tuple-element.155), channel_id=1, source_target_pairs={{0,4},{4,0},{8,12},{12,8},{16,20},{20,16},{24,28},{28,24},{1,5},{5... | collective-permute-start | bytes 6291464 | tf_op jit(solution)/shard_map/ppermute | solution.py:1418
  355.3 55.3 %collective-permute-start.6 = (bf16[1376,256]{1,0:T(8,128)(2,1)}, bf16[1376,256]{1,0:T(8,128)(2,1)}, u32[]{:S(2)}, u32[]{:S(2)}) collective-permute-start(bf16[1376,256]{1,0:T(8,128)(2,1)} %constant_dynamic-slice_fusion), channel_id=1, source_target_pairs={{0,4},{4,0},{8,12},{12,8},{16,20},{20,16},{24,28},{28,24},{1,5},{5... | collective-permute-start | bytes 2113544 | tf_op jit(solution)/shard_map/ppermute | solution.py:1418
  357.0 36.8 %copy-start.2 = (bf16[1024,2048]{1,0:T(8,128)(2,1)S(1)}, bf16[1024,2048]{1,0:T(8,128)(2,1)}, u32[]{:S(2)}) copy-start(bf16[1024,2048]{1,0:T(8,128)(2,1)} %get-tuple-element.134.refs_17_.refs_10_) | copy-start | bytes 12582916
  357.0 36.8 %copy-start.11 = (bf16[1024,8]{1,0:T(8,128)(2,1)S(1)}, bf16[1024,8]{1,0:T(8,128)(2,1)}, u32[]{:S(2)}) copy-start(bf16[1024,8]{1,0:T(8,128)(2,1)} %get-tuple-element.151.refs_4_) | copy-start | bytes 49156
  393.8 16.8 %copy-start.6 = (f32[256,2048]{1,0:T(8,128)S(1)}, f32[256,2048]{1,0:T(8,128)}, u32[]{:S(2)}) copy-start(f32[256,2048]{1,0:T(8,128)} %get-tuple-element.166) | copy-start | bytes 6291460
  393.8 16.8 %copy-start.21 = (f32[2048]{0:T(1024)S(1)}, f32[2048]{0:T(1024)}, u32[]{:S(2)}) copy-start(f32[2048]{0:T(1024)} %param.25) | copy-start | bytes 24580
  571.4 5.1 copy-start.10
  574.1 4.7 copy-start.5
  580.5 2.4 copy-start.15
  580.5 3.4 copy-start.26
  580.5 4.0 copy-start.18
  583.0 2.4 copy-start.17
  583.0 3.2 copy-start.14
  584.5 2.6 copy-start.13
  586.1 2.0 copy-start.25
  586.1 2.6 copy-start.24
  586.1 3.2 copy-start.22
  586.1 3.8 copy-start.27
  586.2 4.3 copy-start.12
  587.1 4.3 copy-start.23
Sparse Core Ops, SparseCore 0:
  186.9 101.9 reduce-scatter.3
  291.2 55.6 reduce-scatter.5
  349.4 54.9 reduce-scatter.7

commit v5 on v4

--- a/solution.py
+++ b/solution.py
@@ -258,8 +258,8 @@
 
 def mixer_backward_kernel(
     pieces, scal, pq, pk, pv, pq16, pk16, pv16, small, do_in, delta_in, s_in, tt_in,
-    cq, ck, cv, dlog_in, dbias_in, left_one, right_one, left_two, right_two, left_three, right_three,
-    dpqk, dpv, dsmall, dcq, dck, dcv, ddecay, product_one, product_two, product_three,
+    cq, ck, cv, dlog_in, dbias_in, left_one, right_one, left_two, right_two, left_three, right_three, left_four,
+    dpqk, dpv, dsmall, dcq, dck, dcv, ddecay, product_one, product_two, product_three, product_four,
     dstate, nq, nk, nv,
 ):
     step = pl.program_id(0)
@@ -274,6 +274,7 @@
 
     product_one[...] = mm_tn(left_one[...], right_one[...]).astype(bf16)
     product_two[...] = mm_tn(left_two[...], right_two[...]).astype(bf16)
+    product_four[...] = mm_tn(left_four[...], right_two[...]).astype(bf16)
 
     @pl.when(step < pieces)
     def _():
@@ -473,6 +474,7 @@
                 pl.BlockSpec((rows, each_one), lambda c, s: (0, c)), whole(*right_one.shape),
                 pl.BlockSpec((rows, each_two), lambda c, s: (0, chunks + c)), whole(*right_two.shape),
                 pl.BlockSpec((rows, piece), lambda c, s: (0, at_piece(c))), whole(rows, width // 2),
+                pl.BlockSpec((rows, each_two), lambda c, s: (0, c)),
             ],
             out_specs=[
                 by_rows(2 * kw), by_rows(vw), by_rows(2 * heads),
@@ -480,6 +482,7 @@
                 pl.BlockSpec((each_one, right_one.shape[1]), lambda c, s: (c, 0)),
                 pl.BlockSpec((each_two, right_two.shape[1]), lambda c, s: (c, 0)),
                 pl.BlockSpec((piece, width // 2), lambda c, s: (at_piece(c), 0)),
+                pl.BlockSpec((each_two, right_two.shape[1]), lambda c, s: (c, 0)),
             ],
             scratch_shapes=[
                 pltpu.VMEM((heads, dk, dv), f32),
@@ -497,13 +500,14 @@
             jax.ShapeDtypeStruct((width, right_one.shape[1]), bf16),
             jax.ShapeDtypeStruct((width // 2, right_two.shape[1]), bf16),
             jax.ShapeDtypeStruct((units, width // 2), bf16),
+            jax.ShapeDtypeStruct((width // 2, right_two.shape[1]), bf16),
         ],
         compiler_params=pltpu.CompilerParams(vmem_limit_bytes=56 * 1024 * 1024),
         cost_estimate=LITTLE,
         name="mixer_backward",
     )(
         scal, pq, pk, pv, pq, pk, pv, small, do, delta, s, tt, cq, ck, cv, dlog, dbias,
-        left_one, right_one, left_two, right_two, left_three, right_three,
+        left_one, right_one, left_two, right_two, left_three, right_three, left_two,
     )
 
 
@@ -532,6 +536,7 @@
 
 VMEM_MOST = 56 * 1024 * 1024
 COLUMNS = 512
+FIRST = 128
 MESH = pl.DeviceIdType.MESH
 
 
@@ -851,7 +856,7 @@
     )
 
 
-def gate_back_kernel(heads, step, gather, length, w, pg, o_in, gain, left, right, dpg, do, dgain, leave):
+def gate_back_kernel(heads, step, gather, length, w, pg, o_in, gain, left, right, dpg, do, dgain, leave_one, leave_two):
     pair = 2 * gather.own.shape[0]
     each = pair // 2
     dv = gain.shape[1]
@@ -882,10 +887,12 @@
 
     @pl.when(step == 1)
     def _():
-        units = leave.shape[0]
+        units, first = leave_one.shape
         for start in range(0, units, COLUMNS):
             where = slice(start, min(start + COLUMNS, units))
-            leave[where, :] = mm_tn(left[:, where], right[...]).astype(bf16)
+            product = mm_tn(left[:, where], right[...]).astype(bf16)
+            leave_one[where, :] = product[:, :first]
+            leave_two[where, :] = product[:, first:]
 
 
 def gate_back(own, length, w_out, pg, o, gain, left, right):
@@ -907,22 +914,26 @@
         [
             by_head, by_head,
             pl.BlockSpec((1, dv), lambda j: (0, 0)),
-            pl.BlockSpec((left.shape[1], right.shape[1] // 2), lambda j: (0, 0)),
+            pl.BlockSpec((left.shape[1], FIRST), lambda j: (0, 0)),
+            pl.BlockSpec((left.shape[1], right.shape[1] // 2 - FIRST), lambda j: (0, 0)),
         ],
         [
             jax.ShapeDtypeStruct(pg.shape, bf16),
             jax.ShapeDtypeStruct(pg.shape, bf16),
             jax.ShapeDtypeStruct((1, dv), f32),
-            jax.ShapeDtypeStruct((left.shape[1], right.shape[1] // 2), bf16),
+            jax.ShapeDtypeStruct((left.shape[1], FIRST), bf16),
+            jax.ShapeDtypeStruct((left.shape[1], right.shape[1] // 2 - FIRST), bf16),
         ],
         (30_000_000_000, 30_000_000), "flip", grid=4,
     )
 
 
-def scatter_kernel(turned, count, filled, *refs):
+def scatter_kernel(turned, count, filled, after, *refs):
     lefts, rights, refs = refs[:count], refs[count : 2 * count], refs[2 * count :]
+    extra_in, refs = refs[: after[1]], refs[after[1] :]
     sources, refs = refs[: filled + 1 if filled else 0], refs[filled + 1 if filled else 0 :]
     out, fills, refs = refs[0], refs[1 : 1 + filled], refs[1 + filled :]
+    extra_out, refs = refs[: after[2]], refs[after[2] :]
     far_own, leave, other, send_sem, recv_sem, fill_sem = refs[:6]
     held = refs[6:]
     loads = [pltpu.make_async_copy(source, kept, fill_sem.at[at]) for at, (source, kept) in enumerate(zip(sources, held))]
@@ -1013,9 +1024,29 @@
             return carry
 
         lax.fori_loop(0, parts, finish, 0)
-
-
-def scatter_products(lefts, rights, turned, collective, fill=None):
+        if after[0] is not None:
+            after[0](out, *extra_in, *extra_out)
+
+
+def norm_after(out, tokens, gain, resid, normed):
+    rows = tokens[...].astype(f32) + out[...]
+    resid[...] = rows
+    inverse = lax.rsqrt(jnp.mean(rows * rows, axis=-1, keepdims=True) + 1e-05)
+    normed[...] = (rows * inverse * gain[...]).astype(bf16)
+
+
+def norm_back_after(out, resid, gain, upstream, d_resid, d_gain):
+    rows = resid[...]
+    inverse = lax.rsqrt(jnp.mean(rows * rows, axis=-1, keepdims=True) + 1e-05)
+    scaled = rows * inverse
+    through = out[...]
+    d_gain[...] = jnp.sum(through * scaled, axis=0, keepdims=True)
+    along = through * gain[...]
+    inner = jnp.mean(along * scaled, axis=-1, keepdims=True)
+    d_resid[...] = (upstream[...].astype(f32) + inverse * (along - scaled * inner)).astype(bf16)
+
+
+def scatter_products(lefts, rights, turned, collective, fill=None, after=None, given=(), made_after=()):
     lefts = [left if isinstance(left, tuple) else (left, 0, left.shape[1]) for left in lefts]
     rows = lefts[0][0].shape[0] // 4
     width = rights[0].shape[0 if turned else 1]
@@ -1035,13 +1066,17 @@
     out_specs = [pl.BlockSpec((rows, width), lambda j: (0, 0))]
     out_shape = [jax.ShapeDtypeStruct((rows, width), f32)]
     fill = list(fill or ())
+    in_specs += [pl.BlockSpec(part.shape, lambda j: (0, 0)) for part in given]
     in_specs += [pl.BlockSpec(memory_space=pl.ANY)] * len(fill)
     for part in fill[1:]:
         made = (fill[0].shape[1], part.shape[1])
         out_specs.append(pl.BlockSpec(made, lambda j: (0, 0)))
         out_shape.append(jax.ShapeDtypeStruct(made, bf16))
+    out_specs += [pl.BlockSpec(part.shape, lambda j: (0, 0)) for part in made_after]
+    out_shape += list(made_after)
+    follow = (after, len(given), len(made_after))
     outs = pl.pallas_call(
-        lambda *refs: scatter_kernel(turned, len(lefts), max(len(fill) - 1, 0), *refs),
+        lambda *refs: scatter_kernel(turned, len(lefts), max(len(fill) - 1, 0), follow, *refs),
         name="scatter_products",
         grid=(2 * parts,),
         in_specs=in_specs,
@@ -1060,8 +1095,8 @@
             vmem_limit_bytes=VMEM_MOST, collective_id=collective, has_side_effects=True
         ),
         cost_estimate=LITTLE,
-    )(*[left[0] for left in lefts], *rights, *fill)
-    return outs if fill else outs[0]
+    )(*[left[0] for left in lefts], *rights, *given, *fill)
+    return outs if fill or made_after else outs[0]
 
 
 def turned_kernel(added, left, right, *refs):
@@ -1476,9 +1511,12 @@
     )
     gated, e_across = together(gated, e_across)
     e_corner = flip(e_across, "tensor", 1)
-    resid = rows_in + scatter_products([gated], [w_out], False, 3)
-    scaled2, inverse2 = row_stats(resid)
-    normed2 = (scaled2 * norm2_gain).astype(jnp.bfloat16)
+    own_rows = jax.ShapeDtypeStruct(tokens.shape, jnp.float32)
+    own_low = jax.ShapeDtypeStruct(tokens.shape, jnp.bfloat16)
+    gain_line = jax.ShapeDtypeStruct((1, width), jnp.float32)
+    _, resid, normed2 = scatter_products(
+        [gated], [w_out], False, 3, None, norm_after, [tokens, norm2_gain[None]], [own_rows, own_low]
+    )
     hidden, d_gate, d_up, cot_full, split2 = feed(
         normed2, (cotangent, e_beside, e_across, e_corner), w_gate.T, w_up.T, w_down
     )
@@ -1488,28 +1526,31 @@
     d_gate, d_up, grad_down, up_other = together(d_gate, d_up, grad_down, up_other)
     grad_down = scatter_far(grad_down)
     up_other = flip(up_other, "dp", 1)
-    d_normed2 = scatter_products([d_gate, d_up], [w_gate.T, w_up.T], False, 4)
-    d_resid_part, grad_norm2 = norm_back(scaled2, inverse2, norm2_gain, d_normed2)
-    d_resid = (cotangent.astype(jnp.float32) + d_resid_part).astype(jnp.bfloat16)
-    dp_gate, do, dgain, gate_other, resid_full = gate_back(
+    _, d_resid, grad_norm2 = scatter_products(
+        [d_gate, d_up], [w_gate.T, w_up.T], False, 4, None,
+        norm_back_after, [resid, norm2_gain[None], cotangent], [own_low, gain_line],
+    )
+    dp_gate, do, dgain, gate_one, gate_two, resid_full = gate_back(
         d_resid, seq_length, w_out, p_gate, mixer_out, gain_row, d_gate, split2
     )
-    do, dp_gate, dgain, resid_full, gate_other, up_other = together(
-        do, dp_gate, dgain, resid_full, gate_other, up_other
-    )
-    gate_other = flip(gate_other, "dp", 1)
+    do, dp_gate, dgain, resid_full, gate_one, gate_two, up_other = together(
+        do, dp_gate, dgain, resid_full, gate_one, gate_two, up_other
+    )
+    gate_one = flip(gate_one, "dp", 1)
     up_kept = turned_product(d_up, split2, right_half=0, other=up_other)
-    do, up_kept = together(do, up_kept)
+    do, up_kept, gate_one, gate_two = together(do, up_kept, gate_one, gate_two)
     grad_up = scatter_far(up_kept)
+    gate_two = flip(gate_two, "dp", 1)
     mixer_grads = mixer_backward(
         scal, p_query, p_key, p_value, p_small, do, delta, states, inverse_t,
         conv_query, conv_key, conv_value, log_row, bias_row, (gathered1, dp_gate), (resid_full, gated),
         (d_gate, split2),
     )
     (
-        dp_pair, dp_value, dp_small, dc_query, dc_key, dc_value, ddecay, grad_gate_out, out_other, gate_kept,
-        grad_down, gate_other,
-    ) = together(*mixer_grads, grad_down, gate_other)
+        dp_pair, dp_value, dp_small, dc_query, dc_key, dc_value, ddecay, grad_gate_out, out_other, gate_kept, out_keep,
+        grad_down, gate_two,
+    ) = together(*mixer_grads, grad_down, gate_two)
+    gate_other = jnp.concatenate([gate_one, gate_two], axis=1)
     each = width // lax.axis_size("dp")
     bit = lax.axis_index("dp") % 2
     down_keep = lax.dynamic_slice_in_dim(grad_down, bit * each, each, 1)
@@ -1523,8 +1564,7 @@
         [(dp_pair, 0, key_width), (dp_pair, 1, key_width), dp_value, dp_gate, dp_small],
         weights1[:4] + (w_small.T,), True, 5, (gathered1, dp_value, dp_pair),
     )
-    out_keep = turned_product(resid_full, gated, left_half=0)
-    d_normed1, out_keep, out_other, down_other = together(d_normed1, out_keep, out_other, down_other)
+    d_normed1, out_other, down_other = together(d_normed1, out_other, down_other)
     grad_down = down_keep.astype(jnp.float32) + down_other.astype(jnp.float32)
     grad_small = in_order(product_tn(dp_small, gathered1))
     d_tokens_part, grad_norm1 = norm_back(scaled1, inverse1, norm1_gain, d_normed1)
@@ -1532,7 +1572,7 @@
     value_width = w_value.shape[1]
     turn = (width // lax.axis_size("dp")) % 128 == 0
     thin = grad_small.reshape(grad_small.shape[0], width)
-    small = [dc_query, dc_key, dc_value, ddecay, thin, grad_norm1[None], grad_norm2[None], dgain]
+    small = [dc_query, dc_key, dc_value, ddecay, thin, grad_norm1[None], grad_norm2, dgain]
     (
         grad_out, grad_gate_out, grad_value, grad_query, grad_key,
         dc_query, dc_key, dc_value, ddecay, thin, grad_norm1, grad_norm2, dgain, mixed,

time: 601 us -> 580 us (0.965); the launches traced: 599 us -> 571 us
  Pallas kernels: 485 us -> 472 us
  other arithmetic: 31.4 us -> 21 us
    pallas_call x1, Pallas kernels: 40.1 us -> 27.6 us  [mixer_forward(): pl.pallas_call(mixer_forward_kernel, grid_spec=pltpu.PrefetchScalarGridSp...]
    pallas_call x2 -> x1, Pallas kernels: 13 us -> 7.54 us  [turned_product(): pl.pallas_call(lambda *refs: turned_kernel(len(more), *refs), name='turne...]
    ppermute x7 -> x8, waiting for transfers between devices: 26.7 us -> 22.3 us  [flip(): lax.ppermute(array, axis, [(place, place ^ bit) for place in range(size)])]
  transfers between devices with their start and end apart: 10 -> 11, of which waited for: 2 -> 3; matrix products, arithmetic and copies ran while one was open for 5% -> 3% of each run, Pallas kernels for 68% -> 69%
where the time goes in v5:
time: 580 us; the launch traced here: 571 us
  Pallas kernels  472 us (81%)
  waiting for transfers between devices  22.4 us (4%)
  other arithmetic  21 us (4%)
  local copies, waits for them, and re-layouts  18.7 us (3%)
  between operations  15.9 us (3%)
  matrix products  14.3 us (2%)
  starting transfers between devices  6.48 us (1%)
    pallas_call x1, Pallas kernels, reduce_groups(): pl.pallas_call(lambda *refs: reduce_kernel(groups, early, shapes, *refs),...  157 us
    pallas_call x3, Pallas kernels, gather_call(): pl.pallas_call(body, name=name, grid=() if grid is None else (grid,), in_...  118 us
    pallas_call x3, Pallas kernels, scatter_products(): pl.pallas_call(lambda *refs: scatter_kernel(turned, len(lefts), max(len(f...  107 us
    pallas_call x1, Pallas kernels, mixer_backward(): pl.pallas_call(lambda *refs: mixer_backward_kernel(pieces, *refs), grid_s...  54.9 us
    pallas_call x1, Pallas kernels, mixer_forward(): pl.pallas_call(mixer_forward_kernel, grid_spec=pltpu.PrefetchScalarGridSp...  27.6 us
    ppermute x8, waiting for transfers between devices, flip(): lax.ppermute(array, axis, [(place, place ^ bit) for place in range(size)])  22.3 us
    dot_general x3, matrix products, product_tn(): lax.dot_general(left, right, (((0,), (0,)), ((), ())), preferred_element_...  14.3 us
    unnamed x70, local copies, waits for them, and re-layouts  12.7 us
  transfers between devices with their start and end apart: 11, of which 3 were waited for; matrix products, arithmetic and copies ran while one was open for 3% of the time, Pallas kernels for 69%

profile of v5, /device:TPU:0, one launch (start us, length us, event | category | flops | bytes accessed | tf_op | source)
XLA Modules:
  0.0 570.8 jit_solution(12104218296857969693)
XLA Ops:
  7.2 0.0 reduce-scatter.4.cloned.1.call-start
  7.2 1.5 fusion.11
  8.8 1.4 pad_maximum_fusion.refs_4_
  10.1 2.5 fusion.4.own_ref
  12.6 39.3 %project.1 = (bf16[1024,512]{1,0:T(8,128)(2,1)}, bf16[1024,512]{1,0:T(8,128)(2,1)}, bf16[1024,1024]{1,0:T(8,128)(2,1)}, bf16[1024,1024]{1,0:T(8,128)(2,1)}, f32[...) custom-call(bf16[256,2048]{1,0:T(8,128)(2,1)} %fusion.4.own_ref, bf16[2048,512]{1,0:T(8,128)(2,1)} %refs_5_.1, ...), custom_call_target="tpu_custom_call" | custom-call | flops 1 | bytes 1 | tf_op jit(solution)/shard_map/project/pallas_call | solution.py:686
  51.9 0.2 collective-permute-start
  52.1 1.3 collective-permute-start.1
  54.7 0.6 pad_add_fusion.scal.refs_0_
  55.3 27.6 %mixer_forward.1 = (bf16[1024,1024]{1,0:T(8,128)(2,1)}, f32[4,128,256]{2,1,0:T(8,128)}, bf16[1024,1024]{1,0:T(8,128)(2,1)}, bf16[1024,1024]{1,0:T(8,128)(2,1)}, ...) custom-call(s32[2]{0:T(128)} %pad_add_fusion.scal.refs_0_, ...), custom_call_target="tpu_custom_call" | custom-call | flops 1 | bytes 1 | tf_op jit(solution)/shard_map/mixer_forward/pallas_call | solution.py:226
  82.9 0.1 collective-permute-start.2
  83.0 33.3 %scatter_products.3 = (f32[256,2048]{1,0:T(8,128)}, f32[256,2048]{1,0:T(8,128)}, bf16[256,2048]{1,0:T(8,128)(2,1)}) custom-call(bf16[1024,1024]{1,0:T(8,128)(2,1)} %get-tuple-element.121.refs_0_.refs_20_, bf16[1024,2048]{1,0:T(8,128)(2,1)} %refs_1_.5, bf16[256,2048]{1,0:T(8,128)(2,1)} %refs_2_.3, f32[1,2048]{1,0:T(1,128)} %bitcast.50), custom_call_target="tpu_custom_call" | custom-call | flops 1 | bytes 1 | tf_op jit(solution)/shard_map/scatter_products/pallas_call | solution.py:1078
  116.4 0.9 copy-done.16
  117.3 0.3 copy-done.17
  117.7 40.8 %feed.1 = (bf16[1024,1376]{1,0:T(8,128)(2,1)}, bf16[1024,1376]{1,0:T(8,128)(2,1)}, bf16[1024,1376]{1,0:T(8,128)(2,1)}, bf16[1024,2048]{1,0:T(8,128)(2,1)}, bf16[1024,2048]{1,0:T(8,128)(2,1)}) custom-call(bf16[256,2048]{1,0:T(8,128)(2,1)} %get-tuple-element.122.own_ref, bf16[256,2048]{1,0:T(8,128)(2,1)} %refs_6_.3, bf16[256,2048]{1,0:T(8,128)(2,1)} %copy-done.16, ...), custom_call_target="tpu_custom_call" | custom-call | flops 1 | bytes 1 | tf_op jit(solution)/shard_map/feed/pallas_call | solution.py:686
  158.5 5.7 %convolution_convert_fusion.1 = bf16[1376,1024]{1,0:T(8,128)(2,1)S(1)} fusion(bf16[1024,1376]{1,0:T(8,128)(2,1)} %get-tuple-element.130.refs_1_.refs_0_, bf16[1024,2048]{1,0:T(8,128)(2,1)} %get-tuple-element.128.refs_6_.refs_1_.refs_22_), kind=kOutput, calls=%fused_computation.4 | convolution fusion | flops 2887090176 | bytes 7798784 | tf_op jit(solution)/shard_map/dot_general | solution.py:515
  164.2 7.9 %convolution_convert_fusion = bf16[1376,2048]{1,0:T(8,128)(2,1)} fusion(bf16[1024,1376]{1,0:T(8,128)(2,1)S(1)} %copy-done.6, bf16[1024,2048]{1,0:T(8,128)(2,1)S(1)} %copy-done.28), kind=kOutput, calls=%fused_computation.2 | convolution fusion | flops 5774180352 | bytes 12648448 | tf_op jit(solution)/shard_map/dot_general | solution.py:515
  172.1 0.0 reduce-scatter.6.cloned.1.call-start
  172.2 1.6 collective-permute-start.3
  173.7 37.2 %scatter_products.4 = (f32[256,2048]{1,0:T(8,128)}, bf16[256,2048]{1,0:T(8,128)(2,1)}, f32[1,2048]{1,0:T(1,128)}) custom-call(bf16[1024,1376]{1,0:T(8,128)(2,1)} %get-tuple-element.129.refs_0_.refs_5_.refs_21_, bf16[1024,1376]{1,0:T(8,128)(2,1)} %get-tuple-element.130.refs_1_.refs_0_, bf16[1376,2048]{1,0:T(8,128)(2,1)} %bitcast.42, ...), custom_call_target="tpu_custom_call" | custom-call | flops 1 | bytes 1 | tf_op jit(solution)/shard_map/scatter_products/pallas_call | solution.py:1078
  211.0 37.9 %gate_back.1 = (bf16[1024,1024]{1,0:T(8,128)(2,1)}, bf16[1024,1024]{1,0:T(8,128)(2,1)}, f32[1,256]{1,0:T(1,128)}, bf16[1376,128]{1,0:T(8,128)(2,1)}, bf16[1376,8...) custom-call(bf16[256,2048]{1,0:T(8,128)(2,1)} %get-tuple-element.132.own_ref, s32[1]{0:T(128)S(6)} %add.68.refs_0_, ...), custom_call_target="tpu_custom_call" | custom-call | flops 1 | bytes 1 | tf_op jit(solution)/shard_map/gate_back/pallas_call | solution.py:686
  249.0 0.6 collective-permute-start.4
  249.6 1.0 copy-done.7
  250.5 7.5 %turned_product.1 = bf16[1376,1024]{1,0:T(8,128)(2,1)} custom-call(bf16[1024,1376]{1,0:T(8,128)(2,1)} %get-tuple-element.130.refs_1_.refs_0_, bf16[1024,2048]{1,0:T(8,128)(2,1)} %get-tuple-element.128.refs_6_.refs_1_.refs_22_, bf16[1376,1024]{1,0:T(8,128)(2,1)} %copy-done.7), custom_call_target="tpu_custom_call" | custom-call | flops 1 | bytes 1 | tf_op jit(solution)/shard_map/turned_product/pallas_call | solution.py:1116
  258.1 2.2 collective-permute-done.4
  260.3 0.0 reduce-scatter.6.cloned.1.call-update
  260.3 0.0 reduce-scatter.8.cloned.1.call-start
  260.3 0.6 collective-permute-start.5
  260.9 54.9 %mixer_backward.1 = (bf16[1024,1024]{1,0:T(8,128)(2,1)}, bf16[1024,1024]{1,0:T(8,128)(2,1)}, bf16[1024,8]{1,0:T(8,128)(2,1)}, f32[4,512]{1,0:T(4,128)}, f32[4,51...) custom-call(s32[2]{0:T(128)} %pad_add_fusion.scal.refs_0_, ...), custom_call_target="tpu_custom_call" | custom-call | flops 1 | bytes 1 | tf_op jit(solution)/shard_map/mixer_backward/pallas_call | solution.py:463
  315.8 0.4 collective-permute-done.5
  316.2 4.2 add_convert_fusion
  320.5 1.3 copy-done.8
  321.8 0.9 constant_dynamic-slice_fusion
  322.7 1.2 collective-permute-start.6
  323.9 1.0 copy.51
  324.9 0.6 gather_fusion
  325.5 0.1 broadcast_in_dim.42
  325.7 0.9 collective-permute-start.7
  326.6 36.9 %scatter_products.5 = (f32[256,2048]{1,0:T(8,128)}, bf16[2048,1024]{1,0:T(8,128)(2,1)}, bf16[2048,1024]{1,0:T(8,128)(2,1)}) custom-call(bf16[1024,1024]{1,0:T(8,128)(2,1)} %get-tuple-element.167.refs_0_.refs_1_.refs_12_, bf16[1024,1024]{1,0:T(8,128)(2,1)} %get-tuple-element.167.refs_0_.refs_1_.refs_12_, ...), custom_call_target="tpu_custom_call" | custom-call | flops 1 | bytes 1 | tf_op jit(solution)/shard_map/scatter_products/pallas_call | solution.py:1078
  363.6 0.7 fusion.16
  364.2 0.6 gather_fusion.1
  364.8 0.6 broadcast_select_fusion.refs_9_
  365.4 19.7 %collective-permute-done.7 = bf16[1376,256]{1,0:T(8,128)(2,1)} collective-permute-done((bf16[1376,256]{1,0:T(8,128)(2,1)}, bf16[1376,256]{1,0:T(8,128)(2,1)}, u32[]{:S(2)}, u32[]{:S(2)}) %collective-permute-start.7) | collective-permute-done | bytes 704544 | tf_op jit(solution)/shard_map/ppermute | solution.py:1453
  385.2 1.2 fusion.6
  386.4 156.6 %reduce_groups.1 = (f32[1024,256]{1,0:T(8,128)}, f32[256,1024]{1,0:T(8,128)}, f32[256,1024]{1,0:T(8,128)}, f32[256,512]{1,0:T(8,128)}, f32[256,512]{1,0:T(8,128)...) custom-call(bf16[1024,1024]{1,0:T(8,128)(2,1)} %get-tuple-element.16, ...), custom_call_target="tpu_custom_call" | custom-call | flops 1 | bytes 1 | tf_op jit(solution)/shard_map/reduce_groups/pallas_call | solution.py:1403
  543.0 0.0 reduce-scatter.6.cloned.1.call-done
  543.1 0.8 dynamic-slice_bitcast_fusion
  543.9 1.3 slice_bitcast_fusion
  545.2 0.6 fusion.15
  545.8 2.4 convert_bitcast_fusion
  548.2 2.3 convert_add_fusion
  550.6 1.7 fusion.10
  552.3 2.4 convert_bitcast_fusion.1
  554.7 1.0 copy.66
  555.7 0.6 copy.67
  556.3 0.8 copy.68
  557.1 0.8 copy.69
  557.9 1.0 copy.70
  558.9 1.0 copy.71
  559.8 0.6 copy.72
  560.4 0.6 copy.73
  561.1 0.6 copy.74
  561.7 0.6 copy.75
  562.2 1.0 copy.76
  563.2 0.6 copy.77
  (71 shorter events, 0.2 us)
Async XLA Ops:
  7.2 309.0 %reduce-scatter.4.cloned.1.call-start = ((), (), s32[]{:S(2)}) async-start(), calls=%async_computation.3 | async-start | bytes 7045120 | tf_op jit(solution)/shard_map/reduce_scatter | solution.py:1466
  12.6 39.3 %copy-start.5 = (bf16[256,2048]{1,0:T(8,128)(2,1)S(1)}, bf16[256,2048]{1,0:T(8,128)(2,1)}, u32[]{:S(2)}) copy-start(bf16[256,2048]{1,0:T(8,128)(2,1)} %refs_6_.3) | copy-start | bytes 3145732
  51.9 31.0 %collective-permute-start = (bf16[256,2048]{1,0:T(8,128)(2,1)S(1)}, bf16[256,2048]{1,0:T(8,128)(2,1)S(1)}, u32[]{:S(2)}, u32[]{:S(2)}) collective-permute-start(bf16[256,2048]{1,0:T(8,128)(2,1)S(1)} %copy-done.5), channel_id=1, source_target_pairs={{0,2},{1,3},{2,0},{3,1},{4,6},{5,7},{6,4},{7,5},{8,10},{9,11},{10,... | collective-permute-start | bytes 3145736 | tf_op jit(solution)/shard_map/ppermute | solution.py:1453
  52.1 64.2 %collective-permute-start.1 = (bf16[256,2048]{1,0:T(8,128)(2,1)S(1)}, bf16[256,2048]{1,0:T(8,128)(2,1)S(1)}, u32[]{:S(2)}, u32[]{:S(2)}) collective-permute-start(bf16[256,2048]{1,0:T(8,128)(2,1)S(1)} %copy-done.5), channel_id=1, source_target_pairs={{0,1},{1,0},{2,3},{3,2},{4,5},{5,4},{6,7},{7,6},{8,9},{9,8},{10,11... | collective-permute-start | bytes 3145736 | tf_op jit(solution)/shard_map/ppermute | solution.py:1453
  82.9 33.4 %copy-start.15 = (bf16[256,2048]{1,0:T(8,128)(2,1)}, bf16[256,2048]{1,0:T(8,128)(2,1)S(1)}, u32[]{:S(2)}) copy-start(bf16[256,2048]{1,0:T(8,128)(2,1)S(1)} %collective-permute-done.refs_2_) | copy-start | bytes 3145732
  82.9 33.5 %collective-permute-start.2 = (bf16[256,2048]{1,0:T(8,128)(2,1)S(1)}, bf16[256,2048]{1,0:T(8,128)(2,1)S(1)}, u32[]{:S(2)}, u32[]{:S(2)}) collective-permute-start(bf16[256,2048]{1,0:T(8,128)(2,1)S(1)} %collective-permute-done.refs_2_), channel_id=1, source_target_pairs={{0,1},{1,0},{2,3},{3,2},{4,5},{5,4},{6,7},{7,6},{8,9},{9,8},{10,11... | collective-permute-start | bytes 3145736 | tf_op jit(solution)/shard_map/ppermute | solution.py:1453
  116.4 1.0 copy-start.16
  116.4 1.3 copy-start.17
  158.4 5.8 %copy-start.6 = (bf16[1024,1376]{1,0:T(8,128)(2,1)S(1)}, bf16[1024,1376]{1,0:T(8,128)(2,1)}, u32[]{:S(2)}) copy-start(bf16[1024,1376]{1,0:T(8,128)(2,1)} %get-tuple-element.126.refs_13_) | copy-start | bytes 8454148
  158.5 5.8 %copy-start.28 = (bf16[1024,2048]{1,0:T(8,128)(2,1)S(1)}, bf16[1024,2048]{1,0:T(8,128)(2,1)}, u32[]{:S(2)}) copy-start(bf16[1024,2048]{1,0:T(8,128)(2,1)} %get-tuple-element.127) | copy-start | bytes 12582916
  172.1 370.9 %reduce-scatter.6.cloned.1.call-start = ((), (), s32[]{:S(2)}) async-start(), calls=%async_computation.4 | async-start | bytes 3522560 | tf_op jit(solution)/shard_map/reduce_scatter | solution.py:1466
  172.2 76.8 %collective-permute-start.3 = (bf16[1376,1024]{1,0:T(8,128)(2,1)S(1)}, bf16[1376,1024]{1,0:T(8,128)(2,1)S(1)}, u32[]{:S(2)}, u32[]{:S(2)}) collective-permute-start(bf16[1376,1024]{1,0:T(8,128)(2,1)S(1)} %convolution_convert_fusion.1), channel_id=1, source_target_pairs={{0,4},{4,0},{8,12},{12,8},{16,20},{20,16},{24,28},{28,24},{1,5},{5... | collective-permute-start | bytes 8454152 | tf_op jit(solution)/shard_map/ppermute | solution.py:1453
  248.9 1.6 copy-start.7
  249.0 11.3 %collective-permute-start.4 = (bf16[1376,128]{1,0:T(8,128)(2,1)}, bf16[1376,128]{1,0:T(8,128)(2,1)S(1)}, u32[]{:S(2)}, u32[]{:S(2)}) collective-permute-start(bf16[1376,128]{1,0:T(8,128)(2,1)} %get-tuple-element.143), channel_id=1, source_target_pairs={{0,4},{4,0},{8,12},{12,8},{16,20},{20,16},{24,28},{28,24},{1,5},{5... | collective-permute-start | bytes 1056776 | tf_op jit(solution)/shard_map/ppermute | solution.py:1453
  260.3 292.0 %reduce-scatter.8.cloned.1.call-start = ((), (), s32[]{:S(2)}) async-start(), calls=%async_computation.5 | async-start | bytes 3522560 | tf_op jit(solution)/shard_map/reduce_scatter | solution.py:1466
  260.3 55.8 %collective-permute-start.5 = (bf16[1376,896]{1,0:T(8,128)(2,1)}, bf16[1376,896]{1,0:T(8,128)(2,1)S(1)}, u32[]{:S(2)}, u32[]{:S(2)}) collective-permute-start(bf16[1376,896]{1,0:T(8,128)(2,1)} %get-tuple-element.164), channel_id=1, source_target_pairs={{0,4},{4,0},{8,12},{12,8},{16,20},{20,16},{24,28},{28,24},{1,5},{5... | collective-permute-start | bytes 7397384 | tf_op jit(solution)/shard_map/ppermute | solution.py:1453
  320.4 1.4 copy-start.8
  320.4 3.4 copy-start.20
  320.4 4.4 copy-start
  322.7 62.5 %collective-permute-start.6 = (bf16[1024,1024]{1,0:T(8,128)(2,1)}, bf16[1024,1024]{1,0:T(8,128)(2,1)}, u32[]{:S(2)}, u32[]{:S(2)}) collective-permute-start(bf16[1024,1024]{1,0:T(8,128)(2,1)} %get-tuple-element.175), channel_id=1, source_target_pairs={{0,4},{4,0},{8,12},{12,8},{16,20},{20,16},{24,28},{28,24},{1,5},{5... | collective-permute-start | bytes 6291464 | tf_op jit(solution)/shard_map/ppermute | solution.py:1453
  325.7 59.5 %collective-permute-start.7 = (bf16[1376,256]{1,0:T(8,128)(2,1)}, bf16[1376,256]{1,0:T(8,128)(2,1)}, u32[]{:S(2)}, u32[]{:S(2)}) collective-permute-start(bf16[1376,256]{1,0:T(8,128)(2,1)} %constant_dynamic-slice_fusion), channel_id=1, source_target_pairs={{0,4},{4,0},{8,12},{12,8},{16,20},{20,16},{24,28},{28,24},{1,5},{5... | collective-permute-start | bytes 2113544 | tf_op jit(solution)/shard_map/ppermute | solution.py:1453
  326.6 36.9 %copy-start.1 = (bf16[1024,2048]{1,0:T(8,128)(2,1)S(1)}, bf16[1024,2048]{1,0:T(8,128)(2,1)}, u32[]{:S(2)}) copy-start(bf16[1024,2048]{1,0:T(8,128)(2,1)} %get-tuple-element.149.refs_17_.refs_10_) | copy-start | bytes 12582916
  326.6 36.9 %copy-start.10 = (bf16[1024,8]{1,0:T(8,128)(2,1)S(1)}, bf16[1024,8]{1,0:T(8,128)(2,1)}, u32[]{:S(2)}) copy-start(bf16[1024,8]{1,0:T(8,128)(2,1)} %get-tuple-element.169.refs_4_) | copy-start | bytes 49156
  363.5 21.6 %copy-start.2 = (bf16[256,2048]{1,0:T(8,128)(2,1)S(1)}, bf16[256,2048]{1,0:T(8,128)(2,1)}, u32[]{:S(2)}) copy-start(bf16[256,2048]{1,0:T(8,128)(2,1)} %refs_2_.3) | copy-start | bytes 3145732
  363.5 21.6 %copy-start.3 = (f32[256,2048]{1,0:T(8,128)S(1)}, f32[256,2048]{1,0:T(8,128)}, u32[]{:S(2)}) copy-start(f32[256,2048]{1,0:T(8,128)} %get-tuple-element.182) | copy-start | bytes 6291460
  363.5 21.6 %copy-start.21 = (f32[2048]{0:T(1024)S(1)}, f32[2048]{0:T(1024)}, u32[]{:S(2)}) copy-start(f32[2048]{0:T(1024)} %param.25) | copy-start | bytes 24580
  543.1 5.2 copy-start.9
  545.8 4.7 copy-start.4
  552.3 2.4 copy-start.14
  552.3 3.4 copy-start.26
  552.3 4.0 copy-start.19
  554.7 2.4 copy-start.18
  554.7 3.2 copy-start.13
  556.3 2.6 copy-start.12
  557.9 2.0 copy-start.25
  557.9 2.6 copy-start.24
  557.9 3.2 copy-start.22
  557.9 3.8 copy-start.27
  557.9 4.3 copy-start.11
  558.9 4.3 copy-start.23
Sparse Core Ops, SparseCore 0:
  172.3 101.7 reduce-scatter.3
  276.4 55.6 reduce-scatter.5
  334.6 54.9 reduce-scatter.7
